TPU v7x, 32 devices: a whole 2x2x4 slice. The times are simulated.
32 devices in a mesh: chan: 4 (over x, core), tm: 8 (over z, y).
Axes of the slice: x: 2, y: 2, z: 4, core: 2. Of those that a mesh axis runs over, the one named last changes fastest.
Arguments:
- record: float32 [2048, 65536], P('chan', 'tm'), may hold values from -6 to 6
- whitening: float32 [65], replicated, may hold values from -0.75 to 0.75
- offsets: int32 [128], P('tm'), may hold values from 0 to 256, as said below
- window_valid: int32 [128], P('tm'), may hold values 0 or 1
Outputs:
- cross_spectra: bfloat16 [64, 2, 2048, 2048], P('tm', None, 'chan')
Inputs may be any that keep to these rules, and one draw needn't show every extreme that they name: `offsets`: some window has offset exactly 256.
All inputs are finite; a program needn't handle non-finite values. No bound on the sum of `window_valid` on one device may be relied on, other than what follows from the above.
Results may differ from a plain program's by a relative error of at most 0.006.
Values may be sent and summed in bfloat16 or wider, within the bound.
No kernel may reach another device: no remote copies, remote signals or barrier semaphores. Data moves between devices by JAX's collectives and lax.ppermute only.
A program may use at most 192 MiB of HBM per device.

v0:
```python
import functools
import math

import jax
import jax.numpy as jnp
import numpy as np
from jax import lax
from jax.experimental import pallas as pl
from jax.experimental.pallas import tpu as pltpu
from jax.sharding import PartitionSpec as P

L = 2048
HOP = 512
JITTER = 256
TAPS = 65
BINS = 64
K0 = 64
RIM = 128
GROUP = L // HOP
EDGE = RIM + JITTER
LANES = 2 * BINS
MIB = 1 << 20
F32 = jnp.float32
BF16 = jnp.bfloat16


def from_behind(shard, axis, by):
    devices = lax.axis_size(axis)
    pairs = [(i, i + by) for i in range(devices) if 0 <= i + by < devices]
    return lax.ppermute(shard, axis, pairs)


def phase_table():
    sample = np.arange(L) - (TAPS - 1)
    angles = 2.0 * np.pi * np.mod(sample[:, None] * (K0 + np.arange(BINS))[None, :], L) / L
    return (np.concatenate([np.cos(angles), -np.sin(angles)], axis=1) / math.sqrt(L)).astype(np.float32)


def matmul(a, b):
    return jnp.dot(a, b, preferred_element_type=F32)


def turn(values, place):
    lane = lax.broadcasted_iota(jnp.int32, (8, LANES), 1)
    bins = K0 + (lane & (BINS - 1))
    angles = ((bins * (place + L)) & (L - 1)).astype(F32) * (2.0 * math.pi / L)
    sine = jnp.sin(angles)
    sine = jnp.where(lane < BINS, -sine, sine)
    return values * jnp.cos(angles)[:1] + pltpu.roll(values, BINS, 1) * sine[:1]


def edge_table(rise, fall, offset):
    start = JITTER - offset
    return jnp.concatenate([rise[pl.ds(start, RIM), :], fall[pl.ds(start, JITTER), :]], axis=0).astype(BF16)


def across(values):
    channels = values.shape[0]
    if channels % 128:
        values = jnp.pad(values, ((0, 128 - channels), (0, 0)))
    return values.T


def outbox_kernel(offsets, valid, record, out):
    top = record[0:8, :]
    row = lax.broadcasted_iota(jnp.int32, top.shape, 0)
    lane = lax.broadcasted_iota(jnp.int32, top.shape, 1)
    first = offsets.shape[0] - GROUP
    for q in range(GROUP):
        top = jnp.where((row == 0) & (lane == q), offsets[first + q].astype(F32), top)
        top = jnp.where((row == 0) & (lane == GROUP + q), valid[first + q].astype(F32), top)
    out[...] = jnp.concatenate([top, record[8:, :]], axis=0).astype(BF16)


def outbox(record, offsets, valid):
    channels, slab = record.shape
    smem = pl.BlockSpec(memory_space=pltpu.SMEM)
    return pl.pallas_call(
        outbox_kernel,
        grid=(1,),
        out_shape=jax.ShapeDtypeStruct((channels, RIM), BF16),
        in_specs=[smem, smem, pl.BlockSpec((channels, RIM), lambda i: (0, slab // RIM - 1))],
        out_specs=pl.BlockSpec(memory_space=pltpu.VMEM),
        name="outbox",
    )(offsets, valid, record)


def tables_kernel(taps, table, blocks, rise, fall, padded):
    padded[0 : TAPS - 1, :] = jnp.zeros((TAPS - 1, LANES), F32)
    padded[TAPS - 1 :, :] = table[TAPS - 1 : TAPS - 1 + padded.shape[0] - (TAPS - 1), :]
    ramp = jnp.zeros((TAPS - 1, LANES), F32)
    gain = jnp.zeros((1, LANES), F32)
    for m in range(TAPS):
        tap = taps[m]
        ramp = ramp + tap * padded[m : m + TAPS - 1, :]
        gain = gain + tap * padded[TAPS - 1 + m : TAPS + m, :]
    gain = jnp.broadcast_to(gain * math.sqrt(L), (8, LANES))
    lane = lax.broadcasted_iota(jnp.int32, (8, LANES), 1)
    swapped = pltpu.roll(gain, BINS, 1)
    gain_re = jnp.where(lane < BINS, gain, swapped)[:1]
    gain_im = jnp.where(lane < BINS, -swapped, gain)[:1]
    columns = table[...]
    pure = columns * gain_re + pltpu.roll(columns, BINS, 1) * gain_im
    blocks[...] = pure.astype(BF16)
    rise[...] = jnp.zeros_like(rise)
    rise[rise.shape[0] - (TAPS - 1) :, :] = -ramp
    ahead = JITTER - (TAPS - 1)
    fall[0:ahead, :] = pure[L - ahead :]
    fall[ahead:JITTER, :] = pure[: TAPS - 1] - ramp
    fall[JITTER:, :] = jnp.zeros((fall.shape[0] - JITTER, LANES), F32)


def tables(whitening):
    vmem = pl.BlockSpec(memory_space=pltpu.VMEM)
    return pl.pallas_call(
        tables_kernel,
        out_shape=(
            jax.ShapeDtypeStruct((L, LANES), BF16),
            jax.ShapeDtypeStruct((EDGE, LANES), F32),
            jax.ShapeDtypeStruct((2 * JITTER, LANES), F32),
        ),
        in_specs=[pl.BlockSpec(memory_space=pltpu.SMEM), vmem],
        out_specs=(vmem, vmem, vmem),
        scratch_shapes=[pltpu.VMEM((2 * TAPS + 6, LANES), F32)],
        compiler_params=pltpu.CompilerParams(vmem_limit_bytes=16 * MIB),
        name="tables",
    )(whitening, phase_table())


def border_kernel(inbox, record, blocks, rise, fall, parts, collected):
    channels = record.shape[0]
    head = inbox[0:16, :].astype(F32)[:1]
    lane = lax.broadcasted_iota(jnp.int32, (1, LANES), 1)

    def told(at):
        return jnp.sum(jnp.where(lane == at, head, 0.0)).astype(jnp.int32)

    before = jnp.zeros((channels, LANES), F32)
    for q in range(GROUP):
        offset = told(q)
        edges = edge_table(rise, fall, offset)
        if q == 0:
            part = matmul(record[:, 0:JITTER].astype(BF16), edges[RIM:])
        else:
            part = matmul(record[:, HOP * q - RIM : HOP * q + JITTER].astype(BF16), edges)
        place = HOP * q + offset - (TAPS - 1)
        part = (part + turn(before, place)) * told(GROUP + q).astype(F32)
        upright = across(part)
        for c in range(collected.shape[0]):
            piece = upright[:, 128 * c : 128 * c + 128]
            collected[c, pl.ds(q, BINS, stride=2 * GROUP), :] = piece[:BINS]
            collected[c, pl.ds(GROUP + q, BINS, stride=2 * GROUP), :] = piece[BINS:]
        if q < GROUP - 1:
            before = before + matmul(
                record[:, HOP * q : HOP * q + HOP].astype(BF16), blocks[HOP * q : HOP * q + HOP, :]
            )
    width = min(128, channels)
    for c in range(collected.shape[0]):
        block = collected[c].reshape(BINS, 2 * GROUP, 128).astype(BF16)
        parts[:, :, width * c : width * c + width] = block[:, :, :width]


def border_parts(record, inbox, blocks, rise, fall):
    channels = record.shape[0]
    vmem = pl.BlockSpec(memory_space=pltpu.VMEM)
    lead = L - HOP + JITTER
    return pl.pallas_call(
        border_kernel,
        grid=(1,),
        out_shape=jax.ShapeDtypeStruct((BINS, 2 * GROUP, channels), BF16),
        in_specs=[vmem, pl.BlockSpec((channels, lead), lambda i: (0, 0)), vmem, vmem, vmem],
        out_specs=vmem,
        scratch_shapes=[pltpu.VMEM((max(channels // 128, 1), 2 * GROUP * BINS, 128), F32)],
        compiler_params=pltpu.CompilerParams(vmem_limit_bytes=24 * MIB),
        cost_estimate=pl.CostEstimate(
            flops=2 * channels * LANES * 3072, bytes_accessed=4 * channels * lead, transcendentals=0
        ),
        name="border_parts",
    )(inbox, record, blocks, rise, fall)


def spectra_kernel(offsets, valid, record, rim, blocks, rise, fall, out, samples, later, collected, sems):
    channels, slab = record.shape
    steps = slab // L
    windows = out.shape[2]

    def fetch(s):
        return pltpu.make_async_copy(
            record.at[:, pl.ds(L * s, L)], samples.at[:, pl.ds(RIM + L * s, L)], sems.at[s]
        )

    for s in range(steps):
        fetch(s).start()
    samples[:, 0:RIM] = rim[...].astype(F32)
    samples[:, RIM + slab :] = jnp.zeros((channels, samples.shape[1] - RIM - slab), F32)

    def block_sums(s):
        found = []
        for i in range(GROUP):
            begin = pl.multiple_of(RIM + L * s + HOP * i, 128)
            found.append(
                matmul(samples[:, pl.ds(begin, HOP)].astype(BF16), blocks[HOP * i : HOP * i + HOP, :])
            )
        return found

    def keep(found):
        total = found[GROUP - 1]
        later[GROUP - 1] = total
        for q in range(GROUP - 2, -1, -1):
            total = total + found[q]
            later[q] = total

    def one_window(w, q, before):
        offset = offsets[w]
        begin = pl.multiple_of(HOP * w, 128)
        ends = samples[:, pl.ds(begin + L, EDGE)] - samples[:, pl.ds(begin, EDGE)]
        part = matmul(ends.astype(BF16), edge_table(rise, fall, offset))
        total = later[q] if before is None else later[q] + before
        part = (part + turn(total, HOP * q + offset - (TAPS - 1))) * valid[w].astype(F32)
        upright = across(part)
        for c in range(collected.shape[0]):
            collected[c, pl.ds(w, LANES, stride=windows), :] = upright[:, 128 * c : 128 * c + 128]

    fetch(0).wait()
    keep(block_sums(0))

    @pl.loop(0, steps - 1)
    def _(s):
        fetch(s + 1).wait()
        found = block_sums(s + 1)
        before = None
        for q in range(GROUP):
            one_window(GROUP * s + q, q, before)
            before = found[q] if before is None else before + found[q]
        keep(found)

    for q in range(GROUP):
        one_window(GROUP * (steps - 1) + q, q, None)

    width = min(128, channels)
    for c in range(collected.shape[0]):
        block = collected[c].reshape(LANES, windows, 128).astype(BF16)
        out[:, 0, :, width * c : width * c + width] = block[:BINS, :, :width]
        out[:, 1, :, width * c : width * c + width] = block[BINS:, :, :width]


def own_spectra(record, rim, offsets, valid, blocks, rise, fall):
    channels, slab = record.shape
    windows = offsets.shape[0]
    smem = pl.BlockSpec(memory_space=pltpu.SMEM)
    vmem = pl.BlockSpec(memory_space=pltpu.VMEM)
    return pl.pallas_call(
        spectra_kernel,
        out_shape=jax.ShapeDtypeStruct((BINS, 2, windows, channels), BF16),
        in_specs=[smem, smem, pl.BlockSpec(memory_space=pl.ANY), vmem, vmem, vmem, vmem],
        out_specs=vmem,
        scratch_shapes=[
            pltpu.VMEM((channels, RIM + slab + L - HOP + JITTER), F32),
            pltpu.VMEM((GROUP, channels, LANES), F32),
            pltpu.VMEM((max(channels // 128, 1), LANES * windows, 128), F32),
            pltpu.SemaphoreType.DMA((slab // L,)),
        ],
        compiler_params=pltpu.CompilerParams(vmem_limit_bytes=40 * MIB),
        cost_estimate=pl.CostEstimate(
            flops=2 * channels * LANES * 896 * windows, bytes_accessed=4 * channels * slab, transcendentals=0
        ),
        name="own_spectra",
    )(offsets, valid, record, rim, blocks, rise, fall)


def join_kernel(own, parts, *chunks):
    windows = own.shape[2]
    half = windows - 2 * GROUP
    part = parts[...].astype(F32)
    row = lax.broadcasted_iota(jnp.int32, part.shape, 1)
    late = row >= GROUP
    moved = jnp.concatenate([part[:, GROUP:], part[:, :GROUP]], axis=1)
    for ri, extra in enumerate((moved, part)):
        spectra = own[:, ri].astype(F32)
        upper = spectra[:, half:] + jnp.where(late, extra, 0.0)
        joined = jnp.concatenate([spectra[:, :half], upper], axis=1).astype(BF16)
        begin = 0
        for chunk in chunks:
            count = chunk.shape[1]
            chunk[0, :, ri] = joined[begin : begin + count]
            begin += count


def chunk_sizes(bins):
    count = min(3, bins)
    return [(bins + count - 1 - c) // count for c in range(count)]


def joined_chunks(own, parts, devices):
    _, _, windows, channels = own.shape
    bins = BINS // devices
    shapes = [(devices, count, 2, windows, channels) for count in chunk_sizes(bins)]
    return pl.pallas_call(
        join_kernel,
        grid=(devices,),
        out_shape=tuple(jax.ShapeDtypeStruct(shape, BF16) for shape in shapes),
        in_specs=[
            pl.BlockSpec((bins, 2, windows, channels), lambda g: (g, 0, 0, 0)),
            pl.BlockSpec((bins, 2 * GROUP, channels), lambda g: (g, 0, 0)),
        ],
        out_specs=tuple(pl.BlockSpec((1,) + shape[1:], lambda g: (g, 0, 0, 0, 0)) for shape in shapes),
        compiler_params=pltpu.CompilerParams(vmem_limit_bytes=16 * MIB),
        name="joined_chunks",
    )(own, parts)


def cross_kernel(scale, stacked, me, own, *rest):
    out = rest[-1]
    sources, _, _, windows, channels = own.shape
    depth = sources * 2 * windows
    straight = own[:, 0].reshape(depth, channels)
    turned = jnp.concatenate([own[:, 0, 1:], -own[:, 0, :1]], axis=1).reshape(depth, channels)
    left = jnp.concatenate([straight, turned], axis=1)
    blocks = rest[0].shape[0] if stacked else len(rest) - 1
    for n in range(blocks):
        if stacked:
            right, at = rest[0][n, :, 0], channels * n
        else:
            right = (own if n == 0 else rest[n - 1])[:, 0]
            at = pl.multiple_of(channels * (me[0] ^ n), 128)
        right = right.reshape(depth, channels)
        both = lax.dot_general(left, right, (((0,), (0,)), ((), ())), preferred_element_type=F32) * scale
        out[0, 0, :, pl.ds(at, channels)] = both[:channels].astype(BF16)
        out[0, 1, :, pl.ds(at, channels)] = both[channels:].astype(BF16)


def cross_products(own, others, result, begin, bins):
    sources, count, _, windows, channels = own.shape
    stacked = not isinstance(others, list)
    blocks = others.shape[0] if stacked else len(others) + 1
    shape = (bins, 2, channels, blocks * channels)
    spec = pl.BlockSpec((sources, 1, 2, windows, channels), lambda f: (0, f, 0, 0, 0))
    smem = pl.BlockSpec(memory_space=pltpu.SMEM)
    operands = [lax.axis_index("chan").astype(jnp.int32).reshape(1), own]
    in_specs = [smem, spec]
    if stacked:
        operands.append(others)
        in_specs.append(pl.BlockSpec((blocks, sources, 1, 2, windows, channels), lambda f: (0, 0, f, 0, 0, 0)))
    else:
        operands += others
        in_specs += [spec] * len(others)
    if result is None:
        result = jnp.zeros((8, 128), BF16)
        aliases = {}
    else:
        aliases = {len(operands): 0}
    operands.append(result)
    in_specs.append(pl.BlockSpec(memory_space=pl.ANY))
    flops = 2 * count * 2 * channels * blocks * channels * sources * 2 * windows
    return pl.pallas_call(
        functools.partial(cross_kernel, 1.0 / (sources * windows), stacked),
        grid=(count,),
        out_shape=jax.ShapeDtypeStruct(shape, BF16),
        in_specs=in_specs,
        out_specs=pl.BlockSpec((1,) + shape[1:], lambda f: (begin + f, 0, 0, 0)),
        input_output_aliases=aliases,
        compiler_params=pltpu.CompilerParams(vmem_limit_bytes=36 * MIB),
        cost_estimate=pl.CostEstimate(
            flops=flops, bytes_accessed=2 * count * 2 * channels * blocks * channels, transcendentals=0
        ),
        name="cross_products",
    )(*operands)


def swapped(shard, axis, bit):
    devices = lax.axis_size(axis)
    return lax.ppermute(shard, axis, [(i, i ^ bit) for i in range(devices)])


def gathered(mine):
    devices = lax.axis_size("chan")
    if devices & (devices - 1) or mine.shape[-1] % 128:
        return lax.all_gather(mine, "chan", axis=0, tiled=False)
    held = {0: mine}
    bit = devices // 2
    while bit:
        held.update({n | bit: swapped(block, "chan", bit) for n, block in list(held.items())})
        bit //= 2
    return [held[n] for n in range(1, devices)]


def per_device(record, whitening, offsets, window_valid):
    devices = lax.axis_size("tm")
    bins = BINS // devices
    inbox = from_behind(outbox(record, offsets, window_valid), "tm", 1)
    blocks, rise, fall = tables(whitening)
    parts = from_behind(border_parts(record, inbox, blocks, rise, fall), "tm", -1)
    own = own_spectra(record, inbox, offsets, window_valid, blocks, rise, fall)
    result, begin = None, 0
    for chunk in joined_chunks(own, parts, devices):
        mine = lax.all_to_all(chunk, "tm", split_axis=0, concat_axis=0, tiled=True)
        result = cross_products(mine, gathered(mine), result, begin, bins)
        begin += chunk.shape[1]
    return result


def solution(mesh):
    in_specs = (P("chan", "tm"), P(), P("tm"), P("tm"))
    out_specs = P("tm", None, "chan", None)
    return jax.shard_map(
        per_device, mesh=mesh, in_specs=in_specs, out_specs=out_specs, check_vma=False
    )
```

profile of v0, /device:TPU:0, one launch (start us, length us, event | category | flops | bytes accessed | tf_op | source)
XLA Modules:
  0.0 136.0 jit_solution(15988676225076540728)
XLA Ops:
  0.0 1.7 %outbox.1 = bf16[512,128]{1,0:T(8,128)(2,1)} custom-call(s32[16]{0:T(128)} %offsets.3, s32[16]{0:T(128)} %valid.3, f32[512,8192]{1,0:T(8,128)} %record.5), custom_call_target="tpu_custom_call" | custom-call | tf_op jit(solution)/shard_map/outbox/pallas_call | solution.py:78
  1.7 4.9 %collective-permute-start = (bf16[512,128]{1,0:T(8,128)(2,1)}, bf16[512,128]{1,0:T(8,128)(2,1)S(1)}, u32[]{:S(2)}, u32[]{:S(2)}) collective-permute-start(bf16[512,128]{1,0:T(8,128)(2,1)} %outbox.1), channel_id=1, source_target_pairs={{0,1},{1,2},{2,3},{3,4},{4,5},{5,6},{6,7},{8,9},{9,10},{10,11},{11... | collective-permute-start | bytes 393224 | tf_op jit(solution)/shard_map/ppermute | solution.py:30
  6.5 1.2 copy-done.1
  7.8 0.7 copy-done.4
  8.4 1.0 tables.1
  9.6 5.8 %copy-done = f32[512,8192]{1,0:T(8,128)S(1)} copy-done((f32[512,8192]{1,0:T(8,128)S(1)}, f32[512,8192]{1,0:T(8,128)}, u32[]{:S(2)}) %copy-start) | copy-done | bytes 16777240
  15.3 1.3 border_parts.1
  16.7 1.3 collective-permute-start.1
  18.0 10.2 %own_spectra.1.own = bf16[64,2,16,512]{3,2,1,0:T(8,128)(2,1)S(1)} custom-call(s32[16]{0:T(128)S(1)} %copy-done.2, s32[16]{0:T(128)S(1)} %copy-done.3, f32[512,8192]{1,0:T(8,128)} %record.5, bf16[512,128]{1,0:T(8,128)(2,1)S(1)} %collective-permute-done.rim.inbox, bf16[2048,128]{1,0:T(8,128)(2,1)S(1)} %get-tuple-element.11.blocks, ...), custom_call_target="tpu_custom_call" | custom-call | flops 1879048192 | bytes 16777216 | tf_op jit(solution)/shard_map/own_spectra/pallas_call | solution.py:252
  28.2 3.8 %collective-permute-done.1.parts = bf16[64,8,512]{2,1,0:T(8,128)(2,1)S(1)} collective-permute-done((bf16[64,8,512]{2,1,0:T(8,128)(2,1)S(1)}, bf16[64,8,512]{2,1,0:T(8,128)(2,1)S(1)}, u32[]{:S(2)}, u32[]{:S(2)}) %collective-permute-start.1) | collective-permute-done | bytes 524320 | tf_op jit(solution)/shard_map/ppermute | solution.py:30
  32.0 2.8 %joined_chunks.1 = (bf16[8,3,2,16,512]{4,3,2,1,0:T(8,128)(2,1)S(1)}, bf16[8,3,2,16,512]{4,3,2,1,0:T(8,128)(2,1)}, bf16[8,2,2,16,512]{4,3,2,1,0:T(8,128)(2,1)}) custom-call(bf16[64,2,16,512]{3,2,1,0:T(8,128)(2,1)S(1)} %own_spectra.1.own, bf16[64,8,512]{2,1,0:T(8,128)(2,1)S(1)} %collective-permute-done.1.parts), custom_call_target="tpu_custom_call" | custom-call | tf_op jit(solution)/shard_map/joined_chunks/pallas_call | solution.py:298
  34.7 24.1 %all_to_all.15.own = bf16[8,3,2,16,512]{4,3,2,1,0:T(8,128)(2,1)S(1)} all-to-all(bf16[8,3,2,16,512]{4,3,2,1,0:T(8,128)(2,1)S(1)} %get-tuple-element.16), channel_id=1, replica_groups=mesh['chan'=4,'tm'=8] {'tm'}, dimensions={0} | all-to-all | bytes 1572864 | tf_op jit(solution)/shard_map/all_to_all | solution.py:396
  58.9 3.6 %all-to-all-start.1 = ((bf16[8,3,2,16,512]{4,3,2,1,0:T(8,128)(2,1)}), bf16[8,3,2,16,512]{4,3,2,1,0:T(8,128)(2,1)S(1)}, u32[]{:S(2)}, u32[]{:S(2)}) async-start(bf16[8,3,2,16,512]{4,3,2,1,0:T(8,128)(2,1)} %get-tuple-element.15), calls=%async_computation.1 | async-start | bytes 1572864 | tf_op jit(solution)/shard_map/all_to_all | solution.py:396
  62.5 1.5 %collective-permute-start.9 = (bf16[8,3,2,16,512]{4,3,2,1,0:T(8,128)(2,1)S(1)}, bf16[8,3,2,16,512]{4,3,2,1,0:T(8,128)(2,1)}, u32[]{:S(2)}, u32[]{:S(2)}) collective-permute-start(bf16[8,3,2,16,512]{4,3,2,1,0:T(8,128)(2,1)S(1)} %all_to_all.15.own), channel_id=1, source_target_pairs={{0,16},{8,24},{16,0},{24,8},{1,17},{9,25},{17,1},{25,9},{2,18},{10... | collective-permute-start | bytes 2359304 | tf_op jit(solution)/shard_map/ppermute | solution.py:372
  64.0 17.6 %all-to-all-done.1.own = bf16[8,3,2,16,512]{4,3,2,1,0:T(8,128)(2,1)S(1)} async-done(((bf16[8,3,2,16,512]{4,3,2,1,0:T(8,128)(2,1)}), bf16[8,3,2,16,512]{4,3,2,1,0:T(8,128)(2,1)S(1)}, u32[]{:S(2)}, u32[]{:S(2)}) %all-to-all-start.1) | async-done | bytes 786464 | tf_op jit(solution)/shard_map/all_to_all | solution.py:396
  81.6 3.5 %all-to-all-start = ((bf16[8,2,2,16,512]{4,3,2,1,0:T(8,128)(2,1)}), bf16[8,2,2,16,512]{4,3,2,1,0:T(8,128)(2,1)S(1)}, u32[]{:S(2)}, u32[]{:S(2)}) async-start(bf16[8,2,2,16,512]{4,3,2,1,0:T(8,128)(2,1)} %get-tuple-element.14), calls=%async_computation | async-start | bytes 1048576 | tf_op jit(solution)/shard_map/all_to_all | solution.py:396
  85.1 1.5 %collective-permute-start.6 = (bf16[8,3,2,16,512]{4,3,2,1,0:T(8,128)(2,1)S(1)}, bf16[8,3,2,16,512]{4,3,2,1,0:T(8,128)(2,1)S(1)}, u32[]{:S(2)}, u32[]{:S(2)}) collective-permute-start(bf16[8,3,2,16,512]{4,3,2,1,0:T(8,128)(2,1)S(1)} %all-to-all-done.1.own), channel_id=1, source_target_pairs={{0,16},{8,24},{16,0},{24,8},{1,17},{9,25},{17,1},{25,9},{2,18},{10... | collective-permute-start | bytes 2359304 | tf_op jit(solution)/shard_map/ppermute | solution.py:372
  87.2 12.3 %all-to-all-done.own = bf16[8,2,2,16,512]{4,3,2,1,0:T(8,128)(2,1)S(1)} async-done(((bf16[8,2,2,16,512]{4,3,2,1,0:T(8,128)(2,1)}), bf16[8,2,2,16,512]{4,3,2,1,0:T(8,128)(2,1)S(1)}, u32[]{:S(2)}, u32[]{:S(2)}) %all-to-all-start) | async-done | bytes 524320 | tf_op jit(solution)/shard_map/all_to_all | solution.py:396
  99.5 1.5 %collective-permute-start.3 = (bf16[8,2,2,16,512]{4,3,2,1,0:T(8,128)(2,1)S(1)}, bf16[8,2,2,16,512]{4,3,2,1,0:T(8,128)(2,1)S(1)}, u32[]{:S(2)}, u32[]{:S(2)}) collective-permute-start(bf16[8,2,2,16,512]{4,3,2,1,0:T(8,128)(2,1)S(1)} %all-to-all-done.own), channel_id=1, source_target_pairs={{0,16},{8,24},{16,0},{24,8},{1,17},{9,25},{17,1},{25,9},{2,18},{10... | collective-permute-start | bytes 1572872 | tf_op jit(solution)/shard_map/ppermute | solution.py:372
  101.0 4.7 %collective-permute-done.6.rest_1_ = bf16[8,3,2,16,512]{4,3,2,1,0:T(8,128)(2,1)S(1)} collective-permute-done((bf16[8,3,2,16,512]{4,3,2,1,0:T(8,128)(2,1)S(1)}, bf16[8,3,2,16,512]{4,3,2,1,0:T(8,128)(2,1)S(1)}, u32[]{:S(2)}, u32[]{:S(2)}) %collective-permute-start.6) | collective-permute-done | bytes 786464 | tf_op jit(solution)/shard_map/ppermute | solution.py:372
  105.7 9.5 %collective-permute-done.3.rest_1_ = bf16[8,2,2,16,512]{4,3,2,1,0:T(8,128)(2,1)S(1)} collective-permute-done((bf16[8,2,2,16,512]{4,3,2,1,0:T(8,128)(2,1)S(1)}, bf16[8,2,2,16,512]{4,3,2,1,0:T(8,128)(2,1)S(1)}, u32[]{:S(2)}, u32[]{:S(2)}) %collective-permute-start.3) | collective-permute-done | bytes 524320 | tf_op jit(solution)/shard_map/ppermute | solution.py:372
  115.7 7.7 %cross_products.3.rest_3_ = bf16[8,2,512,2048]{3,2,1,0:T(8,128)(2,1)} custom-call(s32[1]{0:T(128)} %bitcast.me, bf16[8,3,2,16,512]{4,3,2,1,0:T(8,128)(2,1)S(1)} %all_to_all.15.own, bf16[8,3,2,16,512]{4,3,2,1,0:T(8,128)(2,1)} %collective-permute-done.8.rest_0_, bf16[8,3,2,16,512]{4,3,2,1,0:T(8,128)(2,1)} %collective-permute-done.9.rest_1_, ...), custom_call_target="tpu_custom_call" | custom-call | flops 3221225472 | bytes 12582912 | tf_op jit(solution)/shard_map/cross_products/pallas_call | solution.py:355
  123.5 7.7 %cross_products.4.rest_3_ = bf16[8,2,512,2048]{3,2,1,0:T(8,128)(2,1)} custom-call(s32[1]{0:T(128)} %bitcast.me, bf16[8,3,2,16,512]{4,3,2,1,0:T(8,128)(2,1)S(1)} %all-to-all-done.1.own, bf16[8,3,2,16,512]{4,3,2,1,0:T(8,128)(2,1)} %collective-permute-done.5.rest_0_, ...), custom_call_target="tpu_custom_call", output_to_operand_aliasing={{}: (5, {})} | custom-call | flops 3221225472 | bytes 12582912 | tf_op jit(solution)/shard_map/cross_products/pallas_call | solution.py:355
  131.2 4.9 %cross_products.5 = bf16[8,2,512,2048]{3,2,1,0:T(8,128)(2,1)} custom-call(s32[1]{0:T(128)} %bitcast.me, bf16[8,2,2,16,512]{4,3,2,1,0:T(8,128)(2,1)S(1)} %all-to-all-done.own, bf16[8,2,2,16,512]{4,3,2,1,0:T(8,128)(2,1)S(1)} %collective-permute-done.2.rest_0_, ...), custom_call_target="tpu_custom_call", output_to_operand_aliasing={{}: (5, {})} | custom-call | flops 2147483648 | bytes 8388608 | tf_op jit(solution)/shard_map/cross_products/pallas_call | solution.py:355
  (22 shorter events, 1.2 us)
Async XLA Ops:
  0.0 18.0 %copy-start.2 = (s32[16]{0:T(128)S(1)}, s32[16]{0:T(128)}, u32[]{:S(2)}) copy-start(s32[16]{0:T(128)} %offsets.3) | copy-start | bytes 196
  0.0 18.0 %copy-start.3 = (s32[16]{0:T(128)S(1)}, s32[16]{0:T(128)}, u32[]{:S(2)}) copy-start(s32[16]{0:T(128)} %valid.3) | copy-start | bytes 196
  1.7 7.9 %collective-permute-start = (bf16[512,128]{1,0:T(8,128)(2,1)}, bf16[512,128]{1,0:T(8,128)(2,1)S(1)}, u32[]{:S(2)}, u32[]{:S(2)}) collective-permute-start(bf16[512,128]{1,0:T(8,128)(2,1)} %outbox.1), channel_id=1, source_target_pairs={{0,1},{1,2},{2,3},{3,4},{4,5},{5,6},{6,7},{8,9},{9,10},{10,11},{11... | collective-permute-start | bytes 393224 | tf_op jit(solution)/shard_map/ppermute | solution.py:30
  6.5 1.2 copy-start.1
  7.8 0.7 copy-start.4
  9.6 5.8 %copy-start = (f32[512,8192]{1,0:T(8,128)S(1)}, f32[512,8192]{1,0:T(8,128)}, u32[]{:S(2)}) copy-start(f32[512,8192]{1,0:T(8,128)} %record.5) | copy-start | bytes 50331652
  16.7 15.3 %collective-permute-start.1 = (bf16[64,8,512]{2,1,0:T(8,128)(2,1)S(1)}, bf16[64,8,512]{2,1,0:T(8,128)(2,1)S(1)}, u32[]{:S(2)}, u32[]{:S(2)}) collective-permute-start(bf16[64,8,512]{2,1,0:T(8,128)(2,1)S(1)} %border_parts.1), channel_id=1, source_target_pairs={{1,0},{2,1},{3,2},{4,3},{5,4},{6,5},{7,6},{9,8},{10,9},{11,10},{12... | collective-permute-start | bytes 1572872 | tf_op jit(solution)/shard_map/ppermute | solution.py:30
  58.9 22.7 %all-to-all-start.1 = ((bf16[8,3,2,16,512]{4,3,2,1,0:T(8,128)(2,1)}), bf16[8,3,2,16,512]{4,3,2,1,0:T(8,128)(2,1)S(1)}, u32[]{:S(2)}, u32[]{:S(2)}) async-start(bf16[8,3,2,16,512]{4,3,2,1,0:T(8,128)(2,1)} %get-tuple-element.15), calls=%async_computation.1 | async-start | bytes 1572864 | tf_op jit(solution)/shard_map/all_to_all | solution.py:396
  62.5 24.2 %collective-permute-start.9 = (bf16[8,3,2,16,512]{4,3,2,1,0:T(8,128)(2,1)S(1)}, bf16[8,3,2,16,512]{4,3,2,1,0:T(8,128)(2,1)}, u32[]{:S(2)}, u32[]{:S(2)}) collective-permute-start(bf16[8,3,2,16,512]{4,3,2,1,0:T(8,128)(2,1)S(1)} %all_to_all.15.own), channel_id=1, source_target_pairs={{0,16},{8,24},{16,0},{24,8},{1,17},{9,25},{17,1},{25,9},{2,18},{10... | collective-permute-start | bytes 2359304 | tf_op jit(solution)/shard_map/ppermute | solution.py:372
  81.6 17.9 %all-to-all-start = ((bf16[8,2,2,16,512]{4,3,2,1,0:T(8,128)(2,1)}), bf16[8,2,2,16,512]{4,3,2,1,0:T(8,128)(2,1)S(1)}, u32[]{:S(2)}, u32[]{:S(2)}) async-start(bf16[8,2,2,16,512]{4,3,2,1,0:T(8,128)(2,1)} %get-tuple-element.14), calls=%async_computation | async-start | bytes 1048576 | tf_op jit(solution)/shard_map/all_to_all | solution.py:396
  85.1 20.5 %collective-permute-start.6 = (bf16[8,3,2,16,512]{4,3,2,1,0:T(8,128)(2,1)S(1)}, bf16[8,3,2,16,512]{4,3,2,1,0:T(8,128)(2,1)S(1)}, u32[]{:S(2)}, u32[]{:S(2)}) collective-permute-start(bf16[8,3,2,16,512]{4,3,2,1,0:T(8,128)(2,1)S(1)} %all-to-all-done.1.own), channel_id=1, source_target_pairs={{0,16},{8,24},{16,0},{24,8},{1,17},{9,25},{17,1},{25,9},{2,18},{10... | collective-permute-start | bytes 2359304 | tf_op jit(solution)/shard_map/ppermute | solution.py:372
  86.7 28.5 %collective-permute-start.8 = (bf16[8,3,2,16,512]{4,3,2,1,0:T(8,128)(2,1)S(1)}, bf16[8,3,2,16,512]{4,3,2,1,0:T(8,128)(2,1)}, u32[]{:S(2)}, u32[]{:S(2)}) collective-permute-start(bf16[8,3,2,16,512]{4,3,2,1,0:T(8,128)(2,1)S(1)} %all_to_all.15.own), channel_id=1, source_target_pairs={{0,8},{8,0},{16,24},{24,16},{1,9},{9,1},{17,25},{25,17},{2,10},{10... | collective-permute-start | bytes 2359304 | tf_op jit(solution)/shard_map/ppermute | solution.py:372
  86.7 29.0 %collective-permute-start.10 = (bf16[8,3,2,16,512]{4,3,2,1,0:T(8,128)(2,1)}, bf16[8,3,2,16,512]{4,3,2,1,0:T(8,128)(2,1)}, u32[]{:S(2)}, u32[]{:S(2)}) collective-permute-start(bf16[8,3,2,16,512]{4,3,2,1,0:T(8,128)(2,1)} %collective-permute-done.9.rest_1_), channel_id=1, source_target_pairs={{0,8},{8,0},{16,24},{24,16},{1,9},{9,1},{17,25},{25,17},{2,10},{10... | collective-permute-start | bytes 2359304 | tf_op jit(solution)/shard_map/ppermute | solution.py:372
  99.5 15.7 %collective-permute-start.3 = (bf16[8,2,2,16,512]{4,3,2,1,0:T(8,128)(2,1)S(1)}, bf16[8,2,2,16,512]{4,3,2,1,0:T(8,128)(2,1)S(1)}, u32[]{:S(2)}, u32[]{:S(2)}) collective-permute-start(bf16[8,2,2,16,512]{4,3,2,1,0:T(8,128)(2,1)S(1)} %all-to-all-done.own), channel_id=1, source_target_pairs={{0,16},{8,24},{16,0},{24,8},{1,17},{9,25},{17,1},{25,9},{2,18},{10... | collective-permute-start | bytes 1572872 | tf_op jit(solution)/shard_map/ppermute | solution.py:372
  100.9 22.5 %collective-permute-start.5 = (bf16[8,3,2,16,512]{4,3,2,1,0:T(8,128)(2,1)S(1)}, bf16[8,3,2,16,512]{4,3,2,1,0:T(8,128)(2,1)}, u32[]{:S(2)}, u32[]{:S(2)}) collective-permute-start(bf16[8,3,2,16,512]{4,3,2,1,0:T(8,128)(2,1)S(1)} %all-to-all-done.1.own), channel_id=1, source_target_pairs={{0,8},{8,0},{16,24},{24,16},{1,9},{9,1},{17,25},{25,17},{2,10},{10... | collective-permute-start | bytes 2359304 | tf_op jit(solution)/shard_map/ppermute | solution.py:372
  105.6 17.8 %collective-permute-start.7 = (bf16[8,3,2,16,512]{4,3,2,1,0:T(8,128)(2,1)S(1)}, bf16[8,3,2,16,512]{4,3,2,1,0:T(8,128)(2,1)}, u32[]{:S(2)}, u32[]{:S(2)}) collective-permute-start(bf16[8,3,2,16,512]{4,3,2,1,0:T(8,128)(2,1)S(1)} %collective-permute-done.6.rest_1_), channel_id=1, source_target_pairs={{0,8},{8,0},{16,24},{24,16},{1,9},{9,1},{17,25},{25,17},{2,10},{10... | collective-permute-start | bytes 2359304 | tf_op jit(solution)/shard_map/ppermute | solution.py:372
  115.2 16.0 %collective-permute-start.2 = (bf16[8,2,2,16,512]{4,3,2,1,0:T(8,128)(2,1)S(1)}, bf16[8,2,2,16,512]{4,3,2,1,0:T(8,128)(2,1)S(1)}, u32[]{:S(2)}, u32[]{:S(2)}) collective-permute-start(bf16[8,2,2,16,512]{4,3,2,1,0:T(8,128)(2,1)S(1)} %all-to-all-done.own), channel_id=1, source_target_pairs={{0,8},{8,0},{16,24},{24,16},{1,9},{9,1},{17,25},{25,17},{2,10},{10... | collective-permute-start | bytes 1572872 | tf_op jit(solution)/shard_map/ppermute | solution.py:372
  115.2 16.0 %collective-permute-start.4 = (bf16[8,2,2,16,512]{4,3,2,1,0:T(8,128)(2,1)S(1)}, bf16[8,2,2,16,512]{4,3,2,1,0:T(8,128)(2,1)S(1)}, u32[]{:S(2)}, u32[]{:S(2)}) collective-permute-start(bf16[8,2,2,16,512]{4,3,2,1,0:T(8,128)(2,1)S(1)} %collective-permute-done.3.rest_1_), channel_id=1, source_target_pairs={{0,8},{8,0},{16,24},{24,16},{1,9},{9,1},{17,25},{25,17},{2,10},{10... | collective-permute-start | bytes 1572872 | tf_op jit(solution)/shard_map/ppermute | solution.py:372
where the time goes:
time: 137 us; the launch traced here: 136 us
  waiting for transfers between devices  48 us (35%)
  Pallas kernels  37.2 us (27%)
  blocking collectives  24.1 us (18%)
  starting transfers between devices  18.9 us (14%)
  local copies, waits for them, and re-layouts  7.65 us (6%)
    all_to_all x2, waiting for transfers between devices, per_device(): mine = lax.all_to_all(chunk, 'tm', split_axis=0, concat_axis=0, tiled=True)  29.8 us
    all_to_all x1, blocking collectives, per_device(): mine = lax.all_to_all(chunk, 'tm', split_axis=0, concat_axis=0, tiled=True)  24.1 us
    pallas_call x3, Pallas kernels, cross_products(): pl.pallas_call(functools.partial(cross_kernel, 1.0 / (sources * windows),...  20.3 us
    ppermute x9, waiting for transfers between devices, swapped(): return lax.ppermute(shard, axis, [(i, i ^ bit) for i in range(devices)])  14.2 us
    pallas_call x1, Pallas kernels, own_spectra(): pl.pallas_call(spectra_kernel, out_shape=jax.ShapeDtypeStruct((BINS, 2, w...  10.2 us
    unnamed x10, local copies, waits for them, and re-layouts  7.65 us
    all_to_all x2, starting transfers between devices, per_device(): mine = lax.all_to_all(chunk, 'tm', split_axis=0, concat_axis=0, tiled=True)  7.13 us
    ppermute x2, starting transfers between devices, from_behind(): return lax.ppermute(shard, axis, pairs)  6.16 us
  transfers between devices with their start and end apart: 13, of which 6 were waited for; matrix products, arithmetic and copies ran while one was open for 0% of the time, Pallas kernels for 20%

commit v1 on v0

--- a/solution.py
+++ b/solution.py
@@ -81,6 +81,7 @@
         out_shape=jax.ShapeDtypeStruct((channels, RIM), BF16),
         in_specs=[smem, smem, pl.BlockSpec((channels, RIM), lambda i: (0, slab // RIM - 1))],
         out_specs=pl.BlockSpec(memory_space=pltpu.VMEM),
+        compiler_params=pltpu.CompilerParams(vmem_limit_bytes=50 * MIB),
         name="outbox",
     )(offsets, valid, record)
 
@@ -171,7 +172,7 @@
         in_specs=[vmem, pl.BlockSpec((channels, lead), lambda i: (0, 0)), vmem, vmem, vmem],
         out_specs=vmem,
         scratch_shapes=[pltpu.VMEM((max(channels // 128, 1), 2 * GROUP * BINS, 128), F32)],
-        compiler_params=pltpu.CompilerParams(vmem_limit_bytes=24 * MIB),
+        compiler_params=pltpu.CompilerParams(vmem_limit_bytes=50 * MIB),
         cost_estimate=pl.CostEstimate(
             flops=2 * channels * LANES * 3072, bytes_accessed=4 * channels * lead, transcendentals=0
         ),
@@ -260,7 +261,7 @@
             pltpu.VMEM((max(channels // 128, 1), LANES * windows, 128), F32),
             pltpu.SemaphoreType.DMA((slab // L,)),
         ],
-        compiler_params=pltpu.CompilerParams(vmem_limit_bytes=40 * MIB),
+        compiler_params=pltpu.CompilerParams(vmem_limit_bytes=50 * MIB),
         cost_estimate=pl.CostEstimate(
             flops=2 * channels * LANES * 896 * windows, bytes_accessed=4 * channels * slab, transcendentals=0
         ),
@@ -310,13 +311,14 @@
 
 
 def cross_kernel(scale, stacked, me, own, *rest):
-    out = rest[-1]
+    out, done = rest[-2:]
+    done[...] = jnp.zeros_like(done)
     sources, _, _, windows, channels = own.shape
     depth = sources * 2 * windows
     straight = own[:, 0].reshape(depth, channels)
     turned = jnp.concatenate([own[:, 0, 1:], -own[:, 0, :1]], axis=1).reshape(depth, channels)
     left = jnp.concatenate([straight, turned], axis=1)
-    blocks = rest[0].shape[0] if stacked else len(rest) - 1
+    blocks = rest[0].shape[0] if stacked else len(rest) - 2
     for n in range(blocks):
         if stacked:
             right, at = rest[0][n, :, 0], channels * n
@@ -345,8 +347,7 @@
         operands += others
         in_specs += [spec] * len(others)
     if result is None:
-        result = jnp.zeros((8, 128), BF16)
-        aliases = {}
+        result, aliases = operands[0], {}
     else:
         aliases = {len(operands): 0}
     operands.append(result)
@@ -355,9 +356,12 @@
     return pl.pallas_call(
         functools.partial(cross_kernel, 1.0 / (sources * windows), stacked),
         grid=(count,),
-        out_shape=jax.ShapeDtypeStruct(shape, BF16),
+        out_shape=(jax.ShapeDtypeStruct(shape, BF16), jax.ShapeDtypeStruct((8, 128), F32)),
         in_specs=in_specs,
-        out_specs=pl.BlockSpec((1,) + shape[1:], lambda f: (begin + f, 0, 0, 0)),
+        out_specs=(
+            pl.BlockSpec((1,) + shape[1:], lambda f: (begin + f, 0, 0, 0)),
+            pl.BlockSpec(memory_space=pltpu.VMEM),
+        ),
         input_output_aliases=aliases,
         compiler_params=pltpu.CompilerParams(vmem_limit_bytes=36 * MIB),
         cost_estimate=pl.CostEstimate(
@@ -372,30 +376,61 @@
     return lax.ppermute(shard, axis, [(i, i ^ bit) for i in range(devices)])
 
 
-def gathered(mine):
-    devices = lax.axis_size("chan")
-    if devices & (devices - 1) or mine.shape[-1] % 128:
-        return lax.all_gather(mine, "chan", axis=0, tiled=False)
-    held = {0: mine}
-    bit = devices // 2
+def fan(shard, axis, bit):
+    held = {0: shard}
     while bit:
-        held.update({n | bit: swapped(block, "chan", bit) for n, block in list(held.items())})
+        held.update({n | bit: swapped(block, axis, bit) for n, block in list(held.items())})
         bit //= 2
-    return [held[n] for n in range(1, devices)]
+    return held
+
+
+def after_kernel(shard, done, out):
+    pass
+
+
+def after(shard, done):
+    if done is None:
+        return shard
+    anywhere = pl.BlockSpec(memory_space=pl.ANY)
+    return pl.pallas_call(
+        after_kernel,
+        out_shape=jax.ShapeDtypeStruct(shard.shape, shard.dtype),
+        in_specs=[anywhere, anywhere],
+        out_specs=anywhere,
+        input_output_aliases={0: 0},
+        name="after",
+    )(shard, done)
 
 
 def per_device(record, whitening, offsets, window_valid):
     devices = lax.axis_size("tm")
+    blocks = lax.axis_size("chan")
+    stacked = blocks & (blocks - 1) != 0 or record.shape[0] % 128 != 0
+    top = blocks // 2
+    inbox = from_behind(outbox(record, offsets, window_valid), "tm", 1)
+    transform, rise, fall = tables(whitening)
+    parts = from_behind(border_parts(record, inbox, transform, rise, fall), "tm", -1)
+    own = own_spectra(record, inbox, offsets, window_valid, transform, rise, fall)
+    chunks = joined_chunks(own, parts, devices)
     bins = BINS // devices
-    inbox = from_behind(outbox(record, offsets, window_valid), "tm", 1)
-    blocks, rise, fall = tables(whitening)
-    parts = from_behind(border_parts(record, inbox, blocks, rise, fall), "tm", -1)
-    own = own_spectra(record, inbox, offsets, window_valid, blocks, rise, fall)
-    result, begin = None, 0
-    for chunk in joined_chunks(own, parts, devices):
-        mine = lax.all_to_all(chunk, "tm", split_axis=0, concat_axis=0, tiled=True)
-        result = cross_products(mine, gathered(mine), result, begin, bins)
-        begin += chunk.shape[1]
+    sizes = chunk_sizes(bins)
+    held, result, done = [], None, None
+    for p in range(len(sizes) + 1):
+        if p < len(sizes):
+            mine = lax.all_to_all(chunks[p], "tm", split_axis=0, concat_axis=0, tiled=True)
+            mine = after(mine, done)
+            if stacked:
+                held.append((mine, lax.all_gather(mine, "chan", axis=0, tiled=False)))
+            else:
+                held.append((fan(mine, "chan", top // 2), swapped(mine, "chan", top)))
+        if p:
+            if stacked:
+                mine, others = held[p - 1]
+            else:
+                near, far = held[p - 1]
+                found = near | {n | top: block for n, block in fan(after(far, done), "chan", top // 2).items()}
+                mine, others = found[0], [found[n] for n in range(1, blocks)]
+            result, done = cross_products(mine, others, result, sum(sizes[: p - 1]), bins)
     return result
 
 

time: 137 us -> 123 us (0.90)
  waiting for transfers between devices: 48 us -> 32.5 us
  local copies, waits for them, and re-layouts: 7.65 us -> 9.05 us
    all_to_all x2, waiting for transfers between devices: 29.8 us -> 2.34 us  [per_device(): lax.all_to_all(chunks[p], 'tm', split_axis=0, concat_axis=0, tiled=True)]
    ppermute x9, waiting for transfers between devices: 14.2 us -> 26.4 us  [swapped(): return lax.ppermute(shard, axis, [(i, i ^ bit) for i in range(devices)])]
    pallas_call x1, Pallas kernels: 1.3 us -> 3.33 us  [border_parts(): pl.pallas_call(border_kernel, grid=(1,), out_shape=jax.ShapeDtypeStruct((...]
    ppermute x9, starting transfers between devices: 5.6 us -> 3.59 us  [swapped(): return lax.ppermute(shard, axis, [(i, i ^ bit) for i in range(devices)])]
    unnamed x10 -> x28, local copies, waits for them, and re-layouts: 7.65 us -> 9.05 us
  transfers between devices with their start and end apart: 13 -> 13, of which waited for: 6 -> 7; matrix products, arithmetic and copies ran while one was open for 0% -> 0% of each run, Pallas kernels for 20% -> 22%
where the time goes in v1:
time: 123 us; the launch traced here: 122 us
  Pallas kernels  38.5 us (31%)
  waiting for transfers between devices  32.5 us (26%)
  blocking collectives  24.1 us (20%)
  starting transfers between devices  17.9 us (15%)
  local copies, waits for them, and re-layouts  9.05 us (7%)
    ppermute x9, waiting for transfers between devices, swapped(): return lax.ppermute(shard, axis, [(i, i ^ bit) for i in range(devices)])  26.4 us
    all_to_all x1, blocking collectives, per_device(): lax.all_to_all(chunks[p], 'tm', split_axis=0, concat_axis=0, tiled=True)  24.1 us
    pallas_call x3, Pallas kernels, cross_products(): pl.pallas_call(functools.partial(cross_kernel, 1.0 / (sources * windows),...  20.2 us
    pallas_call x1, Pallas kernels, own_spectra(): pl.pallas_call(spectra_kernel, out_shape=jax.ShapeDtypeStruct((BINS, 2, w...  10.3 us
    unnamed x28, local copies, waits for them, and re-layouts  9.05 us
    all_to_all x2, starting transfers between devices, per_device(): lax.all_to_all(chunks[p], 'tm', split_axis=0, concat_axis=0, tiled=True)  8.18 us
    ppermute x2, starting transfers between devices, from_behind(): return lax.ppermute(shard, axis, pairs)  6.17 us
    ppermute x2, waiting for transfers between devices, from_behind(): return lax.ppermute(shard, axis, pairs)  3.73 us
  transfers between devices with their start and end apart: 13, of which 7 were waited for; matrix products, arithmetic and copies ran while one was open for 0% of the time, Pallas kernels for 22%

profile of v1, /device:TPU:0, one launch (start us, length us, event | category | flops | bytes accessed | tf_op | source)
XLA Modules:
  0.0 122.3 jit_solution(12092823520576490369)
XLA Ops:
  1.3 1.0 outbox.1
  2.3 4.9 %collective-permute-start = (bf16[512,128]{1,0:T(8,128)(2,1)S(1)}, bf16[512,128]{1,0:T(8,128)(2,1)S(1)}, u32[]{:S(2)}, u32[]{:S(2)}) collective-permute-start(bf16[512,128]{1,0:T(8,128)(2,1)S(1)} %outbox.1), channel_id=1, source_target_pairs={{0,1},{1,2},{2,3},{3,4},{4,5},{5,6},{6,7},{8,9},{9,10},{10,11},{11... | collective-permute-start | bytes 393224 | tf_op jit(solution)/shard_map/ppermute | solution.py:30
  7.2 1.2 copy-done.6
  10.1 3.3 %border_parts.1 = bf16[64,8,512]{2,1,0:T(8,128)(2,1)S(1)} custom-call(bf16[512,128]{1,0:T(8,128)(2,1)S(1)} %collective-permute-done.rim.inbox, f32[512,8192]{1,0:T(8,128)} %record.5, bf16[2048,128]{1,0:T(8,128)(2,1)S(1)} %get-tuple-element.16.blocks, f32[384,128]{1,0:T(8,128)S(1)} %get-tuple-element.17.rise, f32[512,128]{1,0:T(8,128)S(1)} %get-tuple-element.18.fall), custom_call_target="tpu_custom_call" | custom-call | flops 402653184 | bytes 3670016 | tf_op jit(solution)/shard_map/border_parts/pallas_call | solution.py:168
  13.4 1.3 %collective-permute-start.1 = (bf16[64,8,512]{2,1,0:T(8,128)(2,1)S(1)}, bf16[64,8,512]{2,1,0:T(8,128)(2,1)S(1)}, u32[]{:S(2)}, u32[]{:S(2)}) collective-permute-start(bf16[64,8,512]{2,1,0:T(8,128)(2,1)S(1)} %border_parts.1), channel_id=1, source_target_pairs={{1,0},{2,1},{3,2},{4,3},{5,4},{6,5},{7,6},{9,8},{10,9},{11,10},{12... | collective-permute-start | bytes 1572872 | tf_op jit(solution)/shard_map/ppermute | solution.py:30
  14.7 10.3 %own_spectra.1.own = bf16[64,2,16,512]{3,2,1,0:T(8,128)(2,1)S(1)} custom-call(s32[16]{0:T(128)S(1)} %copy-done.10, s32[16]{0:T(128)S(1)} %copy-done.12, f32[512,8192]{1,0:T(8,128)} %record.5, bf16[512,128]{1,0:T(8,128)(2,1)S(1)} %collective-permute-done.rim.inbox, bf16[2048,128]{1,0:T(8,128)(2,1)S(1)} %get-tuple-element.16.blocks, ...), custom_call_target="tpu_custom_call" | custom-call | flops 1879048192 | bytes 16777216 | tf_op jit(solution)/shard_map/own_spectra/pallas_call | solution.py:253
  25.0 3.7 %collective-permute-done.1.parts = bf16[64,8,512]{2,1,0:T(8,128)(2,1)S(1)} collective-permute-done((bf16[64,8,512]{2,1,0:T(8,128)(2,1)S(1)}, bf16[64,8,512]{2,1,0:T(8,128)(2,1)S(1)}, u32[]{:S(2)}, u32[]{:S(2)}) %collective-permute-start.1) | collective-permute-done | bytes 524320 | tf_op jit(solution)/shard_map/ppermute | solution.py:30
  28.7 2.8 %joined_chunks.1 = (bf16[8,3,2,16,512]{4,3,2,1,0:T(8,128)(2,1)S(1)}, bf16[8,3,2,16,512]{4,3,2,1,0:T(8,128)(2,1)}, bf16[8,2,2,16,512]{4,3,2,1,0:T(8,128)(2,1)}) custom-call(bf16[64,2,16,512]{3,2,1,0:T(8,128)(2,1)S(1)} %own_spectra.1.own, bf16[64,8,512]{2,1,0:T(8,128)(2,1)S(1)} %collective-permute-done.1.parts), custom_call_target="tpu_custom_call" | custom-call | tf_op jit(solution)/shard_map/joined_chunks/pallas_call | solution.py:299
  31.5 24.1 %all_to_all.15.own = bf16[8,3,2,16,512]{4,3,2,1,0:T(8,128)(2,1)S(1)} all-to-all(bf16[8,3,2,16,512]{4,3,2,1,0:T(8,128)(2,1)S(1)} %get-tuple-element.20), channel_id=1, replica_groups=mesh['chan'=4,'tm'=8] {'tm'}, dimensions={0} | all-to-all | bytes 1572864 | tf_op jit(solution)/shard_map/all_to_all | solution.py:420
  55.6 3.6 %all-to-all-start.2 = ((bf16[8,3,2,16,512]{4,3,2,1,0:T(8,128)(2,1)}), bf16[8,3,2,16,512]{4,3,2,1,0:T(8,128)(2,1)S(1)}, u32[]{:S(2)}, u32[]{:S(2)}) async-start(bf16[8,3,2,16,512]{4,3,2,1,0:T(8,128)(2,1)} %get-tuple-element.22), calls=%async_computation.2 | async-start | bytes 1572864 | tf_op jit(solution)/shard_map/all_to_all | solution.py:420
  59.2 1.5 %collective-permute-start.3 = (bf16[8,3,2,16,512]{4,3,2,1,0:T(8,128)(2,1)S(1)}, bf16[8,3,2,16,512]{4,3,2,1,0:T(8,128)(2,1)}, u32[]{:S(2)}, u32[]{:S(2)}) collective-permute-start(bf16[8,3,2,16,512]{4,3,2,1,0:T(8,128)(2,1)S(1)} %all_to_all.15.own), channel_id=1, source_target_pairs={{0,16},{8,24},{16,0},{24,8},{1,17},{9,25},{17,1},{25,9},{2,18},{10... | collective-permute-start | bytes 2359304 | tf_op jit(solution)/shard_map/ppermute | solution.py:376
  60.8 16.4 %collective-permute-done.3.rest_1_ = bf16[8,3,2,16,512]{4,3,2,1,0:T(8,128)(2,1)} collective-permute-done((bf16[8,3,2,16,512]{4,3,2,1,0:T(8,128)(2,1)S(1)}, bf16[8,3,2,16,512]{4,3,2,1,0:T(8,128)(2,1)}, u32[]{:S(2)}, u32[]{:S(2)}) %collective-permute-start.3) | collective-permute-done | bytes 786464 | tf_op jit(solution)/shard_map/ppermute | solution.py:376
  77.2 1.1 all-to-all-done.2.own
  78.3 1.5 %collective-permute-start.8 = (bf16[8,3,2,16,512]{4,3,2,1,0:T(8,128)(2,1)S(1)}, bf16[8,3,2,16,512]{4,3,2,1,0:T(8,128)(2,1)S(1)}, u32[]{:S(2)}, u32[]{:S(2)}) collective-permute-start(bf16[8,3,2,16,512]{4,3,2,1,0:T(8,128)(2,1)S(1)} %all-to-all-done.2.own), channel_id=1, source_target_pairs={{0,16},{8,24},{16,0},{24,8},{1,17},{9,25},{17,1},{25,9},{2,18},{10... | collective-permute-start | bytes 2359304 | tf_op jit(solution)/shard_map/ppermute | solution.py:376
  79.8 4.6 %all-to-all-start = ((bf16[8,2,2,16,512]{4,3,2,1,0:T(8,128)(2,1)}), bf16[8,2,2,16,512]{4,3,2,1,0:T(8,128)(2,1)S(1)}, u32[]{:S(2)}, u32[]{:S(2)}) async-start(bf16[8,2,2,16,512]{4,3,2,1,0:T(8,128)(2,1)} %get-tuple-element.19), calls=%async_computation | async-start | bytes 1048576 | tf_op jit(solution)/shard_map/all_to_all | solution.py:420
  84.5 7.8 %cross_products.3 = (bf16[8,2,512,2048]{3,2,1,0:T(8,128)(2,1)}, f32[8,128]{1,0:T(8,128)S(1)}) custom-call(s32[1]{0:T(128)} %bitcast.me.rest_3_, bf16[8,3,2,16,512]{4,3,2,1,0:T(8,128)(2,1)S(1)} %all_to_all.15.own, bf16[8,3,2,16,512]{4,3,2,1,0:T(8,128)(2,1)} %collective-permute-done.2.rest_0_, bf16[8,3,2,16,512]{4,3,2,1,0:T(8,128)(2,1)} %collective-permute-done.3.rest_1_, ...), custom_call_target="tpu_custom_call" | custom-call | flops 3221225472 | bytes 12582912 | tf_op jit(solution)/shard_map/cross_products/pallas_call | solution.py:356
  92.8 4.4 %collective-permute-done.8.shard = bf16[8,3,2,16,512]{4,3,2,1,0:T(8,128)(2,1)S(1)} collective-permute-done((bf16[8,3,2,16,512]{4,3,2,1,0:T(8,128)(2,1)S(1)}, bf16[8,3,2,16,512]{4,3,2,1,0:T(8,128)(2,1)S(1)}, u32[]{:S(2)}, u32[]{:S(2)}) %collective-permute-start.8) | collective-permute-done | bytes 786464 | tf_op jit(solution)/shard_map/ppermute | solution.py:376
  98.1 1.2 all-to-all-done.shard
  100.7 1.1 copy-done.3
  101.8 7.6 %cross_products.4 = (bf16[8,2,512,2048]{3,2,1,0:T(8,128)(2,1)}, f32[8,128]{1,0:T(8,128)S(1)}) custom-call(s32[1]{0:T(128)} %bitcast.me.rest_3_, bf16[8,3,2,16,512]{4,3,2,1,0:T(8,128)(2,1)S(1)} %all-to-all-done.2.own, bf16[8,3,2,16,512]{4,3,2,1,0:T(8,128)(2,1)} %collective-permute-done.7.rest_0_, ...), custom_call_target="tpu_custom_call", output_to_operand_aliasing={{0}: (5, {})} | custom-call | flops 3221225472 | bytes 12582912 | tf_op jit(solution)/shard_map/cross_products/pallas_call | solution.py:356
  109.9 3.5 %collective-permute-done.6.shard = bf16[8,2,2,16,512]{4,3,2,1,0:T(8,128)(2,1)S(1)} collective-permute-done((bf16[8,2,2,16,512]{4,3,2,1,0:T(8,128)(2,1)}, bf16[8,2,2,16,512]{4,3,2,1,0:T(8,128)(2,1)S(1)}, u32[]{:S(2)}, u32[]{:S(2)}) %collective-permute-start.6) | collective-permute-done | bytes 524320 | tf_op jit(solution)/shard_map/ppermute | solution.py:376
  114.2 2.1 %collective-permute-done.10.rest_2_ = bf16[8,2,2,16,512]{4,3,2,1,0:T(8,128)(2,1)S(1)} collective-permute-done((bf16[8,2,2,16,512]{4,3,2,1,0:T(8,128)(2,1)}, bf16[8,2,2,16,512]{4,3,2,1,0:T(8,128)(2,1)S(1)}, u32[]{:S(2)}, u32[]{:S(2)}) %collective-permute-start.10) | collective-permute-done | bytes 524320 | tf_op jit(solution)/shard_map/ppermute | solution.py:376
  116.4 1.0 copy-done.5
  117.4 4.9 %cross_products.5 = (bf16[8,2,512,2048]{3,2,1,0:T(8,128)(2,1)}, f32[8,128]{1,0:T(8,128)}) custom-call(s32[1]{0:T(128)} %bitcast.me.rest_3_, bf16[8,2,2,16,512]{4,3,2,1,0:T(8,128)(2,1)S(1)} %copy-done.1, bf16[8,2,2,16,512]{4,3,2,1,0:T(8,128)(2,1)S(1)} %collective-permute-done.5.rest_0_, ...), custom_call_target="tpu_custom_call", output_to_operand_aliasing={{0}: (5, {})} | custom-call | flops 2147483648 | bytes 8388608 | tf_op jit(solution)/shard_map/cross_products/pallas_call | solution.py:356
  (42 shorter events, 7.2 us)
Async XLA Ops:
  0.0 0.7 copy-start.9
  0.7 0.7 copy-start.11
  1.3 13.4 %copy-start.10 = (s32[16]{0:T(128)S(1)}, s32[16]{0:T(128)}, u32[]{:S(2)}) copy-start(s32[16]{0:T(128)} %offsets.3) | copy-start | bytes 196
  1.3 13.4 %copy-start.12 = (s32[16]{0:T(128)S(1)}, s32[16]{0:T(128)}, u32[]{:S(2)}) copy-start(s32[16]{0:T(128)} %valid.3) | copy-start | bytes 196
  2.3 7.8 %collective-permute-start = (bf16[512,128]{1,0:T(8,128)(2,1)S(1)}, bf16[512,128]{1,0:T(8,128)(2,1)S(1)}, u32[]{:S(2)}, u32[]{:S(2)}) collective-permute-start(bf16[512,128]{1,0:T(8,128)(2,1)S(1)} %outbox.1), channel_id=1, source_target_pairs={{0,1},{1,2},{2,3},{3,4},{4,5},{5,6},{6,7},{8,9},{9,10},{10,11},{11... | collective-permute-start | bytes 393224 | tf_op jit(solution)/shard_map/ppermute | solution.py:30
  7.2 1.2 %copy-start.6 = (f32[2048,128]{1,0:T(8,128)S(1)}, f32[2048,128]{1,0:T(8,128)}, u32[]{:S(2)}) copy-start(f32[2048,128]{1,0:T(8,128)} %constant.7.clone.table) | copy-start | bytes 3145732
  13.4 15.3 %collective-permute-start.1 = (bf16[64,8,512]{2,1,0:T(8,128)(2,1)S(1)}, bf16[64,8,512]{2,1,0:T(8,128)(2,1)S(1)}, u32[]{:S(2)}, u32[]{:S(2)}) collective-permute-start(bf16[64,8,512]{2,1,0:T(8,128)(2,1)S(1)} %border_parts.1), channel_id=1, source_target_pairs={{1,0},{2,1},{3,2},{4,3},{5,4},{6,5},{7,6},{9,8},{10,9},{11,10},{12... | collective-permute-start | bytes 1572872 | tf_op jit(solution)/shard_map/ppermute | solution.py:30
  55.6 22.7 %all-to-all-start.2 = ((bf16[8,3,2,16,512]{4,3,2,1,0:T(8,128)(2,1)}), bf16[8,3,2,16,512]{4,3,2,1,0:T(8,128)(2,1)S(1)}, u32[]{:S(2)}, u32[]{:S(2)}) async-start(bf16[8,3,2,16,512]{4,3,2,1,0:T(8,128)(2,1)} %get-tuple-element.22), calls=%async_computation.2 | async-start | bytes 1572864 | tf_op jit(solution)/shard_map/all_to_all | solution.py:420
  59.2 18.0 %collective-permute-start.3 = (bf16[8,3,2,16,512]{4,3,2,1,0:T(8,128)(2,1)S(1)}, bf16[8,3,2,16,512]{4,3,2,1,0:T(8,128)(2,1)}, u32[]{:S(2)}, u32[]{:S(2)}) collective-permute-start(bf16[8,3,2,16,512]{4,3,2,1,0:T(8,128)(2,1)S(1)} %all_to_all.15.own), channel_id=1, source_target_pairs={{0,16},{8,24},{16,0},{24,8},{1,17},{9,25},{17,1},{25,9},{2,18},{10... | collective-permute-start | bytes 2359304 | tf_op jit(solution)/shard_map/ppermute | solution.py:376
  60.8 23.7 %collective-permute-start.2 = (bf16[8,3,2,16,512]{4,3,2,1,0:T(8,128)(2,1)S(1)}, bf16[8,3,2,16,512]{4,3,2,1,0:T(8,128)(2,1)}, u32[]{:S(2)}, u32[]{:S(2)}) collective-permute-start(bf16[8,3,2,16,512]{4,3,2,1,0:T(8,128)(2,1)S(1)} %all_to_all.15.own), channel_id=1, source_target_pairs={{0,8},{8,0},{16,24},{24,16},{1,9},{9,1},{17,25},{25,17},{2,10},{10... | collective-permute-start | bytes 2359304 | tf_op jit(solution)/shard_map/ppermute | solution.py:376
  77.2 7.2 %collective-permute-start.4 = (bf16[8,3,2,16,512]{4,3,2,1,0:T(8,128)(2,1)}, bf16[8,3,2,16,512]{4,3,2,1,0:T(8,128)(2,1)}, u32[]{:S(2)}, u32[]{:S(2)}) collective-permute-start(bf16[8,3,2,16,512]{4,3,2,1,0:T(8,128)(2,1)} %collective-permute-done.3.rest_1_), channel_id=1, source_target_pairs={{0,8},{8,0},{16,24},{24,16},{1,9},{9,1},{17,25},{25,17},{2,10},{10... | collective-permute-start | bytes 2359304 | tf_op jit(solution)/shard_map/ppermute | solution.py:376
  78.3 18.8 %collective-permute-start.8 = (bf16[8,3,2,16,512]{4,3,2,1,0:T(8,128)(2,1)S(1)}, bf16[8,3,2,16,512]{4,3,2,1,0:T(8,128)(2,1)S(1)}, u32[]{:S(2)}, u32[]{:S(2)}) collective-permute-start(bf16[8,3,2,16,512]{4,3,2,1,0:T(8,128)(2,1)S(1)} %all-to-all-done.2.own), channel_id=1, source_target_pairs={{0,16},{8,24},{16,0},{24,8},{1,17},{9,25},{17,1},{25,9},{2,18},{10... | collective-permute-start | bytes 2359304 | tf_op jit(solution)/shard_map/ppermute | solution.py:376
  79.8 19.5 %all-to-all-start = ((bf16[8,2,2,16,512]{4,3,2,1,0:T(8,128)(2,1)}), bf16[8,2,2,16,512]{4,3,2,1,0:T(8,128)(2,1)S(1)}, u32[]{:S(2)}, u32[]{:S(2)}) async-start(bf16[8,2,2,16,512]{4,3,2,1,0:T(8,128)(2,1)} %get-tuple-element.19), calls=%async_computation | async-start | bytes 1048576 | tf_op jit(solution)/shard_map/all_to_all | solution.py:420
  84.4 16.2 %collective-permute-start.7 = (bf16[8,3,2,16,512]{4,3,2,1,0:T(8,128)(2,1)S(1)}, bf16[8,3,2,16,512]{4,3,2,1,0:T(8,128)(2,1)}, u32[]{:S(2)}, u32[]{:S(2)}) collective-permute-start(bf16[8,3,2,16,512]{4,3,2,1,0:T(8,128)(2,1)S(1)} %all-to-all-done.2.own), channel_id=1, source_target_pairs={{0,8},{8,0},{16,24},{24,16},{1,9},{9,1},{17,25},{25,17},{2,10},{10... | collective-permute-start | bytes 2359304 | tf_op jit(solution)/shard_map/ppermute | solution.py:376
  97.2 0.9 copy-start.2
  98.1 2.5 %collective-permute-start.9 = (bf16[8,3,2,16,512]{4,3,2,1,0:T(8,128)(2,1)}, bf16[8,3,2,16,512]{4,3,2,1,0:T(8,128)(2,1)S(1)}, u32[]{:S(2)}, u32[]{:S(2)}) collective-permute-start(bf16[8,3,2,16,512]{4,3,2,1,0:T(8,128)(2,1)} %after.4.rest_1_), channel_id=1, source_target_pairs={{0,8},{8,0},{16,24},{24,16},{1,9},{9,1},{17,25},{25,17},{2,10},{10... | collective-permute-start | bytes 2359304 | tf_op jit(solution)/shard_map/ppermute | solution.py:376
  99.3 0.8 copy-start
  100.1 16.3 %copy-start.1 = (bf16[8,2,2,16,512]{4,3,2,1,0:T(8,128)(2,1)S(1)}, bf16[8,2,2,16,512]{4,3,2,1,0:T(8,128)(2,1)}, u32[]{:S(2)}) copy-start(bf16[8,2,2,16,512]{4,3,2,1,0:T(8,128)(2,1)} %after.3.own) | copy-start | bytes 1572868
  100.1 13.3 %collective-permute-start.6 = (bf16[8,2,2,16,512]{4,3,2,1,0:T(8,128)(2,1)}, bf16[8,2,2,16,512]{4,3,2,1,0:T(8,128)(2,1)S(1)}, u32[]{:S(2)}, u32[]{:S(2)}) collective-permute-start(bf16[8,2,2,16,512]{4,3,2,1,0:T(8,128)(2,1)} %after.3.own), channel_id=1, source_target_pairs={{0,16},{8,24},{16,0},{24,8},{1,17},{9,25},{17,1},{25,9},{2,18},{10... | collective-permute-start | bytes 1572872 | tf_op jit(solution)/shard_map/ppermute | solution.py:376
  100.6 13.6 %collective-permute-start.5 = (bf16[8,2,2,16,512]{4,3,2,1,0:T(8,128)(2,1)}, bf16[8,2,2,16,512]{4,3,2,1,0:T(8,128)(2,1)S(1)}, u32[]{:S(2)}, u32[]{:S(2)}) collective-permute-start(bf16[8,2,2,16,512]{4,3,2,1,0:T(8,128)(2,1)} %after.3.own), channel_id=1, source_target_pairs={{0,8},{8,0},{16,24},{24,16},{1,9},{9,1},{17,25},{25,17},{2,10},{10... | collective-permute-start | bytes 1572872 | tf_op jit(solution)/shard_map/ppermute | solution.py:376
  100.6 1.1 copy-start.3
  113.4 0.8 copy-start.4
  114.2 2.1 %collective-permute-start.10 = (bf16[8,2,2,16,512]{4,3,2,1,0:T(8,128)(2,1)}, bf16[8,2,2,16,512]{4,3,2,1,0:T(8,128)(2,1)S(1)}, u32[]{:S(2)}, u32[]{:S(2)}) collective-permute-start(bf16[8,2,2,16,512]{4,3,2,1,0:T(8,128)(2,1)} %after.5.rest_1_), channel_id=1, source_target_pairs={{0,8},{8,0},{16,24},{24,16},{1,9},{9,1},{17,25},{25,17},{2,10},{10... | collective-permute-start | bytes 1572872 | tf_op jit(solution)/shard_map/ppermute | solution.py:376
  116.4 1.0 copy-start.5
  (3 other events, 1.8 us)

commit v2 on v1

--- a/solution.py
+++ b/solution.py
@@ -81,7 +81,7 @@
         out_shape=jax.ShapeDtypeStruct((channels, RIM), BF16),
         in_specs=[smem, smem, pl.BlockSpec((channels, RIM), lambda i: (0, slab // RIM - 1))],
         out_specs=pl.BlockSpec(memory_space=pltpu.VMEM),
-        compiler_params=pltpu.CompilerParams(vmem_limit_bytes=50 * MIB),
+        compiler_params=pltpu.CompilerParams(vmem_limit_bytes=60 * MIB),
         name="outbox",
     )(offsets, valid, record)
 
@@ -269,22 +269,24 @@
     )(offsets, valid, record, rim, blocks, rise, fall)
 
 
-def join_kernel(own, parts, *chunks):
+def join_kernel(sizes, devices, me, own, parts, *outs):
     windows = own.shape[2]
+    bins = sum(sizes)
     half = windows - 2 * GROUP
-    part = parts[...].astype(F32)
-    row = lax.broadcasted_iota(jnp.int32, part.shape, 1)
-    late = row >= GROUP
-    moved = jnp.concatenate([part[:, GROUP:], part[:, :GROUP]], axis=1)
-    for ri, extra in enumerate((moved, part)):
-        spectra = own[:, ri].astype(F32)
-        upper = spectra[:, half:] + jnp.where(late, extra, 0.0)
-        joined = jnp.concatenate([spectra[:, :half], upper], axis=1).astype(BF16)
-        begin = 0
-        for chunk in chunks:
-            count = chunk.shape[1]
-            chunk[0, :, ri] = joined[begin : begin + count]
-            begin += count
+    for d in range(devices):
+        group = me[0] ^ d
+        part = parts[pl.ds(group * bins, bins)].astype(F32)
+        row = lax.broadcasted_iota(jnp.int32, part.shape, 1)
+        moved = jnp.concatenate([part[:, GROUP:], part[:, :GROUP]], axis=1)
+        for ri, extra in enumerate((moved, part)):
+            spectra = own[pl.ds(group * bins, bins), ri].astype(F32)
+            upper = spectra[:, half:] + jnp.where(row >= GROUP, extra, 0.0)
+            joined = jnp.concatenate([spectra[:, :half], upper], axis=1).astype(BF16)
+            outs[d][:, ri] = joined[: sizes[0]]
+            begin = sizes[0]
+            for count, out in zip(sizes[1:], outs[devices:]):
+                out[pl.ds(group, 1), :, ri] = joined[begin : begin + count][None]
+                begin += count
 
 
 def chunk_sizes(bins):
@@ -294,20 +296,36 @@
 
 def joined_chunks(own, parts, devices):
     _, _, windows, channels = own.shape
-    bins = BINS // devices
-    shapes = [(devices, count, 2, windows, channels) for count in chunk_sizes(bins)]
-    return pl.pallas_call(
-        join_kernel,
-        grid=(devices,),
+    sizes = chunk_sizes(BINS // devices)
+    vmem = pl.BlockSpec(memory_space=pltpu.VMEM)
+    shapes = [(sizes[0], 2, windows, channels)] * devices
+    shapes += [(devices, count, 2, windows, channels) for count in sizes[1:]]
+    outs = pl.pallas_call(
+        functools.partial(join_kernel, sizes, devices),
         out_shape=tuple(jax.ShapeDtypeStruct(shape, BF16) for shape in shapes),
-        in_specs=[
-            pl.BlockSpec((bins, 2, windows, channels), lambda g: (g, 0, 0, 0)),
-            pl.BlockSpec((bins, 2 * GROUP, channels), lambda g: (g, 0, 0)),
-        ],
-        out_specs=tuple(pl.BlockSpec((1,) + shape[1:], lambda g: (g, 0, 0, 0, 0)) for shape in shapes),
+        in_specs=[pl.BlockSpec(memory_space=pltpu.SMEM), vmem, vmem],
+        out_specs=(vmem,) * len(shapes),
         compiler_params=pltpu.CompilerParams(vmem_limit_bytes=16 * MIB),
         name="joined_chunks",
-    )(own, parts)
+    )(lax.axis_index("tm").astype(jnp.int32).reshape(1), own, parts)
+    return outs[:devices], outs[devices:]
+
+
+def stack_kernel(*refs):
+    for d, piece in enumerate(refs[:-1]):
+        refs[-1][d] = piece[...]
+
+
+def stacked_pieces(pieces):
+    vmem = pl.BlockSpec(memory_space=pltpu.VMEM)
+    return pl.pallas_call(
+        stack_kernel,
+        out_shape=jax.ShapeDtypeStruct((len(pieces),) + pieces[0].shape, BF16),
+        in_specs=[vmem] * len(pieces),
+        out_specs=vmem,
+        compiler_params=pltpu.CompilerParams(vmem_limit_bytes=16 * MIB),
+        name="stacked_pieces",
+    )(*pieces)
 
 
 def cross_kernel(scale, stacked, me, own, *rest):
@@ -385,19 +403,19 @@
 
 
 def after_kernel(shard, done, out):
-    pass
+    out[...] = shard[...]
 
 
 def after(shard, done):
     if done is None:
         return shard
-    anywhere = pl.BlockSpec(memory_space=pl.ANY)
+    vmem = pl.BlockSpec(memory_space=pltpu.VMEM)
     return pl.pallas_call(
         after_kernel,
         out_shape=jax.ShapeDtypeStruct(shard.shape, shard.dtype),
-        in_specs=[anywhere, anywhere],
-        out_specs=anywhere,
-        input_output_aliases={0: 0},
+        in_specs=[vmem, vmem],
+        out_specs=vmem,
+        compiler_params=pltpu.CompilerParams(vmem_limit_bytes=8 * MIB),
         name="after",
     )(shard, done)
 
@@ -411,13 +429,17 @@
     transform, rise, fall = tables(whitening)
     parts = from_behind(border_parts(record, inbox, transform, rise, fall), "tm", -1)
     own = own_spectra(record, inbox, offsets, window_valid, transform, rise, fall)
-    chunks = joined_chunks(own, parts, devices)
+    pieces, chunks = joined_chunks(own, parts, devices)
     bins = BINS // devices
     sizes = chunk_sizes(bins)
+    pieces = [pieces[0]] + [swapped(pieces[d], "tm", d) for d in range(1, devices)]
     held, result, done = [], None, None
     for p in range(len(sizes) + 1):
         if p < len(sizes):
-            mine = lax.all_to_all(chunks[p], "tm", split_axis=0, concat_axis=0, tiled=True)
+            if p == 0:
+                mine = stacked_pieces(pieces)
+            else:
+                mine = lax.all_to_all(chunks[p - 1], "tm", split_axis=0, concat_axis=0, tiled=True)
             mine = after(mine, done)
             if stacked:
                 held.append((mine, lax.all_gather(mine, "chan", axis=0, tiled=False)))
@@ -428,7 +450,9 @@
                 mine, others = held[p - 1]
             else:
                 near, far = held[p - 1]
-                found = near | {n | top: block for n, block in fan(after(far, done), "chan", top // 2).items()}
+                if p == len(sizes):
+                    far = after(far, done)
+                found = near | {n | top: block for n, block in fan(far, "chan", top // 2).items()}
                 mine, others = found[0], [found[n] for n in range(1, blocks)]
             result, done = cross_products(mine, others, result, sum(sizes[: p - 1]), bins)
     return result

time: 123 us -> 133 us (1.081); the launches traced: 122 us -> 131 us
  blocking collectives: 24.1 us -> 0 us
  waiting for transfers between devices: 32.5 us -> 54 us
  starting transfers between devices: 17.9 us -> 36.7 us
  local copies, waits for them, and re-layouts: 9.05 us -> 1.88 us
    all_to_all x1 -> x0, blocking collectives: 24.1 us -> none  [per_device(): lax.all_to_all(chunks[p], 'tm', split_axis=0, concat_axis=0, tiled=True)]
    ppermute x9 -> x16, waiting for transfers between devices: 26.4 us -> 49.9 us  [swapped(): return lax.ppermute(shard, axis, [(i, i ^ bit) for i in range(devices)])]
    ppermute x9 -> x16, starting transfers between devices: 3.59 us -> 20.4 us  [swapped(): return lax.ppermute(shard, axis, [(i, i ^ bit) for i in range(devices)])]
    unnamed x28 -> x8, local copies, waits for them, and re-layouts: 9.05 us -> 1.88 us
    all_to_all x2, waiting for transfers between devices: 2.34 us -> 0.21 us  [per_device(): lax.all_to_all(chunks[p - 1], 'tm', split_axis=0, concat_axis=0, tiled=True)]
    all_to_all x2, starting transfers between devices: 8.18 us -> 10.1 us  [per_device(): lax.all_to_all(chunks[p - 1], 'tm', split_axis=0, concat_axis=0, tiled=True)]
    pallas_call x1 -> x2, Pallas kernels: 2.79 us -> 1.31 us  [the longest x1 1.26 us: joined_chunks(): pl.pallas_call(functools.partial(join_kernel, sizes, devices), out_shape=...]
  transfers between devices with their start and end apart: 13 -> 20, of which waited for: 7 -> 10; matrix products, arithmetic and copies ran while one was open for 0% -> 0% of each run, Pallas kernels for 22% -> 20%
where the time goes in v2:
time: 133 us; the launch traced here: 131 us
  waiting for transfers between devices  54 us (41%)
  Pallas kernels  37.8 us (28%)
  starting transfers between devices  36.7 us (28%)
  local copies, waits for them, and re-layouts  1.88 us (1%)
    ppermute x16, waiting for transfers between devices, swapped(): return lax.ppermute(shard, axis, [(i, i ^ bit) for i in range(devices)])  49.9 us
    ppermute x16, starting transfers between devices, swapped(): return lax.ppermute(shard, axis, [(i, i ^ bit) for i in range(devices)])  20.4 us
    pallas_call x3, Pallas kernels, cross_products(): pl.pallas_call(functools.partial(cross_kernel, 1.0 / (sources * windows),...  20.3 us
    pallas_call x1, Pallas kernels, own_spectra(): pl.pallas_call(spectra_kernel, out_shape=jax.ShapeDtypeStruct((BINS, 2, w...  10.2 us
    all_to_all x2, starting transfers between devices, per_device(): lax.all_to_all(chunks[p - 1], 'tm', split_axis=0, concat_axis=0, tiled=True)  10.1 us
    ppermute x2, starting transfers between devices, from_behind(): return lax.ppermute(shard, axis, pairs)  6.16 us
    ppermute x2, waiting for transfers between devices, from_behind(): return lax.ppermute(shard, axis, pairs)  3.98 us
    pallas_call x1, Pallas kernels, border_parts(): pl.pallas_call(border_kernel, grid=(1,), out_shape=jax.ShapeDtypeStruct((...  3.32 us
  transfers between devices with their start and end apart: 20, of which 10 were waited for; matrix products, arithmetic and copies ran while one was open for 0% of the time, Pallas kernels for 20%

profile of v2, /device:TPU:0, one launch (start us, length us, event | category | flops | bytes accessed | tf_op | source)
XLA Modules:
  0.0 130.6 jit_solution(13536614276882669943)
XLA Ops:
  0.0 1.7 %outbox.1 = bf16[512,128]{1,0:T(8,128)(2,1)} custom-call(s32[16]{0:T(128)} %offsets.3, s32[16]{0:T(128)} %valid.3, f32[512,8192]{1,0:T(8,128)} %record.5), custom_call_target="tpu_custom_call" | custom-call | tf_op jit(solution)/shard_map/outbox/pallas_call | solution.py:78
  1.7 4.9 %collective-permute-start = (bf16[512,128]{1,0:T(8,128)(2,1)}, bf16[512,128]{1,0:T(8,128)(2,1)S(1)}, u32[]{:S(2)}, u32[]{:S(2)}) collective-permute-start(bf16[512,128]{1,0:T(8,128)(2,1)} %outbox.1), channel_id=1, source_target_pairs={{0,1},{1,2},{2,3},{3,4},{4,5},{5,6},{6,7},{8,9},{9,10},{10,11},{11... | collective-permute-start | bytes 393224 | tf_op jit(solution)/shard_map/ppermute | solution.py:30
  9.6 3.3 %border_parts.1 = bf16[64,8,512]{2,1,0:T(8,128)(2,1)S(1)} custom-call(bf16[512,128]{1,0:T(8,128)(2,1)S(1)} %collective-permute-done.rim.inbox, f32[512,8192]{1,0:T(8,128)} %record.5, bf16[2048,128]{1,0:T(8,128)(2,1)S(1)} %get-tuple-element.23.blocks, f32[384,128]{1,0:T(8,128)S(1)} %get-tuple-element.24.rise, f32[512,128]{1,0:T(8,128)S(1)} %get-tuple-element.25.fall), custom_call_target="tpu_custom_call" | custom-call | flops 402653184 | bytes 3670016 | tf_op jit(solution)/shard_map/border_parts/pallas_call | solution.py:168
  14.2 10.2 %own_spectra.1.own = bf16[64,2,16,512]{3,2,1,0:T(8,128)(2,1)S(1)} custom-call(s32[16]{0:T(128)S(1)} %copy-done.1, s32[16]{0:T(128)S(1)} %copy-done.2, f32[512,8192]{1,0:T(8,128)} %record.5, bf16[512,128]{1,0:T(8,128)(2,1)S(1)} %collective-permute-done.rim.inbox, bf16[2048,128]{1,0:T(8,128)(2,1)S(1)} %get-tuple-element.23.blocks, ...), custom_call_target="tpu_custom_call" | custom-call | flops 1879048192 | bytes 16777216 | tf_op jit(solution)/shard_map/own_spectra/pallas_call | solution.py:253
  24.5 3.8 %collective-permute-done.1.parts = bf16[64,8,512]{2,1,0:T(8,128)(2,1)S(1)} collective-permute-done((bf16[64,8,512]{2,1,0:T(8,128)(2,1)S(1)}, bf16[64,8,512]{2,1,0:T(8,128)(2,1)S(1)}, u32[]{:S(2)}, u32[]{:S(2)}) %collective-permute-start.1) | collective-permute-done | bytes 524320 | tf_op jit(solution)/shard_map/ppermute | solution.py:30
  29.5 6.0 %all-to-all-start.1 = ((bf16[8,3,2,16,512]{4,3,2,1,0:T(8,128)(2,1)}), bf16[8,3,2,16,512]{4,3,2,1,0:T(8,128)(2,1)S(1)}, u32[]{:S(2)}, u32[]{:S(2)}) async-start(bf16[8,3,2,16,512]{4,3,2,1,0:T(8,128)(2,1)} %get-tuple-element.36), calls=%async_computation.1 | async-start | bytes 1572864 | tf_op jit(solution)/shard_map/all_to_all | solution.py:442
  35.5 2.0 %collective-permute-start.2 = (bf16[3,2,16,512]{3,2,1,0:T(8,128)(2,1)S(1)}, bf16[3,2,16,512]{3,2,1,0:T(8,128)(2,1)S(1)}, u32[]{:S(2)}, u32[]{:S(2)}) collective-permute-start(bf16[3,2,16,512]{3,2,1,0:T(8,128)(2,1)S(1)} %get-tuple-element.28), channel_id=1, source_target_pairs={{0,1},{1,0},{2,3},{3,2},{4,5},{5,4},{6,7},{7,6},{8,9},{9,8},{10,11... | collective-permute-start | bytes 294920 | tf_op jit(solution)/shard_map/ppermute | solution.py:394
  37.5 1.5 %collective-permute-start.3 = (bf16[3,2,16,512]{3,2,1,0:T(8,128)(2,1)S(1)}, bf16[3,2,16,512]{3,2,1,0:T(8,128)(2,1)S(1)}, u32[]{:S(2)}, u32[]{:S(2)}) collective-permute-start(bf16[3,2,16,512]{3,2,1,0:T(8,128)(2,1)S(1)} %get-tuple-element.29), channel_id=1, source_target_pairs={{0,2},{1,3},{2,0},{3,1},{4,6},{5,7},{6,4},{7,5},{8,10},{9,11},{10,... | collective-permute-start | bytes 294920 | tf_op jit(solution)/shard_map/ppermute | solution.py:394
  39.0 2.9 %collective-permute-start.5 = (bf16[3,2,16,512]{3,2,1,0:T(8,128)(2,1)S(1)}, bf16[3,2,16,512]{3,2,1,0:T(8,128)(2,1)S(1)}, u32[]{:S(2)}, u32[]{:S(2)}) collective-permute-start(bf16[3,2,16,512]{3,2,1,0:T(8,128)(2,1)S(1)} %get-tuple-element.31), channel_id=1, source_target_pairs={{0,4},{1,5},{2,6},{3,7},{4,0},{5,1},{6,2},{7,3},{8,12},{9,13},{10,... | collective-permute-start | bytes 294920 | tf_op jit(solution)/shard_map/ppermute | solution.py:394
  43.4 4.0 %collective-permute-start.7 = (bf16[3,2,16,512]{3,2,1,0:T(8,128)(2,1)S(1)}, bf16[3,2,16,512]{3,2,1,0:T(8,128)(2,1)S(1)}, u32[]{:S(2)}, u32[]{:S(2)}) collective-permute-start(bf16[3,2,16,512]{3,2,1,0:T(8,128)(2,1)S(1)} %get-tuple-element.33), channel_id=1, source_target_pairs={{0,6},{1,7},{2,4},{3,5},{4,2},{5,3},{6,0},{7,1},{8,14},{9,15},{10,... | collective-permute-start | bytes 294920 | tf_op jit(solution)/shard_map/ppermute | solution.py:394
  47.4 4.4 %collective-permute-done.3.refs_2_ = bf16[3,2,16,512]{3,2,1,0:T(8,128)(2,1)S(1)} collective-permute-done((bf16[3,2,16,512]{3,2,1,0:T(8,128)(2,1)S(1)}, bf16[3,2,16,512]{3,2,1,0:T(8,128)(2,1)S(1)}, u32[]{:S(2)}, u32[]{:S(2)}) %collective-permute-start.3) | collective-permute-done | bytes 98336 | tf_op jit(solution)/shard_map/ppermute | solution.py:394
  51.8 4.6 %collective-permute-start.8 = (bf16[3,2,16,512]{3,2,1,0:T(8,128)(2,1)S(1)}, bf16[3,2,16,512]{3,2,1,0:T(8,128)(2,1)S(1)}, u32[]{:S(2)}, u32[]{:S(2)}) collective-permute-start(bf16[3,2,16,512]{3,2,1,0:T(8,128)(2,1)S(1)} %get-tuple-element.34), channel_id=1, source_target_pairs={{0,7},{1,6},{2,5},{3,4},{4,3},{5,2},{6,1},{7,0},{8,15},{9,14},{10,... | collective-permute-start | bytes 294920 | tf_op jit(solution)/shard_map/ppermute | solution.py:394
  56.4 10.3 %collective-permute-done.5.refs_4_ = bf16[3,2,16,512]{3,2,1,0:T(8,128)(2,1)S(1)} collective-permute-done((bf16[3,2,16,512]{3,2,1,0:T(8,128)(2,1)S(1)}, bf16[3,2,16,512]{3,2,1,0:T(8,128)(2,1)S(1)}, u32[]{:S(2)}, u32[]{:S(2)}) %collective-permute-start.5) | collective-permute-done | bytes 98336 | tf_op jit(solution)/shard_map/ppermute | solution.py:394
  66.7 2.9 %collective-permute-done.6.refs_5_ = bf16[3,2,16,512]{3,2,1,0:T(8,128)(2,1)S(1)} collective-permute-done((bf16[3,2,16,512]{3,2,1,0:T(8,128)(2,1)S(1)}, bf16[3,2,16,512]{3,2,1,0:T(8,128)(2,1)S(1)}, u32[]{:S(2)}, u32[]{:S(2)}) %collective-permute-start.6) | collective-permute-done | bytes 98336 | tf_op jit(solution)/shard_map/ppermute | solution.py:394
  69.6 1.5 %collective-permute-start.10 = (bf16[8,3,2,16,512]{4,3,2,1,0:T(8,128)(2,1)S(1)}, bf16[8,3,2,16,512]{4,3,2,1,0:T(8,128)(2,1)}, u32[]{:S(2)}, u32[]{:S(2)}) collective-permute-start(bf16[8,3,2,16,512]{4,3,2,1,0:T(8,128)(2,1)S(1)} %stacked_pieces.1.own), channel_id=1, source_target_pairs={{0,16},{8,24},{16,0},{24,8},{1,17},{9,25},{17,1},{25,9},{2,18},{10... | collective-permute-start | bytes 2359304 | tf_op jit(solution)/shard_map/ppermute | solution.py:394
  71.7 18.6 %collective-permute-done.10.rest_1_ = bf16[8,3,2,16,512]{4,3,2,1,0:T(8,128)(2,1)} collective-permute-done((bf16[8,3,2,16,512]{4,3,2,1,0:T(8,128)(2,1)S(1)}, bf16[8,3,2,16,512]{4,3,2,1,0:T(8,128)(2,1)}, u32[]{:S(2)}, u32[]{:S(2)}) %collective-permute-start.10) | collective-permute-done | bytes 786464 | tf_op jit(solution)/shard_map/ppermute | solution.py:394
  90.2 4.1 %all-to-all-start = ((bf16[8,2,2,16,512]{4,3,2,1,0:T(8,128)(2,1)}), bf16[8,2,2,16,512]{4,3,2,1,0:T(8,128)(2,1)S(1)}, u32[]{:S(2)}, u32[]{:S(2)}) async-start(bf16[8,2,2,16,512]{4,3,2,1,0:T(8,128)(2,1)} %get-tuple-element.26), calls=%async_computation | async-start | bytes 1048576 | tf_op jit(solution)/shard_map/all_to_all | solution.py:442
  94.5 7.0 %collective-permute-done.15.rest_1_ = bf16[8,3,2,16,512]{4,3,2,1,0:T(8,128)(2,1)S(1)} collective-permute-done((bf16[8,3,2,16,512]{4,3,2,1,0:T(8,128)(2,1)S(1)}, bf16[8,3,2,16,512]{4,3,2,1,0:T(8,128)(2,1)S(1)}, u32[]{:S(2)}, u32[]{:S(2)}) %collective-permute-start.15) | collective-permute-done | bytes 786464 | tf_op jit(solution)/shard_map/ppermute | solution.py:394
  101.5 7.8 %cross_products.3 = (bf16[8,2,512,2048]{3,2,1,0:T(8,128)(2,1)}, f32[8,128]{1,0:T(8,128)S(1)}) custom-call(s32[1]{0:T(128)} %bitcast.me.rest_3_, bf16[8,3,2,16,512]{4,3,2,1,0:T(8,128)(2,1)S(1)} %stacked_pieces.1.own, bf16[8,3,2,16,512]{4,3,2,1,0:T(8,128)(2,1)} %collective-permute-done.9.rest_0_, bf16[8,3,2,16,512]{4,3,2,1,0:T(8,128)(2,1)} %collective-permute-done.10.rest_1_, ...), custom_call_target="tpu_custom_call" | custom-call | flops 3221225472 | bytes 12582912 | tf_op jit(solution)/shard_map/cross_products/pallas_call | solution.py:374
  109.5 1.5 %collective-permute-start.13 = (bf16[8,2,2,16,512]{4,3,2,1,0:T(8,128)(2,1)S(1)}, bf16[8,2,2,16,512]{4,3,2,1,0:T(8,128)(2,1)S(1)}, u32[]{:S(2)}, u32[]{:S(2)}) collective-permute-start(bf16[8,2,2,16,512]{4,3,2,1,0:T(8,128)(2,1)S(1)} %after.2.own), channel_id=1, source_target_pairs={{0,16},{8,24},{16,0},{24,8},{1,17},{9,25},{17,1},{25,9},{2,18},{10... | collective-permute-start | bytes 1572872 | tf_op jit(solution)/shard_map/ppermute | solution.py:394
  111.0 7.7 %cross_products.4 = (bf16[8,2,512,2048]{3,2,1,0:T(8,128)(2,1)}, f32[8,128]{1,0:T(8,128)S(1)}) custom-call(s32[1]{0:T(128)} %bitcast.me.rest_3_, bf16[8,3,2,16,512]{4,3,2,1,0:T(8,128)(2,1)S(1)} %all-to-all-done.1.own, bf16[8,3,2,16,512]{4,3,2,1,0:T(8,128)(2,1)} %collective-permute-done.14.rest_0_, ...), custom_call_target="tpu_custom_call", output_to_operand_aliasing={{0}: (5, {})} | custom-call | flops 3221225472 | bytes 12582912 | tf_op jit(solution)/shard_map/cross_products/pallas_call | solution.py:374
  118.7 5.0 %collective-permute-done.13.shard = bf16[8,2,2,16,512]{4,3,2,1,0:T(8,128)(2,1)S(1)} collective-permute-done((bf16[8,2,2,16,512]{4,3,2,1,0:T(8,128)(2,1)S(1)}, bf16[8,2,2,16,512]{4,3,2,1,0:T(8,128)(2,1)S(1)}, u32[]{:S(2)}, u32[]{:S(2)}) %collective-permute-start.13) | collective-permute-done | bytes 524320 | tf_op jit(solution)/shard_map/ppermute | solution.py:394
  123.8 1.9 %collective-permute-done.17.rest_2_ = bf16[8,2,2,16,512]{4,3,2,1,0:T(8,128)(2,1)S(1)} collective-permute-done((bf16[8,2,2,16,512]{4,3,2,1,0:T(8,128)(2,1)S(1)}, bf16[8,2,2,16,512]{4,3,2,1,0:T(8,128)(2,1)S(1)}, u32[]{:S(2)}, u32[]{:S(2)}) %collective-permute-start.17) | collective-permute-done | bytes 524320 | tf_op jit(solution)/shard_map/ppermute | solution.py:394
  125.7 4.9 %cross_products.5 = (bf16[8,2,512,2048]{3,2,1,0:T(8,128)(2,1)}, f32[8,128]{1,0:T(8,128)}) custom-call(s32[1]{0:T(128)} %bitcast.me.rest_3_, bf16[8,2,2,16,512]{4,3,2,1,0:T(8,128)(2,1)S(1)} %after.2.own, bf16[8,2,2,16,512]{4,3,2,1,0:T(8,128)(2,1)S(1)} %collective-permute-done.12.rest_0_, ...), custom_call_target="tpu_custom_call", output_to_operand_aliasing={{0}: (5, {})} | custom-call | flops 2147483648 | bytes 8388608 | tf_op jit(solution)/shard_map/cross_products/pallas_call | solution.py:374
  (35 shorter events, 8.3 us)
Async XLA Ops:
  0.0 14.2 %copy-start.1 = (s32[16]{0:T(128)S(1)}, s32[16]{0:T(128)}, u32[]{:S(2)}) copy-start(s32[16]{0:T(128)} %offsets.3) | copy-start | bytes 196
  0.0 14.2 %copy-start.2 = (s32[16]{0:T(128)S(1)}, s32[16]{0:T(128)}, u32[]{:S(2)}) copy-start(s32[16]{0:T(128)} %valid.3) | copy-start | bytes 196
  1.7 7.9 %collective-permute-start = (bf16[512,128]{1,0:T(8,128)(2,1)}, bf16[512,128]{1,0:T(8,128)(2,1)S(1)}, u32[]{:S(2)}, u32[]{:S(2)}) collective-permute-start(bf16[512,128]{1,0:T(8,128)(2,1)} %outbox.1), channel_id=1, source_target_pairs={{0,1},{1,2},{2,3},{3,4},{4,5},{5,6},{6,7},{8,9},{9,10},{10,11},{11... | collective-permute-start | bytes 393224 | tf_op jit(solution)/shard_map/ppermute | solution.py:30
  6.5 1.2 copy-start
  7.8 0.7 copy-start.3
  12.9 15.3 %collective-permute-start.1 = (bf16[64,8,512]{2,1,0:T(8,128)(2,1)S(1)}, bf16[64,8,512]{2,1,0:T(8,128)(2,1)S(1)}, u32[]{:S(2)}, u32[]{:S(2)}) collective-permute-start(bf16[64,8,512]{2,1,0:T(8,128)(2,1)S(1)} %border_parts.1), channel_id=1, source_target_pairs={{1,0},{2,1},{3,2},{4,3},{5,4},{6,5},{7,6},{9,8},{10,9},{11,10},{12... | collective-permute-start | bytes 1572872 | tf_op jit(solution)/shard_map/ppermute | solution.py:30
  29.5 41.6 %all-to-all-start.1 = ((bf16[8,3,2,16,512]{4,3,2,1,0:T(8,128)(2,1)}), bf16[8,3,2,16,512]{4,3,2,1,0:T(8,128)(2,1)S(1)}, u32[]{:S(2)}, u32[]{:S(2)}) async-start(bf16[8,3,2,16,512]{4,3,2,1,0:T(8,128)(2,1)} %get-tuple-element.36), calls=%async_computation.1 | async-start | bytes 1572864 | tf_op jit(solution)/shard_map/all_to_all | solution.py:442
  35.5 7.9 %collective-permute-start.2 = (bf16[3,2,16,512]{3,2,1,0:T(8,128)(2,1)S(1)}, bf16[3,2,16,512]{3,2,1,0:T(8,128)(2,1)S(1)}, u32[]{:S(2)}, u32[]{:S(2)}) collective-permute-start(bf16[3,2,16,512]{3,2,1,0:T(8,128)(2,1)S(1)} %get-tuple-element.28), channel_id=1, source_target_pairs={{0,1},{1,0},{2,3},{3,2},{4,5},{5,4},{6,7},{7,6},{8,9},{9,8},{10,11... | collective-permute-start | bytes 294920 | tf_op jit(solution)/shard_map/ppermute | solution.py:394
  37.5 14.2 %collective-permute-start.3 = (bf16[3,2,16,512]{3,2,1,0:T(8,128)(2,1)S(1)}, bf16[3,2,16,512]{3,2,1,0:T(8,128)(2,1)S(1)}, u32[]{:S(2)}, u32[]{:S(2)}) collective-permute-start(bf16[3,2,16,512]{3,2,1,0:T(8,128)(2,1)S(1)} %get-tuple-element.29), channel_id=1, source_target_pairs={{0,2},{1,3},{2,0},{3,1},{4,6},{5,7},{6,4},{7,5},{8,10},{9,11},{10,... | collective-permute-start | bytes 294920 | tf_op jit(solution)/shard_map/ppermute | solution.py:394
  39.0 17.4 %collective-permute-start.4 = (bf16[3,2,16,512]{3,2,1,0:T(8,128)(2,1)S(1)}, bf16[3,2,16,512]{3,2,1,0:T(8,128)(2,1)S(1)}, u32[]{:S(2)}, u32[]{:S(2)}) collective-permute-start(bf16[3,2,16,512]{3,2,1,0:T(8,128)(2,1)S(1)} %get-tuple-element.30), channel_id=1, source_target_pairs={{0,3},{1,2},{2,1},{3,0},{4,7},{5,6},{6,5},{7,4},{8,11},{9,10},{10,... | collective-permute-start | bytes 294920 | tf_op jit(solution)/shard_map/ppermute | solution.py:394
  39.0 27.6 %collective-permute-start.5 = (bf16[3,2,16,512]{3,2,1,0:T(8,128)(2,1)S(1)}, bf16[3,2,16,512]{3,2,1,0:T(8,128)(2,1)S(1)}, u32[]{:S(2)}, u32[]{:S(2)}) collective-permute-start(bf16[3,2,16,512]{3,2,1,0:T(8,128)(2,1)S(1)} %get-tuple-element.31), channel_id=1, source_target_pairs={{0,4},{1,5},{2,6},{3,7},{4,0},{5,1},{6,2},{7,3},{8,12},{9,13},{10,... | collective-permute-start | bytes 294920 | tf_op jit(solution)/shard_map/ppermute | solution.py:394
  41.9 27.6 %collective-permute-start.6 = (bf16[3,2,16,512]{3,2,1,0:T(8,128)(2,1)S(1)}, bf16[3,2,16,512]{3,2,1,0:T(8,128)(2,1)S(1)}, u32[]{:S(2)}, u32[]{:S(2)}) collective-permute-start(bf16[3,2,16,512]{3,2,1,0:T(8,128)(2,1)S(1)} %get-tuple-element.32), channel_id=1, source_target_pairs={{0,5},{1,4},{2,7},{3,6},{4,1},{5,0},{6,3},{7,2},{8,13},{9,12},{10,... | collective-permute-start | bytes 294920 | tf_op jit(solution)/shard_map/ppermute | solution.py:394
  43.4 26.1 %collective-permute-start.7 = (bf16[3,2,16,512]{3,2,1,0:T(8,128)(2,1)S(1)}, bf16[3,2,16,512]{3,2,1,0:T(8,128)(2,1)S(1)}, u32[]{:S(2)}, u32[]{:S(2)}) collective-permute-start(bf16[3,2,16,512]{3,2,1,0:T(8,128)(2,1)S(1)} %get-tuple-element.33), channel_id=1, source_target_pairs={{0,6},{1,7},{2,4},{3,5},{4,2},{5,3},{6,0},{7,1},{8,14},{9,15},{10,... | collective-permute-start | bytes 294920 | tf_op jit(solution)/shard_map/ppermute | solution.py:394
  51.8 17.8 %collective-permute-start.8 = (bf16[3,2,16,512]{3,2,1,0:T(8,128)(2,1)S(1)}, bf16[3,2,16,512]{3,2,1,0:T(8,128)(2,1)S(1)}, u32[]{:S(2)}, u32[]{:S(2)}) collective-permute-start(bf16[3,2,16,512]{3,2,1,0:T(8,128)(2,1)S(1)} %get-tuple-element.34), channel_id=1, source_target_pairs={{0,7},{1,6},{2,5},{3,4},{4,3},{5,2},{6,1},{7,0},{8,15},{9,14},{10,... | collective-permute-start | bytes 294920 | tf_op jit(solution)/shard_map/ppermute | solution.py:394
  69.6 20.6 %collective-permute-start.10 = (bf16[8,3,2,16,512]{4,3,2,1,0:T(8,128)(2,1)S(1)}, bf16[8,3,2,16,512]{4,3,2,1,0:T(8,128)(2,1)}, u32[]{:S(2)}, u32[]{:S(2)}) collective-permute-start(bf16[8,3,2,16,512]{4,3,2,1,0:T(8,128)(2,1)S(1)} %stacked_pieces.1.own), channel_id=1, source_target_pairs={{0,16},{8,24},{16,0},{24,8},{1,17},{9,25},{17,1},{25,9},{2,18},{10... | collective-permute-start | bytes 2359304 | tf_op jit(solution)/shard_map/ppermute | solution.py:394
  71.1 30.4 %collective-permute-start.15 = (bf16[8,3,2,16,512]{4,3,2,1,0:T(8,128)(2,1)S(1)}, bf16[8,3,2,16,512]{4,3,2,1,0:T(8,128)(2,1)S(1)}, u32[]{:S(2)}, u32[]{:S(2)}) collective-permute-start(bf16[8,3,2,16,512]{4,3,2,1,0:T(8,128)(2,1)S(1)} %all-to-all-done.1.own), channel_id=1, source_target_pairs={{0,16},{8,24},{16,0},{24,8},{1,17},{9,25},{17,1},{25,9},{2,18},{10... | collective-permute-start | bytes 2359304 | tf_op jit(solution)/shard_map/ppermute | solution.py:394
  71.7 29.8 %collective-permute-start.9 = (bf16[8,3,2,16,512]{4,3,2,1,0:T(8,128)(2,1)S(1)}, bf16[8,3,2,16,512]{4,3,2,1,0:T(8,128)(2,1)}, u32[]{:S(2)}, u32[]{:S(2)}) collective-permute-start(bf16[8,3,2,16,512]{4,3,2,1,0:T(8,128)(2,1)S(1)} %stacked_pieces.1.own), channel_id=1, source_target_pairs={{0,8},{8,0},{16,24},{24,16},{1,9},{9,1},{17,25},{25,17},{2,10},{10... | collective-permute-start | bytes 2359304 | tf_op jit(solution)/shard_map/ppermute | solution.py:394
  90.2 11.3 %collective-permute-start.11 = (bf16[8,3,2,16,512]{4,3,2,1,0:T(8,128)(2,1)}, bf16[8,3,2,16,512]{4,3,2,1,0:T(8,128)(2,1)}, u32[]{:S(2)}, u32[]{:S(2)}) collective-permute-start(bf16[8,3,2,16,512]{4,3,2,1,0:T(8,128)(2,1)} %collective-permute-done.10.rest_1_), channel_id=1, source_target_pairs={{0,8},{8,0},{16,24},{24,16},{1,9},{9,1},{17,25},{25,17},{2,10},{10... | collective-permute-start | bytes 2359304 | tf_op jit(solution)/shard_map/ppermute | solution.py:394
  90.2 19.2 %all-to-all-start = ((bf16[8,2,2,16,512]{4,3,2,1,0:T(8,128)(2,1)}), bf16[8,2,2,16,512]{4,3,2,1,0:T(8,128)(2,1)S(1)}, u32[]{:S(2)}, u32[]{:S(2)}) async-start(bf16[8,2,2,16,512]{4,3,2,1,0:T(8,128)(2,1)} %get-tuple-element.26), calls=%async_computation | async-start | bytes 1048576 | tf_op jit(solution)/shard_map/all_to_all | solution.py:442
  94.3 16.7 %collective-permute-start.14 = (bf16[8,3,2,16,512]{4,3,2,1,0:T(8,128)(2,1)S(1)}, bf16[8,3,2,16,512]{4,3,2,1,0:T(8,128)(2,1)}, u32[]{:S(2)}, u32[]{:S(2)}) collective-permute-start(bf16[8,3,2,16,512]{4,3,2,1,0:T(8,128)(2,1)S(1)} %all-to-all-done.1.own), channel_id=1, source_target_pairs={{0,8},{8,0},{16,24},{24,16},{1,9},{9,1},{17,25},{25,17},{2,10},{10... | collective-permute-start | bytes 2359304 | tf_op jit(solution)/shard_map/ppermute | solution.py:394
  101.5 9.6 %collective-permute-start.16 = (bf16[8,3,2,16,512]{4,3,2,1,0:T(8,128)(2,1)S(1)}, bf16[8,3,2,16,512]{4,3,2,1,0:T(8,128)(2,1)}, u32[]{:S(2)}, u32[]{:S(2)}) collective-permute-start(bf16[8,3,2,16,512]{4,3,2,1,0:T(8,128)(2,1)S(1)} %collective-permute-done.15.rest_1_), channel_id=1, source_target_pairs={{0,8},{8,0},{16,24},{24,16},{1,9},{9,1},{17,25},{25,17},{2,10},{10... | collective-permute-start | bytes 2359304 | tf_op jit(solution)/shard_map/ppermute | solution.py:394
  109.5 14.2 %collective-permute-start.13 = (bf16[8,2,2,16,512]{4,3,2,1,0:T(8,128)(2,1)S(1)}, bf16[8,2,2,16,512]{4,3,2,1,0:T(8,128)(2,1)S(1)}, u32[]{:S(2)}, u32[]{:S(2)}) collective-permute-start(bf16[8,2,2,16,512]{4,3,2,1,0:T(8,128)(2,1)S(1)} %after.2.own), channel_id=1, source_target_pairs={{0,16},{8,24},{16,0},{24,8},{1,17},{9,25},{17,1},{25,9},{2,18},{10... | collective-permute-start | bytes 1572872 | tf_op jit(solution)/shard_map/ppermute | solution.py:394
  111.0 12.8 %collective-permute-start.12 = (bf16[8,2,2,16,512]{4,3,2,1,0:T(8,128)(2,1)S(1)}, bf16[8,2,2,16,512]{4,3,2,1,0:T(8,128)(2,1)S(1)}, u32[]{:S(2)}, u32[]{:S(2)}) collective-permute-start(bf16[8,2,2,16,512]{4,3,2,1,0:T(8,128)(2,1)S(1)} %after.2.own), channel_id=1, source_target_pairs={{0,8},{8,0},{16,24},{24,16},{1,9},{9,1},{17,25},{25,17},{2,10},{10... | collective-permute-start | bytes 1572872 | tf_op jit(solution)/shard_map/ppermute | solution.py:394
  123.7 2.0 %collective-permute-start.17 = (bf16[8,2,2,16,512]{4,3,2,1,0:T(8,128)(2,1)S(1)}, bf16[8,2,2,16,512]{4,3,2,1,0:T(8,128)(2,1)S(1)}, u32[]{:S(2)}, u32[]{:S(2)}) collective-permute-start(bf16[8,2,2,16,512]{4,3,2,1,0:T(8,128)(2,1)S(1)} %after.3.rest_1_), channel_id=1, source_target_pairs={{0,8},{8,0},{16,24},{24,16},{1,9},{9,1},{17,25},{25,17},{2,10},{10... | collective-permute-start | bytes 1572872 | tf_op jit(solution)/shard_map/ppermute | solution.py:394

commit v3 on v1

v3 whole, which is shorter than its diff:
```python
import functools
import math

import jax
import jax.numpy as jnp
import numpy as np
from jax import lax
from jax.experimental import pallas as pl
from jax.experimental.pallas import tpu as pltpu
from jax.sharding import PartitionSpec as P

L = 2048
HOP = 512
JITTER = 256
TAPS = 65
BINS = 64
K0 = 64
RIM = 128
GROUP = L // HOP
EDGE = RIM + JITTER
LANES = 2 * BINS
MIB = 1 << 20
F32 = jnp.float32
BF16 = jnp.bfloat16


def from_behind(shard, axis, by):
    devices = lax.axis_size(axis)
    pairs = [(i, i + by) for i in range(devices) if 0 <= i + by < devices]
    return lax.ppermute(shard, axis, pairs)


def phase_table():
    sample = np.arange(L) - (TAPS - 1)
    angles = 2.0 * np.pi * np.mod(sample[:, None] * (K0 + np.arange(BINS))[None, :], L) / L
    return (np.concatenate([np.cos(angles), -np.sin(angles)], axis=1) / math.sqrt(L)).astype(np.float32)


def matmul(a, b):
    return jnp.dot(a, b, preferred_element_type=F32)


def turn(values, place):
    lane = lax.broadcasted_iota(jnp.int32, (8, LANES), 1)
    bins = K0 + (lane & (BINS - 1))
    angles = ((bins * (place + L)) & (L - 1)).astype(F32) * (2.0 * math.pi / L)
    sine = jnp.sin(angles)
    sine = jnp.where(lane < BINS, -sine, sine)
    return values * jnp.cos(angles)[:1] + pltpu.roll(values, BINS, 1) * sine[:1]


def edge_table(rise, fall, offset):
    start = JITTER - offset
    return jnp.concatenate([rise[pl.ds(start, RIM), :], fall[pl.ds(start, JITTER), :]], axis=0).astype(BF16)


def across(values):
    channels = values.shape[0]
    if channels % 128:
        values = jnp.pad(values, ((0, 128 - channels), (0, 0)))
    return values.T


def outbox_kernel(offsets, valid, record, out):
    top = record[0:8, :]
    row = lax.broadcasted_iota(jnp.int32, top.shape, 0)
    lane = lax.broadcasted_iota(jnp.int32, top.shape, 1)
    first = offsets.shape[0] - GROUP
    for q in range(GROUP):
        top = jnp.where((row == 0) & (lane == q), offsets[first + q].astype(F32), top)
        top = jnp.where((row == 0) & (lane == GROUP + q), valid[first + q].astype(F32), top)
    out[...] = jnp.concatenate([top, record[8:, :]], axis=0).astype(BF16)


def outbox(record, offsets, valid):
    channels, slab = record.shape
    smem = pl.BlockSpec(memory_space=pltpu.SMEM)
    return pl.pallas_call(
        outbox_kernel,
        grid=(1,),
        out_shape=jax.ShapeDtypeStruct((channels, RIM), BF16),
        in_specs=[smem, smem, pl.BlockSpec((channels, RIM), lambda i: (0, slab // RIM - 1))],
        out_specs=pl.BlockSpec(memory_space=pltpu.VMEM),
        compiler_params=pltpu.CompilerParams(vmem_limit_bytes=60 * MIB),
        name="outbox",
    )(offsets, valid, record)


def tables_kernel(taps, table, blocks, rise, fall, padded):
    padded[0 : TAPS - 1, :] = jnp.zeros((TAPS - 1, LANES), F32)
    padded[TAPS - 1 :, :] = table[TAPS - 1 : TAPS - 1 + padded.shape[0] - (TAPS - 1), :]
    ramp = jnp.zeros((TAPS - 1, LANES), F32)
    gain = jnp.zeros((1, LANES), F32)
    for m in range(TAPS):
        tap = taps[m]
        ramp = ramp + tap * padded[m : m + TAPS - 1, :]
        gain = gain + tap * padded[TAPS - 1 + m : TAPS + m, :]
    gain = jnp.broadcast_to(gain * math.sqrt(L), (8, LANES))
    lane = lax.broadcasted_iota(jnp.int32, (8, LANES), 1)
    swapped = pltpu.roll(gain, BINS, 1)
    gain_re = jnp.where(lane < BINS, gain, swapped)[:1]
    gain_im = jnp.where(lane < BINS, -swapped, gain)[:1]
    columns = table[...]
    pure = columns * gain_re + pltpu.roll(columns, BINS, 1) * gain_im
    blocks[...] = pure.astype(BF16)
    rise[...] = jnp.zeros_like(rise)
    rise[rise.shape[0] - (TAPS - 1) :, :] = -ramp
    ahead = JITTER - (TAPS - 1)
    fall[0:ahead, :] = pure[L - ahead :]
    fall[ahead:JITTER, :] = pure[: TAPS - 1] - ramp
    fall[JITTER:, :] = jnp.zeros((fall.shape[0] - JITTER, LANES), F32)


def tables(whitening):
    vmem = pl.BlockSpec(memory_space=pltpu.VMEM)
    return pl.pallas_call(
        tables_kernel,
        out_shape=(
            jax.ShapeDtypeStruct((L, LANES), BF16),
            jax.ShapeDtypeStruct((EDGE, LANES), F32),
            jax.ShapeDtypeStruct((2 * JITTER, LANES), F32),
        ),
        in_specs=[pl.BlockSpec(memory_space=pltpu.SMEM), vmem],
        out_specs=(vmem, vmem, vmem),
        scratch_shapes=[pltpu.VMEM((2 * TAPS + 6, LANES), F32)],
        compiler_params=pltpu.CompilerParams(vmem_limit_bytes=16 * MIB),
        name="tables",
    )(whitening, phase_table())


def border_kernel(inbox, record, blocks, rise, fall, done, parts, collected):
    channels = record.shape[0]
    head = inbox[0:16, :].astype(F32)[:1]
    lane = lax.broadcasted_iota(jnp.int32, (1, LANES), 1)

    def told(at):
        return jnp.sum(jnp.where(lane == at, head, 0.0)).astype(jnp.int32)

    before = jnp.zeros((channels, LANES), F32)
    for q in range(GROUP):
        offset = told(q)
        edges = edge_table(rise, fall, offset)
        if q == 0:
            part = matmul(record[:, 0:JITTER].astype(BF16), edges[RIM:])
        else:
            part = matmul(record[:, HOP * q - RIM : HOP * q + JITTER].astype(BF16), edges)
        place = HOP * q + offset - (TAPS - 1)
        part = (part + turn(before, place)) * told(GROUP + q).astype(F32)
        upright = across(part)
        for c in range(collected.shape[0]):
            piece = upright[:, 128 * c : 128 * c + 128]
            collected[c, pl.ds(q, BINS, stride=2 * GROUP), :] = piece[:BINS]
            collected[c, pl.ds(GROUP + q, BINS, stride=2 * GROUP), :] = piece[BINS:]
        if q < GROUP - 1:
            before = before + matmul(
                record[:, HOP * q : HOP * q + HOP].astype(BF16), blocks[HOP * q : HOP * q + HOP, :]
            )
    width = min(128, channels)
    for c in range(collected.shape[0]):
        block = collected[c].reshape(BINS, 2 * GROUP, 128).astype(BF16)
        parts[:, :, width * c : width * c + width] = block[:, :, :width]


def border_parts(record, inbox, blocks, rise, fall, done):
    channels = record.shape[0]
    vmem = pl.BlockSpec(memory_space=pltpu.VMEM)
    lead = L - HOP + JITTER
    return pl.pallas_call(
        border_kernel,
        grid=(1,),
        out_shape=jax.ShapeDtypeStruct((BINS, 2 * GROUP, channels), BF16),
        in_specs=[vmem, pl.BlockSpec((channels, lead), lambda i: (0, 0)), vmem, vmem, vmem, vmem],
        out_specs=vmem,
        scratch_shapes=[pltpu.VMEM((max(channels // 128, 1), 2 * GROUP * BINS, 128), F32)],
        compiler_params=pltpu.CompilerParams(vmem_limit_bytes=50 * MIB),
        cost_estimate=pl.CostEstimate(
            flops=2 * channels * LANES * 3072, bytes_accessed=4 * channels * lead, transcendentals=0
        ),
        name="border_parts",
    )(inbox, record, blocks, rise, fall, done)


def spectra_kernel(first, span, offsets, valid, record, rim, blocks, rise, fall, out, done, samples, later, collected, sems):
    channels, slab = record.shape
    windows = GROUP * span
    tail = L - HOP + JITTER
    end = RIM + L * span
    base = L * first
    if first == 0:
        fetches = [(base + L * s, RIM + L * s, L) for s in range(span)]
        samples[:, 0:RIM] = rim[...].astype(F32)
    else:
        fetches = [(base - RIM, 0, RIM + L)] + [(base + L * s, RIM + L * s, L) for s in range(1, span)]
    more = base + L * span < slab
    if more:
        fetches.append((base + L * span, end, tail))
    else:
        samples[:, end:] = jnp.zeros((channels, tail), F32)
    copies = [
        pltpu.make_async_copy(record.at[:, pl.ds(src, size)], samples.at[:, pl.ds(dst, size)], sems.at[i])
        for i, (src, dst, size) in enumerate(fetches)
    ]
    for copy in copies:
        copy.start()
    done[...] = jnp.zeros_like(done)

    def block_sums(s):
        return [
            matmul(
                samples[:, RIM + L * s + HOP * i : RIM + L * s + HOP * i + HOP].astype(BF16),
                blocks[HOP * i : HOP * i + HOP, :],
            )
            for i in range(GROUP if s < span else GROUP - 1)
        ]

    def keep(found):
        total = found[GROUP - 1]
        later[GROUP - 1] = total
        for q in range(GROUP - 2, -1, -1):
            total = total + found[q]
            later[q] = total

    copies[0].wait()
    keep(block_sums(0))
    for s in range(span):
        if s + 1 < len(copies):
            copies[s + 1].wait()
        found = block_sums(s + 1) if s + 1 < span or more else []
        before = None
        for q in range(GROUP):
            w = GROUP * s + q
            offset = offsets[GROUP * first + w]
            begin = HOP * w
            ends = samples[:, begin + L : begin + L + EDGE] - samples[:, begin : begin + EDGE]
            part = matmul(ends.astype(BF16), edge_table(rise, fall, offset))
            total = later[q] if before is None else later[q] + before
            part = (part + turn(total, HOP * q + offset - (TAPS - 1))) * valid[GROUP * first + w].astype(F32)
            upright = across(part)
            for c in range(collected.shape[0]):
                piece = upright[:, 128 * c : 128 * c + 128]
                collected[c, pl.ds(w, BINS, stride=2 * windows), :] = piece[:BINS]
                collected[c, pl.ds(windows + w, BINS, stride=2 * windows), :] = piece[BINS:]
            if found and q < GROUP - 1:
                before = found[q] if before is None else before + found[q]
        if s + 1 < span:
            keep(found)

    width = min(128, channels)
    for c in range(collected.shape[0]):
        block = collected[c].reshape(BINS, 2 * windows, 128).astype(BF16)
        out[:, :, width * c : width * c + width] = block[:, :, :width]


def own_spectra(record, rim, offsets, valid, transform, rise, fall, half):
    channels, slab = record.shape
    span = slab // L // 2
    windows = GROUP * span
    smem = pl.BlockSpec(memory_space=pltpu.SMEM)
    vmem = pl.BlockSpec(memory_space=pltpu.VMEM)
    return pl.pallas_call(
        functools.partial(spectra_kernel, span * half, span),
        out_shape=(
            jax.ShapeDtypeStruct((BINS, 2 * windows, channels), BF16),
            jax.ShapeDtypeStruct((8, 128), F32),
        ),
        in_specs=[smem, smem, pl.BlockSpec(memory_space=pl.ANY), vmem, vmem, vmem, vmem],
        out_specs=(vmem, vmem),
        scratch_shapes=[
            pltpu.VMEM((channels, RIM + L * span + L - HOP + JITTER), F32),
            pltpu.VMEM((GROUP, channels, LANES), F32),
            pltpu.VMEM((max(channels // 128, 1), LANES * windows, 128), F32),
            pltpu.SemaphoreType.DMA((span + 1,)),
        ],
        compiler_params=pltpu.CompilerParams(vmem_limit_bytes=50 * MIB),
        cost_estimate=pl.CostEstimate(
            flops=2 * channels * LANES * 896 * windows, bytes_accessed=2 * channels * slab, transcendentals=0
        ),
        name=f"own_spectra_{half}",
    )(offsets, valid, record, rim, transform, rise, fall)


def join_kernel(sizes, own, parts, *chunks):
    bins = sum(sizes)
    rows = own.shape[1] // 2
    for group in range(chunks[0].shape[0]):
        part = parts[group * bins : group * bins + bins].astype(F32)
        row = lax.broadcasted_iota(jnp.int32, part.shape, 1)
        moved = jnp.concatenate([part[:, GROUP:], part[:, :GROUP]], axis=1)
        spectra = own[group * bins : group * bins + bins].astype(F32)
        late = [jnp.where(row >= GROUP, extra, 0.0) for extra in (moved, part)]
        cut = rows - 2 * GROUP
        joined = jnp.concatenate(
            [piece for ri in range(2) for piece in (spectra[:, rows * ri : rows * ri + cut], spectra[:, rows * ri + cut : rows * ri + rows] + late[ri]) if piece.shape[1]],
            axis=1,
        ).astype(BF16)
        begin = 0
        for count, chunk in zip(sizes, chunks):
            chunk[group] = joined[begin : begin + count]
            begin += count


def chunk_sizes(bins):
    return [(bins + 1) // 2, bins // 2]


def joined_chunks(own, parts, devices):
    _, rows, channels = own.shape
    sizes = chunk_sizes(BINS // devices)
    vmem = pl.BlockSpec(memory_space=pltpu.VMEM)
    shapes = [(devices, count, rows, channels) for count in sizes]
    return pl.pallas_call(
        functools.partial(join_kernel, sizes),
        out_shape=tuple(jax.ShapeDtypeStruct(shape, BF16) for shape in shapes),
        in_specs=[vmem, vmem],
        out_specs=(vmem,) * len(shapes),
        compiler_params=pltpu.CompilerParams(vmem_limit_bytes=16 * MIB),
        name="joined_chunks",
    )(own, parts)


def cross_kernel(scale, stacked, me, *rest):
    out, done, left = rest[-3:]
    done[...] = jnp.zeros_like(done)
    early, late = rest[0], rest[1]
    sources, _, rows, channels = early.shape
    depth = sources * rows
    half = rows // 2
    for i, own in enumerate((early, late)):
        straight = own[:, 0].astype(F32)
        turned = jnp.concatenate([straight[:, half:], -straight[:, :half]], axis=1)
        for j, side in enumerate((straight, turned)):
            left[channels * j : channels * j + channels, depth * i : depth * i + depth] = side.reshape(depth, channels).T.astype(BF16)
    blocks = rest[2].shape[0] if stacked else (len(rest) - 4) // 2
    tile = min(256, channels)
    for n in range(blocks):
        if stacked:
            pair = [rest[2][n], rest[3][n]]
            at = channels * n
        else:
            pair = [rest[2 * n][...], rest[2 * n + 1][...]]
            at = pl.multiple_of(channels * (me[0] ^ n), 128)
        right = jnp.concatenate([one[:, 0].reshape(depth, channels) for one in pair], axis=0)
        for j in range(0, channels, tile):
            for r in range(0, 2 * channels, tile):
                both = matmul(left[r : r + tile, :], right[:, j : j + tile]) * scale
                out[0, r // channels, r % channels : r % channels + tile, pl.ds(at + j, tile)] = both.astype(BF16)


def cross_products(early, late, result, begin, bins):
    sources, count, rows, channels = late[0].shape
    stacked = not isinstance(late[1], list)
    blocks = late[1].shape[0] if stacked else len(late[1]) + 1
    shape = (bins, 2, channels, blocks * channels)
    specs = [
        pl.BlockSpec((sources, 1, rows, channels), lambda f: (0, begin + f, 0, 0)),
        pl.BlockSpec((sources, 1, rows, channels), lambda f: (0, f, 0, 0)),
    ]
    operands = [lax.axis_index("chan").astype(jnp.int32).reshape(1), early[0], late[0]]
    in_specs = [pl.BlockSpec(memory_space=pltpu.SMEM)] + specs
    if stacked:
        operands += [early[1], late[1]]
        in_specs += [
            pl.BlockSpec((blocks, sources, 1, rows, channels), lambda f: (0, 0, begin + f, 0, 0)),
            pl.BlockSpec((blocks, sources, 1, rows, channels), lambda f: (0, 0, f, 0, 0)),
        ]
    else:
        for pair in zip(early[1], late[1]):
            operands += pair
            in_specs += specs
    if result is None:
        result, aliases = operands[0], {}
    else:
        aliases = {len(operands): 0}
    operands.append(result)
    in_specs.append(pl.BlockSpec(memory_space=pl.ANY))
    depth = 2 * sources * rows
    return pl.pallas_call(
        functools.partial(cross_kernel, 2.0 / depth, stacked),
        grid=(count,),
        out_shape=(jax.ShapeDtypeStruct(shape, BF16), jax.ShapeDtypeStruct((8, 128), F32)),
        in_specs=in_specs,
        out_specs=(
            pl.BlockSpec((1,) + shape[1:], lambda f: (begin + f, 0, 0, 0)),
            pl.BlockSpec(memory_space=pltpu.VMEM),
        ),
        scratch_shapes=[pltpu.VMEM((2 * channels, depth), BF16)],
        input_output_aliases=aliases,
        compiler_params=pltpu.CompilerParams(vmem_limit_bytes=36 * MIB),
        cost_estimate=pl.CostEstimate(
            flops=4 * count * channels * blocks * channels * depth,
            bytes_accessed=4 * count * channels * blocks * channels,
            transcendentals=0,
        ),
        name="cross_products",
    )(*operands)


def swapped(shard, axis, bit):
    devices = lax.axis_size(axis)
    return lax.ppermute(shard, axis, [(i, i ^ bit) for i in range(devices)])


def fan(shard, axis, bit):
    held = {0: shard}
    while bit:
        held.update({n | bit: swapped(block, axis, bit) for n, block in list(held.items())})
        bit //= 2
    return held


def after_kernel(shard, done, out):
    out[...] = shard[...]


def after(shard, done):
    if done is None:
        return shard
    vmem = pl.BlockSpec(memory_space=pltpu.VMEM)
    return pl.pallas_call(
        after_kernel,
        out_shape=jax.ShapeDtypeStruct(shard.shape, shard.dtype),
        in_specs=[vmem, vmem],
        out_specs=vmem,
        compiler_params=pltpu.CompilerParams(vmem_limit_bytes=8 * MIB),
        name="after",
    )(shard, done)


def per_device(record, whitening, offsets, window_valid):
    devices = lax.axis_size("tm")
    blocks = lax.axis_size("chan")
    stacked = blocks & (blocks - 1) != 0 or record.shape[0] % 128 != 0
    top = blocks // 2
    bins = BINS // devices

    def exchanged(chunk):
        return lax.all_to_all(chunk, "tm", split_axis=0, concat_axis=0, tiled=True)

    def spread(mine, ready, done):
        if stacked:
            return mine, lax.all_gather(mine, "chan", axis=0, tiled=False)
        near = fan(mine, "chan", top // 2)
        far = after(swapped(mine, "chan", top), ready if done is None else done)
        found = near | {n | top: block for n, block in fan(far, "chan", top // 2).items()}
        return mine, [found[n] for n in range(1, blocks)]

    inbox = from_behind(outbox(record, offsets, window_valid), "tm", 1)
    transform, rise, fall = tables(whitening)
    early, done = own_spectra(record, inbox, offsets, window_valid, transform, rise, fall, 0)
    parts = from_behind(border_parts(record, inbox, transform, rise, fall, done), "tm", -1)
    late, _ = own_spectra(record, inbox, offsets, window_valid, transform, rise, fall, 1)
    sizes = chunk_sizes(bins)
    early = exchanged(early.reshape((devices, bins) + early.shape[1:]))
    late = [exchanged(chunk) for chunk in joined_chunks(late, parts, devices)]
    early = spread(early, late[0], None)
    result, done, begin = None, None, 0
    for p, mine in enumerate(late):
        result, done = cross_products(early, spread(mine, None, done), result, begin, bins)
        begin += sizes[p]
    return result


def solution(mesh):
    in_specs = (P("chan", "tm"), P(), P("tm"), P("tm"))
    out_specs = P("tm", None, "chan", None)
    return jax.shard_map(
        per_device, mesh=mesh, in_specs=in_specs, out_specs=out_specs, check_vma=False
    )
```

time: 123 us -> 124 us (level)
  waiting for transfers between devices: 32.5 us -> 41.3 us
  blocking collectives: 24.1 us -> 15.9 us
  local copies, waits for them, and re-layouts: 9.05 us -> 3.2 us
  Pallas kernels: 38.5 us -> 41.8 us
  starting transfers between devices: 17.9 us -> 20.8 us
    all_to_all x2, waiting for transfers between devices: 2.34 us -> 30.9 us  [exchanged(): return lax.all_to_all(chunk, 'tm', split_axis=0, concat_axis=0, tiled=True)]
    ppermute x9, waiting for transfers between devices: 26.4 us -> 10.2 us  [swapped(): return lax.ppermute(shard, axis, [(i, i ^ bit) for i in range(devices)])]
    all_to_all x1, blocking collectives: 24.1 us -> 15.9 us  [exchanged(): return lax.all_to_all(chunk, 'tm', split_axis=0, concat_axis=0, tiled=True)]
    unnamed x28 -> x14, local copies, waits for them, and re-layouts: 9.05 us -> 3.2 us
    ppermute x2, waiting for transfers between devices: 3.73 us -> 0.19 us  [from_behind(): return lax.ppermute(shard, axis, pairs)]
    all_to_all x2, starting transfers between devices: 8.18 us -> 10.4 us  [exchanged(): return lax.all_to_all(chunk, 'tm', split_axis=0, concat_axis=0, tiled=True)]
    pallas_call x5, Pallas kernels: 33.2 us -> 34.7 us  [the longest x2 19.5 us: cross_products(): pl.pallas_call(functools.partial(cross_kernel, 2.0 / depth, stacked), gri...]
  transfers between devices with their start and end apart: 13 -> 13, of which waited for: 7 -> 6; matrix products, arithmetic and copies ran while one was open for 0% -> 0% of each run, Pallas kernels for 22% -> 18%
where the time goes in v3:
time: 124 us; the launch traced here: 123 us
  Pallas kernels  41.8 us (34%)
  waiting for transfers between devices  41.3 us (33%)
  starting transfers between devices  20.8 us (17%)
  blocking collectives  15.9 us (13%)
  local copies, waits for them, and re-layouts  3.2 us (3%)
    all_to_all x2, waiting for transfers between devices, exchanged(): return lax.all_to_all(chunk, 'tm', split_axis=0, concat_axis=0, tiled=True)  30.9 us
    pallas_call x2, Pallas kernels, cross_products(): pl.pallas_call(functools.partial(cross_kernel, 2.0 / depth, stacked), gri...  19.5 us
    all_to_all x1, blocking collectives, exchanged(): return lax.all_to_all(chunk, 'tm', split_axis=0, concat_axis=0, tiled=True)  15.9 us
    pallas_call x2, Pallas kernels, own_spectra(): pl.pallas_call(functools.partial(spectra_kernel, span * half, span), out_...  14.9 us
    all_to_all x2, starting transfers between devices, exchanged(): return lax.all_to_all(chunk, 'tm', split_axis=0, concat_axis=0, tiled=True)  10.4 us
    ppermute x9, waiting for transfers between devices, swapped(): return lax.ppermute(shard, axis, [(i, i ^ bit) for i in range(devices)])  10.2 us
    ppermute x2, starting transfers between devices, from_behind(): return lax.ppermute(shard, axis, pairs)  6.16 us
    ppermute x9, starting transfers between devices, swapped(): return lax.ppermute(shard, axis, [(i, i ^ bit) for i in range(devices)])  4.26 us
  transfers between devices with their start and end apart: 13, of which 6 were waited for; matrix products, arithmetic and copies ran while one was open for 0% of the time, Pallas kernels for 18%

profile of v3, /device:TPU:0, one launch (start us, length us, event | category | flops | bytes accessed | tf_op | source)
XLA Modules:
  0.0 123.1 jit_solution(14159281258792455780)
XLA Ops:
  0.0 1.7 %outbox.1 = bf16[512,128]{1,0:T(8,128)(2,1)} custom-call(s32[16]{0:T(128)} %offsets.5, s32[16]{0:T(128)} %valid.5, f32[512,8192]{1,0:T(8,128)} %record.7), custom_call_target="tpu_custom_call" | custom-call | tf_op jit(solution)/shard_map/outbox/pallas_call | solution.py:78
  1.7 4.9 %collective-permute-start = (bf16[512,128]{1,0:T(8,128)(2,1)}, bf16[512,128]{1,0:T(8,128)(2,1)S(1)}, u32[]{:S(2)}, u32[]{:S(2)}) collective-permute-start(bf16[512,128]{1,0:T(8,128)(2,1)} %outbox.1), channel_id=1, source_target_pairs={{0,1},{1,2},{2,3},{3,4},{4,5},{5,6},{6,7},{8,9},{9,10},{10,11},{11... | collective-permute-start | bytes 393224 | tf_op jit(solution)/shard_map/ppermute | solution.py:30
  6.5 1.2 copy-done
  7.8 0.7 copy-done.6
  8.4 1.0 tables.1
  9.6 0.7 copy-done.2
  10.2 0.7 copy-done.4
  10.9 8.0 %own_spectra_0.1 = (bf16[64,16,512]{2,1,0:T(8,128)(2,1)}, f32[8,128]{1,0:T(8,128)S(1)}) custom-call(s32[16]{0:T(128)S(1)} %copy-done.2, s32[16]{0:T(128)S(1)} %copy-done.4, f32[512,8192]{1,0:T(8,128)} %record.7, bf16[512,128]{1,0:T(8,128)(2,1)S(1)} %collective-permute-done.rim.inbox, bf16[2048,128]{1,0:T(8,128)(2,1)S(1)} %get-tuple-element.16.blocks, ...), custom_call_target="tpu_custom_call" | custom-call | flops 939524096 | bytes 8388608 | tf_op jit(solution)/shard_map/own_spectra_0/pallas_call | solution.py:260
  18.9 6.7 %all-to-all-start = ((bf16[8,8,16,512]{3,2,1,0:T(8,128)(2,1)}), bf16[8,8,16,512]{3,2,1,0:T(8,128)(2,1)S(1)}, u32[]{:S(2)}, u32[]{:S(2)}) async-start(bf16[8,8,16,512]{3,2,1,0:T(8,128)(2,1)} %bitcast.1), calls=%async_computation | async-start | bytes 2097152 | tf_op jit(solution)/shard_map/all_to_all | solution.py:437
  25.6 3.3 %border_parts.1 = bf16[64,8,512]{2,1,0:T(8,128)(2,1)S(1)} custom-call(bf16[512,128]{1,0:T(8,128)(2,1)S(1)} %collective-permute-done.rim.inbox, f32[512,8192]{1,0:T(8,128)} %record.7, bf16[2048,128]{1,0:T(8,128)(2,1)S(1)} %get-tuple-element.16.blocks, f32[384,128]{1,0:T(8,128)S(1)} %get-tuple-element.17.rise, f32[512,128]{1,0:T(8,128)S(1)} %get-tuple-element.18.fall, ...), custom_call_target="tpu_custom_call" | custom-call | flops 402653184 | bytes 3670016 | tf_op jit(solution)/shard_map/border_parts/pallas_call | solution.py:168
  29.0 1.3 %collective-permute-start.1 = (bf16[64,8,512]{2,1,0:T(8,128)(2,1)S(1)}, bf16[64,8,512]{2,1,0:T(8,128)(2,1)S(1)}, u32[]{:S(2)}, u32[]{:S(2)}) collective-permute-start(bf16[64,8,512]{2,1,0:T(8,128)(2,1)S(1)} %border_parts.1), channel_id=1, source_target_pairs={{1,0},{2,1},{3,2},{4,3},{5,4},{6,5},{7,6},{9,8},{10,9},{11,10},{12... | collective-permute-start | bytes 1572872 | tf_op jit(solution)/shard_map/ppermute | solution.py:30
  30.3 22.6 %all-to-all-done.rest_0_ = bf16[8,8,16,512]{3,2,1,0:T(8,128)(2,1)S(1)} async-done(((bf16[8,8,16,512]{3,2,1,0:T(8,128)(2,1)}), bf16[8,8,16,512]{3,2,1,0:T(8,128)(2,1)S(1)}, u32[]{:S(2)}, u32[]{:S(2)}) %all-to-all-start) | async-done | bytes 1048608 | tf_op jit(solution)/shard_map/all_to_all | solution.py:437
  52.8 1.5 %collective-permute-start.4 = (bf16[8,8,16,512]{3,2,1,0:T(8,128)(2,1)S(1)}, bf16[8,8,16,512]{3,2,1,0:T(8,128)(2,1)S(1)}, u32[]{:S(2)}, u32[]{:S(2)}) collective-permute-start(bf16[8,8,16,512]{3,2,1,0:T(8,128)(2,1)S(1)} %all-to-all-done.rest_0_), channel_id=1, source_target_pairs={{0,16},{8,24},{16,0},{24,8},{1,17},{9,25},{17,1},{25,9},{2,18},{10... | collective-permute-start | bytes 3145736 | tf_op jit(solution)/shard_map/ppermute | solution.py:400
  54.3 6.9 %own_spectra_1.1 = (bf16[64,16,512]{2,1,0:T(8,128)(2,1)S(1)}, f32[8,128]{1,0:T(8,128)}) custom-call(s32[16]{0:T(128)S(1)} %copy-done.3, s32[16]{0:T(128)S(1)} %copy-done.5, f32[512,8192]{1,0:T(8,128)} %record.7, bf16[512,128]{1,0:T(8,128)(2,1)S(1)} %collective-permute-done.rim.inbox, bf16[2048,128]{1,0:T(8,128)(2,1)S(1)} %get-tuple-element.16.blocks, ...), custom_call_target="tpu_custom_call" | custom-call | flops 939524096 | bytes 8388608 | tf_op jit(solution)/shard_map/own_spectra_1/pallas_call | solution.py:260
  61.6 15.9 %all_to_all.15.done.rest_1_ = bf16[8,4,16,512]{3,2,1,0:T(8,128)(2,1)S(1)} all-to-all(bf16[8,4,16,512]{3,2,1,0:T(8,128)(2,1)S(1)} %get-tuple-element.23), channel_id=1, replica_groups=mesh['chan'=4,'tm'=8] {'tm'}, dimensions={0} | all-to-all | bytes 1048576 | tf_op jit(solution)/shard_map/all_to_all | solution.py:437
  77.5 1.5 %collective-permute-start.7 = (bf16[8,4,16,512]{3,2,1,0:T(8,128)(2,1)S(1)}, bf16[8,4,16,512]{3,2,1,0:T(8,128)(2,1)}, u32[]{:S(2)}, u32[]{:S(2)}) collective-permute-start(bf16[8,4,16,512]{3,2,1,0:T(8,128)(2,1)S(1)} %all_to_all.15.done.rest_1_), channel_id=1, source_target_pairs={{0,16},{8,24},{16,0},{24,8},{1,17},{9,25},{17,1},{25,9},{2,18},{10... | collective-permute-start | bytes 1572872 | tf_op jit(solution)/shard_map/ppermute | solution.py:400
  79.6 3.7 %all-to-all-start.1 = ((bf16[8,4,16,512]{3,2,1,0:T(8,128)(2,1)}), bf16[8,4,16,512]{3,2,1,0:T(8,128)(2,1)S(1)}, u32[]{:S(2)}, u32[]{:S(2)}) async-start(bf16[8,4,16,512]{3,2,1,0:T(8,128)(2,1)} %copy-done.1), calls=%async_computation.1 | async-start | bytes 1048576 | tf_op jit(solution)/shard_map/all_to_all | solution.py:437
  83.4 6.2 %collective-permute-done.7.rest_5_ = bf16[8,4,16,512]{3,2,1,0:T(8,128)(2,1)} collective-permute-done((bf16[8,4,16,512]{3,2,1,0:T(8,128)(2,1)S(1)}, bf16[8,4,16,512]{3,2,1,0:T(8,128)(2,1)}, u32[]{:S(2)}, u32[]{:S(2)}) %collective-permute-start.7) | collective-permute-done | bytes 524320 | tf_op jit(solution)/shard_map/ppermute | solution.py:400
  89.6 8.4 %all-to-all-done.1.rest_1_ = bf16[8,4,16,512]{3,2,1,0:T(8,128)(2,1)S(1)} async-done(((bf16[8,4,16,512]{3,2,1,0:T(8,128)(2,1)}), bf16[8,4,16,512]{3,2,1,0:T(8,128)(2,1)S(1)}, u32[]{:S(2)}, u32[]{:S(2)}) %all-to-all-start.1) | async-done | bytes 524320 | tf_op jit(solution)/shard_map/all_to_all | solution.py:437
  98.6 10.0 %cross_products.2 = (bf16[8,2,512,2048]{3,2,1,0:T(8,128)(2,1)}, f32[8,128]{1,0:T(8,128)S(1)}) custom-call(s32[1]{0:T(128)} %bitcast.me.rest_8_, bf16[8,8,16,512]{3,2,1,0:T(8,128)(2,1)S(1)} %all-to-all-done.rest_0_, bf16[8,4,16,512]{3,2,1,0:T(8,128)(2,1)S(1)} %all_to_all.15.done.rest_1_, bf16[8,8,16,512]{3,2,1,0:T(8,128)(2,1)} %collective-permute-done.2.rest_2_, ...), custom_call_target="tpu_custom_call" | custom-call | flops 4294967296 | bytes 16777216 | tf_op jit(solution)/shard_map/cross_products/pallas_call | solution.py:377
  108.6 2.0 %collective-permute-done.5.shard = bf16[8,4,16,512]{3,2,1,0:T(8,128)(2,1)} collective-permute-done((bf16[8,4,16,512]{3,2,1,0:T(8,128)(2,1)S(1)}, bf16[8,4,16,512]{3,2,1,0:T(8,128)(2,1)}, u32[]{:S(2)}, u32[]{:S(2)}) %collective-permute-start.5) | collective-permute-done | bytes 524320 | tf_op jit(solution)/shard_map/ppermute | solution.py:400
  110.6 1.1 after.3.rest_5_
  111.8 1.9 %collective-permute-done.10.rest_7_ = bf16[8,4,16,512]{3,2,1,0:T(8,128)(2,1)S(1)} collective-permute-done((bf16[8,4,16,512]{3,2,1,0:T(8,128)(2,1)S(1)}, bf16[8,4,16,512]{3,2,1,0:T(8,128)(2,1)S(1)}, u32[]{:S(2)}, u32[]{:S(2)}) %collective-permute-start.10) | collective-permute-done | bytes 524320 | tf_op jit(solution)/shard_map/ppermute | solution.py:400
  113.7 9.5 %cross_products.3 = (bf16[8,2,512,2048]{3,2,1,0:T(8,128)(2,1)}, f32[8,128]{1,0:T(8,128)}) custom-call(s32[1]{0:T(128)} %bitcast.me.rest_8_, bf16[8,8,16,512]{3,2,1,0:T(8,128)(2,1)S(1)} %all-to-all-done.rest_0_, bf16[8,4,16,512]{3,2,1,0:T(8,128)(2,1)S(1)} %all-to-all-done.1.rest_1_, ...), custom_call_target="tpu_custom_call", output_to_operand_aliasing={{0}: (9, {})} | custom-call | flops 4294967296 | bytes 16777216 | tf_op jit(solution)/shard_map/cross_products/pallas_call | solution.py:377
  (27 shorter events, 1.9 us)
Async XLA Ops:
  0.0 54.3 %copy-start.5 = (s32[16]{0:T(128)S(1)}, s32[16]{0:T(128)}, u32[]{:S(2)}) copy-start(s32[16]{0:T(128)} %valid.5) | copy-start | bytes 196
  0.0 54.3 %copy-start.3 = (s32[16]{0:T(128)S(1)}, s32[16]{0:T(128)}, u32[]{:S(2)}) copy-start(s32[16]{0:T(128)} %offsets.5) | copy-start | bytes 196
  1.7 7.9 %collective-permute-start = (bf16[512,128]{1,0:T(8,128)(2,1)}, bf16[512,128]{1,0:T(8,128)(2,1)S(1)}, u32[]{:S(2)}, u32[]{:S(2)}) collective-permute-start(bf16[512,128]{1,0:T(8,128)(2,1)} %outbox.1), channel_id=1, source_target_pairs={{0,1},{1,2},{2,3},{3,4},{4,5},{5,6},{6,7},{8,9},{9,10},{10,11},{11... | collective-permute-start | bytes 393224 | tf_op jit(solution)/shard_map/ppermute | solution.py:30
  6.5 1.2 copy-start
  7.8 0.7 copy-start.6
  9.6 0.7 copy-start.2
  10.2 0.7 copy-start.4
  18.9 33.9 %all-to-all-start = ((bf16[8,8,16,512]{3,2,1,0:T(8,128)(2,1)}), bf16[8,8,16,512]{3,2,1,0:T(8,128)(2,1)S(1)}, u32[]{:S(2)}, u32[]{:S(2)}) async-start(bf16[8,8,16,512]{3,2,1,0:T(8,128)(2,1)} %bitcast.1), calls=%async_computation | async-start | bytes 2097152 | tf_op jit(solution)/shard_map/all_to_all | solution.py:437
  29.0 32.3 %collective-permute-start.1 = (bf16[64,8,512]{2,1,0:T(8,128)(2,1)S(1)}, bf16[64,8,512]{2,1,0:T(8,128)(2,1)S(1)}, u32[]{:S(2)}, u32[]{:S(2)}) collective-permute-start(bf16[64,8,512]{2,1,0:T(8,128)(2,1)S(1)} %border_parts.1), channel_id=1, source_target_pairs={{1,0},{2,1},{3,2},{4,3},{5,4},{6,5},{7,6},{9,8},{10,9},{11,10},{12... | collective-permute-start | bytes 1572872 | tf_op jit(solution)/shard_map/ppermute | solution.py:30
  52.8 26.2 %collective-permute-start.4 = (bf16[8,8,16,512]{3,2,1,0:T(8,128)(2,1)S(1)}, bf16[8,8,16,512]{3,2,1,0:T(8,128)(2,1)S(1)}, u32[]{:S(2)}, u32[]{:S(2)}) collective-permute-start(bf16[8,8,16,512]{3,2,1,0:T(8,128)(2,1)S(1)} %all-to-all-done.rest_0_), channel_id=1, source_target_pairs={{0,16},{8,24},{16,0},{24,8},{1,17},{9,25},{17,1},{25,9},{2,18},{10... | collective-permute-start | bytes 3145736 | tf_op jit(solution)/shard_map/ppermute | solution.py:400
  61.6 18.1 %copy-start.1 = (bf16[8,4,16,512]{3,2,1,0:T(8,128)(2,1)}, bf16[8,4,16,512]{3,2,1,0:T(8,128)(2,1)S(1)}, u32[]{:S(2)}) copy-start(bf16[8,4,16,512]{3,2,1,0:T(8,128)(2,1)S(1)} %get-tuple-element.22) | copy-start | bytes 1572868
  77.5 12.2 %collective-permute-start.7 = (bf16[8,4,16,512]{3,2,1,0:T(8,128)(2,1)S(1)}, bf16[8,4,16,512]{3,2,1,0:T(8,128)(2,1)}, u32[]{:S(2)}, u32[]{:S(2)}) collective-permute-start(bf16[8,4,16,512]{3,2,1,0:T(8,128)(2,1)S(1)} %all_to_all.15.done.rest_1_), channel_id=1, source_target_pairs={{0,16},{8,24},{16,0},{24,8},{1,17},{9,25},{17,1},{25,9},{2,18},{10... | collective-permute-start | bytes 1572872 | tf_op jit(solution)/shard_map/ppermute | solution.py:400
  79.0 19.6 %collective-permute-start.2 = (bf16[8,8,16,512]{3,2,1,0:T(8,128)(2,1)S(1)}, bf16[8,8,16,512]{3,2,1,0:T(8,128)(2,1)}, u32[]{:S(2)}, u32[]{:S(2)}) collective-permute-start(bf16[8,8,16,512]{3,2,1,0:T(8,128)(2,1)S(1)} %all-to-all-done.rest_0_), channel_id=1, source_target_pairs={{0,8},{8,0},{16,24},{24,16},{1,9},{9,1},{17,25},{25,17},{2,10},{10... | collective-permute-start | bytes 3145736 | tf_op jit(solution)/shard_map/ppermute | solution.py:400
  79.1 19.5 %collective-permute-start.8 = (bf16[8,8,16,512]{3,2,1,0:T(8,128)(2,1)S(1)}, bf16[8,8,16,512]{3,2,1,0:T(8,128)(2,1)}, u32[]{:S(2)}, u32[]{:S(2)}) collective-permute-start(bf16[8,8,16,512]{3,2,1,0:T(8,128)(2,1)S(1)} %after.2.rest_4_), channel_id=1, source_target_pairs={{0,8},{8,0},{16,24},{24,16},{1,9},{9,1},{17,25},{25,17},{2,10},{10... | collective-permute-start | bytes 3145736 | tf_op jit(solution)/shard_map/ppermute | solution.py:400
  79.6 18.4 %all-to-all-start.1 = ((bf16[8,4,16,512]{3,2,1,0:T(8,128)(2,1)}), bf16[8,4,16,512]{3,2,1,0:T(8,128)(2,1)S(1)}, u32[]{:S(2)}, u32[]{:S(2)}) async-start(bf16[8,4,16,512]{3,2,1,0:T(8,128)(2,1)} %copy-done.1), calls=%async_computation.1 | async-start | bytes 1048576 | tf_op jit(solution)/shard_map/all_to_all | solution.py:437
  83.3 15.2 %collective-permute-start.6 = (bf16[8,4,16,512]{3,2,1,0:T(8,128)(2,1)S(1)}, bf16[8,4,16,512]{3,2,1,0:T(8,128)(2,1)}, u32[]{:S(2)}, u32[]{:S(2)}) collective-permute-start(bf16[8,4,16,512]{3,2,1,0:T(8,128)(2,1)S(1)} %all_to_all.15.done.rest_1_), channel_id=1, source_target_pairs={{0,8},{8,0},{16,24},{24,16},{1,9},{9,1},{17,25},{25,17},{2,10},{10... | collective-permute-start | bytes 1572872 | tf_op jit(solution)/shard_map/ppermute | solution.py:400
  89.6 8.9 %collective-permute-start.9 = (bf16[8,4,16,512]{3,2,1,0:T(8,128)(2,1)}, bf16[8,4,16,512]{3,2,1,0:T(8,128)(2,1)}, u32[]{:S(2)}, u32[]{:S(2)}) collective-permute-start(bf16[8,4,16,512]{3,2,1,0:T(8,128)(2,1)} %collective-permute-done.7.rest_5_), channel_id=1, source_target_pairs={{0,8},{8,0},{16,24},{24,16},{1,9},{9,1},{17,25},{25,17},{2,10},{10... | collective-permute-start | bytes 1572872 | tf_op jit(solution)/shard_map/ppermute | solution.py:400
  98.0 12.6 %collective-permute-start.5 = (bf16[8,4,16,512]{3,2,1,0:T(8,128)(2,1)S(1)}, bf16[8,4,16,512]{3,2,1,0:T(8,128)(2,1)}, u32[]{:S(2)}, u32[]{:S(2)}) collective-permute-start(bf16[8,4,16,512]{3,2,1,0:T(8,128)(2,1)S(1)} %all-to-all-done.1.rest_1_), channel_id=1, source_target_pairs={{0,16},{8,24},{16,0},{24,8},{1,17},{9,25},{17,1},{25,9},{2,18},{10... | collective-permute-start | bytes 1572872 | tf_op jit(solution)/shard_map/ppermute | solution.py:400
  98.6 13.2 %collective-permute-start.3 = (bf16[8,4,16,512]{3,2,1,0:T(8,128)(2,1)S(1)}, bf16[8,4,16,512]{3,2,1,0:T(8,128)(2,1)S(1)}, u32[]{:S(2)}, u32[]{:S(2)}) collective-permute-start(bf16[8,4,16,512]{3,2,1,0:T(8,128)(2,1)S(1)} %all-to-all-done.1.rest_1_), channel_id=1, source_target_pairs={{0,8},{8,0},{16,24},{24,16},{1,9},{9,1},{17,25},{25,17},{2,10},{10... | collective-permute-start | bytes 1572872 | tf_op jit(solution)/shard_map/ppermute | solution.py:400
  111.7 2.0 %collective-permute-start.10 = (bf16[8,4,16,512]{3,2,1,0:T(8,128)(2,1)S(1)}, bf16[8,4,16,512]{3,2,1,0:T(8,128)(2,1)S(1)}, u32[]{:S(2)}, u32[]{:S(2)}) collective-permute-start(bf16[8,4,16,512]{3,2,1,0:T(8,128)(2,1)S(1)} %after.3.rest_5_), channel_id=1, source_target_pairs={{0,8},{8,0},{16,24},{24,16},{1,9},{9,1},{17,25},{25,17},{2,10},{10... | collective-permute-start | bytes 1572872 | tf_op jit(solution)/shard_map/ppermute | solution.py:400

commit v4 on v3

--- a/solution.py
+++ b/solution.py
@@ -128,8 +128,9 @@
     )(whitening, phase_table())
 
 
-def border_kernel(inbox, record, blocks, rise, fall, done, parts, collected):
+def border_kernel(inbox, record, blocks, rise, fall, parts, done, collected):
     channels = record.shape[0]
+    done[...] = jnp.zeros_like(done)
     head = inbox[0:16, :].astype(F32)[:1]
     lane = lax.broadcasted_iota(jnp.int32, (1, LANES), 1)
 
@@ -161,39 +162,41 @@
         parts[:, :, width * c : width * c + width] = block[:, :, :width]
 
 
-def border_parts(record, inbox, blocks, rise, fall, done):
+def border_parts(record, inbox, blocks, rise, fall):
     channels = record.shape[0]
     vmem = pl.BlockSpec(memory_space=pltpu.VMEM)
     lead = L - HOP + JITTER
     return pl.pallas_call(
         border_kernel,
         grid=(1,),
-        out_shape=jax.ShapeDtypeStruct((BINS, 2 * GROUP, channels), BF16),
-        in_specs=[vmem, pl.BlockSpec((channels, lead), lambda i: (0, 0)), vmem, vmem, vmem, vmem],
-        out_specs=vmem,
+        out_shape=(jax.ShapeDtypeStruct((BINS, 2 * GROUP, channels), BF16), jax.ShapeDtypeStruct((8, 128), F32)),
+        in_specs=[vmem, pl.BlockSpec((channels, lead), lambda i: (0, 0)), vmem, vmem, vmem],
+        out_specs=(vmem, vmem),
         scratch_shapes=[pltpu.VMEM((max(channels // 128, 1), 2 * GROUP * BINS, 128), F32)],
         compiler_params=pltpu.CompilerParams(vmem_limit_bytes=50 * MIB),
         cost_estimate=pl.CostEstimate(
             flops=2 * channels * LANES * 3072, bytes_accessed=4 * channels * lead, transcendentals=0
         ),
         name="border_parts",
-    )(inbox, record, blocks, rise, fall, done)
-
-
-def spectra_kernel(first, span, offsets, valid, record, rim, blocks, rise, fall, out, done, samples, later, collected, sems):
+    )(inbox, record, blocks, rise, fall)
+
+
+def spectra_kernel(first, span, offsets, valid, record, rim, blocks, rise, fall, done, out, samples, later, collected, sems):
     channels, slab = record.shape
     windows = GROUP * span
     tail = L - HOP + JITTER
     end = RIM + L * span
     base = L * first
+    fetches = [(base + HOP * i, RIM + HOP * i, HOP) for i in range(GROUP * span)]
     if first == 0:
-        fetches = [(base + L * s, RIM + L * s, L) for s in range(span)]
         samples[:, 0:RIM] = rim[...].astype(F32)
     else:
-        fetches = [(base - RIM, 0, RIM + L)] + [(base + L * s, RIM + L * s, L) for s in range(1, span)]
+        fetches[0] = (base - RIM, 0, RIM + HOP)
     more = base + L * span < slab
     if more:
-        fetches.append((base + L * span, end, tail))
+        fetches += [(base + HOP * i, RIM + HOP * i, HOP) for i in range(GROUP * span, GROUP * (span + 1) - 1)]
+        left = tail - HOP * (GROUP - 1)
+        fetches.append((base + L * span + tail - left, end + tail - left, left))
     else:
         samples[:, end:] = jnp.zeros((channels, tail), F32)
     copies = [
@@ -202,16 +205,22 @@
     ]
     for copy in copies:
         copy.start()
-    done[...] = jnp.zeros_like(done)
+
+    def arrived(i):
+        if i < len(copies):
+            copies[i].wait()
 
     def block_sums(s):
-        return [
-            matmul(
-                samples[:, RIM + L * s + HOP * i : RIM + L * s + HOP * i + HOP].astype(BF16),
-                blocks[HOP * i : HOP * i + HOP, :],
+        found = []
+        for i in range(GROUP if s < span else GROUP - 1):
+            arrived(GROUP * s + i)
+            found.append(
+                matmul(
+                    samples[:, RIM + L * s + HOP * i : RIM + L * s + HOP * i + HOP].astype(BF16),
+                    blocks[HOP * i : HOP * i + HOP, :],
+                )
             )
-            for i in range(GROUP if s < span else GROUP - 1)
-        ]
+        return found
 
     def keep(found):
         total = found[GROUP - 1]
@@ -220,12 +229,11 @@
             total = total + found[q]
             later[q] = total
 
-    copies[0].wait()
     keep(block_sums(0))
     for s in range(span):
-        if s + 1 < len(copies):
-            copies[s + 1].wait()
         found = block_sums(s + 1) if s + 1 < span or more else []
+        if s + 1 == span and more:
+            arrived(len(copies) - 1)
         before = None
         for q in range(GROUP):
             w = GROUP * s + q
@@ -251,7 +259,7 @@
         out[:, :, width * c : width * c + width] = block[:, :, :width]
 
 
-def own_spectra(record, rim, offsets, valid, transform, rise, fall, half):
+def own_spectra(record, rim, offsets, valid, transform, rise, fall, done, half):
     channels, slab = record.shape
     span = slab // L // 2
     windows = GROUP * span
@@ -259,27 +267,26 @@
     vmem = pl.BlockSpec(memory_space=pltpu.VMEM)
     return pl.pallas_call(
         functools.partial(spectra_kernel, span * half, span),
-        out_shape=(
-            jax.ShapeDtypeStruct((BINS, 2 * windows, channels), BF16),
-            jax.ShapeDtypeStruct((8, 128), F32),
-        ),
-        in_specs=[smem, smem, pl.BlockSpec(memory_space=pl.ANY), vmem, vmem, vmem, vmem],
-        out_specs=(vmem, vmem),
+        out_shape=jax.ShapeDtypeStruct((BINS, 2 * windows, channels), BF16),
+        in_specs=[smem, smem, pl.BlockSpec(memory_space=pl.ANY), vmem, vmem, vmem, vmem, vmem],
+        out_specs=vmem,
         scratch_shapes=[
             pltpu.VMEM((channels, RIM + L * span + L - HOP + JITTER), F32),
             pltpu.VMEM((GROUP, channels, LANES), F32),
             pltpu.VMEM((max(channels // 128, 1), LANES * windows, 128), F32),
-            pltpu.SemaphoreType.DMA((span + 1,)),
+            pltpu.SemaphoreType.DMA((GROUP * (span + 1),)),
         ],
         compiler_params=pltpu.CompilerParams(vmem_limit_bytes=50 * MIB),
         cost_estimate=pl.CostEstimate(
             flops=2 * channels * LANES * 896 * windows, bytes_accessed=2 * channels * slab, transcendentals=0
         ),
         name=f"own_spectra_{half}",
-    )(offsets, valid, record, rim, transform, rise, fall)
+    )(offsets, valid, record, rim, transform, rise, fall, done)
 
 
 def join_kernel(sizes, own, parts, *chunks):
+    *chunks, done = chunks
+    done[...] = jnp.zeros_like(done)
     bins = sum(sizes)
     rows = own.shape[1] // 2
     for group in range(chunks[0].shape[0]):
@@ -300,7 +307,7 @@
 
 
 def chunk_sizes(bins):
-    return [(bins + 1) // 2, bins // 2]
+    return [bins - 3 * bins // 8, 3 * bins // 8]
 
 
 def joined_chunks(own, parts, devices):
@@ -308,20 +315,19 @@
     sizes = chunk_sizes(BINS // devices)
     vmem = pl.BlockSpec(memory_space=pltpu.VMEM)
     shapes = [(devices, count, rows, channels) for count in sizes]
-    return pl.pallas_call(
+    *chunks, done = pl.pallas_call(
         functools.partial(join_kernel, sizes),
-        out_shape=tuple(jax.ShapeDtypeStruct(shape, BF16) for shape in shapes),
+        out_shape=tuple(jax.ShapeDtypeStruct(shape, BF16) for shape in shapes) + (jax.ShapeDtypeStruct((8, 128), F32),),
         in_specs=[vmem, vmem],
-        out_specs=(vmem,) * len(shapes),
+        out_specs=(vmem,) * (len(shapes) + 1),
         compiler_params=pltpu.CompilerParams(vmem_limit_bytes=16 * MIB),
         name="joined_chunks",
     )(own, parts)
-
-
-def cross_kernel(scale, stacked, me, *rest):
-    out, done, left = rest[-3:]
-    done[...] = jnp.zeros_like(done)
-    early, late = rest[0], rest[1]
+    return chunks, done
+
+
+def left_kernel(early, late, done, out, ready):
+    ready[...] = jnp.zeros_like(ready)
     sources, _, rows, channels = early.shape
     depth = sources * rows
     half = rows // 2
@@ -329,12 +335,40 @@
         straight = own[:, 0].astype(F32)
         turned = jnp.concatenate([straight[:, half:], -straight[:, :half]], axis=1)
         for j, side in enumerate((straight, turned)):
-            left[channels * j : channels * j + channels, depth * i : depth * i + depth] = side.reshape(depth, channels).T.astype(BF16)
-    blocks = rest[2].shape[0] if stacked else (len(rest) - 4) // 2
+            out[0, channels * j : channels * j + channels, depth * i : depth * i + depth] = (
+                side.reshape(depth, channels).T.astype(BF16)
+            )
+
+
+def left_sides(early, late, begin, done):
+    sources, count, rows, channels = late.shape
+    shape = (count, 2 * channels, 2 * sources * rows)
+    vmem = pl.BlockSpec(memory_space=pltpu.VMEM)
+    return pl.pallas_call(
+        left_kernel,
+        grid=(count,),
+        out_shape=(jax.ShapeDtypeStruct(shape, BF16), jax.ShapeDtypeStruct((8, 128), F32)),
+        in_specs=[
+            pl.BlockSpec((sources, 1, rows, channels), lambda f: (0, begin + f, 0, 0)),
+            pl.BlockSpec((sources, 1, rows, channels), lambda f: (0, f, 0, 0)),
+            vmem,
+        ],
+        out_specs=(pl.BlockSpec((1,) + shape[1:], lambda f: (f, 0, 0)), vmem),
+        compiler_params=pltpu.CompilerParams(vmem_limit_bytes=16 * MIB),
+        name="left_sides",
+    )(early, late, done)
+
+
+def cross_kernel(scale, stacked, me, left, *rest):
+    out, done = rest[-2:]
+    done[...] = jnp.zeros_like(done)
+    sources, _, rows, channels = rest[0].shape[-4:]
+    depth = sources * rows
+    blocks = rest[0].shape[0] if stacked else (len(rest) - 3) // 2
     tile = min(256, channels)
     for n in range(blocks):
         if stacked:
-            pair = [rest[2][n], rest[3][n]]
+            pair = [rest[0][n], rest[1][n]]
             at = channels * n
         else:
             pair = [rest[2 * n][...], rest[2 * n + 1][...]]
@@ -342,11 +376,11 @@
         right = jnp.concatenate([one[:, 0].reshape(depth, channels) for one in pair], axis=0)
         for j in range(0, channels, tile):
             for r in range(0, 2 * channels, tile):
-                both = matmul(left[r : r + tile, :], right[:, j : j + tile]) * scale
+                both = matmul(left[0, r : r + tile, :], right[:, j : j + tile]) * scale
                 out[0, r // channels, r % channels : r % channels + tile, pl.ds(at + j, tile)] = both.astype(BF16)
 
 
-def cross_products(early, late, result, begin, bins):
+def cross_products(left, early, late, result, begin, bins):
     sources, count, rows, channels = late[0].shape
     stacked = not isinstance(late[1], list)
     blocks = late[1].shape[0] if stacked else len(late[1]) + 1
@@ -355,8 +389,8 @@
         pl.BlockSpec((sources, 1, rows, channels), lambda f: (0, begin + f, 0, 0)),
         pl.BlockSpec((sources, 1, rows, channels), lambda f: (0, f, 0, 0)),
     ]
-    operands = [lax.axis_index("chan").astype(jnp.int32).reshape(1), early[0], late[0]]
-    in_specs = [pl.BlockSpec(memory_space=pltpu.SMEM)] + specs
+    operands = [lax.axis_index("chan").astype(jnp.int32).reshape(1), left]
+    in_specs = [pl.BlockSpec(memory_space=pltpu.SMEM), pl.BlockSpec((1,) + left.shape[1:], lambda f: (f, 0, 0))]
     if stacked:
         operands += [early[1], late[1]]
         in_specs += [
@@ -364,7 +398,7 @@
             pl.BlockSpec((blocks, sources, 1, rows, channels), lambda f: (0, 0, f, 0, 0)),
         ]
     else:
-        for pair in zip(early[1], late[1]):
+        for pair in zip([early[0]] + early[1], [late[0]] + late[1]):
             operands += pair
             in_specs += specs
     if result is None:
@@ -383,7 +417,6 @@
             pl.BlockSpec((1,) + shape[1:], lambda f: (begin + f, 0, 0, 0)),
             pl.BlockSpec(memory_space=pltpu.VMEM),
         ),
-        scratch_shapes=[pltpu.VMEM((2 * channels, depth), BF16)],
         input_output_aliases=aliases,
         compiler_params=pltpu.CompilerParams(vmem_limit_bytes=36 * MIB),
         cost_estimate=pl.CostEstimate(
@@ -436,27 +469,30 @@
     def exchanged(chunk):
         return lax.all_to_all(chunk, "tm", split_axis=0, concat_axis=0, tiled=True)
 
-    def spread(mine, ready, done):
+    def spread(mine, ready):
         if stacked:
             return mine, lax.all_gather(mine, "chan", axis=0, tiled=False)
         near = fan(mine, "chan", top // 2)
-        far = after(swapped(mine, "chan", top), ready if done is None else done)
+        far = after(swapped(mine, "chan", top), ready)
         found = near | {n | top: block for n, block in fan(far, "chan", top // 2).items()}
         return mine, [found[n] for n in range(1, blocks)]
 
     inbox = from_behind(outbox(record, offsets, window_valid), "tm", 1)
     transform, rise, fall = tables(whitening)
-    early, done = own_spectra(record, inbox, offsets, window_valid, transform, rise, fall, 0)
-    parts = from_behind(border_parts(record, inbox, transform, rise, fall, done), "tm", -1)
-    late, _ = own_spectra(record, inbox, offsets, window_valid, transform, rise, fall, 1)
-    sizes = chunk_sizes(bins)
-    early = exchanged(early.reshape((devices, bins) + early.shape[1:]))
-    late = [exchanged(chunk) for chunk in joined_chunks(late, parts, devices)]
-    early = spread(early, late[0], None)
-    result, done, begin = None, None, 0
-    for p, mine in enumerate(late):
-        result, done = cross_products(early, spread(mine, None, done), result, begin, bins)
-        begin += sizes[p]
+    parts, done = border_parts(record, inbox, transform, rise, fall)
+    parts = from_behind(parts, "tm", -1)
+    early, late = (
+        own_spectra(record, inbox, offsets, window_valid, transform, rise, fall, done, half) for half in range(2)
+    )
+    late, done = joined_chunks(late, parts, devices)
+    early = after(exchanged(early.reshape((devices, bins) + early.shape[1:])), done)
+    late = [exchanged(chunk) for chunk in late]
+    early = spread(early, late[0])
+    result, begin = None, 0
+    for mine in late:
+        left, done = left_sides(early[0], mine, begin, done)
+        result, done = cross_products(left, early, spread(mine, done), result, begin, bins)
+        begin += mine.shape[1]
     return result
 
 

time: 124 us -> 142 us (1.15)
  starting transfers between devices: 20.8 us -> 37.7 us
  blocking collectives: 15.9 us -> 0 us
  waiting for transfers between devices: 41.3 us -> 51.1 us
  Pallas kernels: 41.8 us -> 47 us
  local copies, waits for them, and re-layouts: 3.2 us -> 5.43 us
    ppermute x2, waiting for transfers between devices: 0.19 us -> 17.9 us  [from_behind(): return lax.ppermute(shard, axis, pairs)]
    all_to_all x1 -> x0, blocking collectives: 15.9 us -> none  [exchanged(): return lax.all_to_all(chunk, 'tm', split_axis=0, concat_axis=0, tiled=True)]
    all_to_all x2 -> x3, starting transfers between devices: 10.4 us -> 25.9 us  [exchanged(): return lax.all_to_all(chunk, 'tm', split_axis=0, concat_axis=0, tiled=True)]
    all_to_all x2 -> x3, waiting for transfers between devices: 30.9 us -> 22.5 us  [exchanged(): return lax.all_to_all(chunk, 'tm', split_axis=0, concat_axis=0, tiled=True)]
    pallas_call x1 -> x3, Pallas kernels: 3.34 us -> 6.08 us  [the longest x1 4.13 us: border_parts(): pl.pallas_call(border_kernel, grid=(1,), out_shape=(jax.ShapeDtypeStruct(...]
    unnamed x14 -> x16, local copies, waits for them, and re-layouts: 3.2 us -> 5.43 us
    ppermute x9, starting transfers between devices: 4.26 us -> 5.72 us  [swapped(): return lax.ppermute(shard, axis, [(i, i ^ bit) for i in range(devices)])]
  transfers between devices with their start and end apart: 13 -> 14, of which waited for: 6 -> 7; matrix products, arithmetic and copies ran while one was open for 0% -> 0% of each run, Pallas kernels for 18% -> 17%
where the time goes in v4:
time: 142 us; the launch traced here: 141 us
  waiting for transfers between devices  51.1 us (36%)
  Pallas kernels  47 us (33%)
  starting transfers between devices  37.7 us (27%)
  local copies, waits for them, and re-layouts  5.43 us (4%)
    all_to_all x3, starting transfers between devices, exchanged(): return lax.all_to_all(chunk, 'tm', split_axis=0, concat_axis=0, tiled=True)  25.9 us
    all_to_all x3, waiting for transfers between devices, exchanged(): return lax.all_to_all(chunk, 'tm', split_axis=0, concat_axis=0, tiled=True)  22.5 us
    pallas_call x2, Pallas kernels, cross_products(): pl.pallas_call(functools.partial(cross_kernel, 2.0 / depth, stacked), gri...  18.6 us
    ppermute x2, waiting for transfers between devices, from_behind(): return lax.ppermute(shard, axis, pairs)  17.9 us
    pallas_call x2, Pallas kernels, own_spectra(): pl.pallas_call(functools.partial(spectra_kernel, span * half, span), out_...  16.2 us
    ppermute x9, waiting for transfers between devices, swapped(): return lax.ppermute(shard, axis, [(i, i ^ bit) for i in range(devices)])  10.6 us
    ppermute x2, starting transfers between devices, from_behind(): return lax.ppermute(shard, axis, pairs)  6.15 us
    ppermute x9, starting transfers between devices, swapped(): return lax.ppermute(shard, axis, [(i, i ^ bit) for i in range(devices)])  5.72 us
  transfers between devices with their start and end apart: 14, of which 7 were waited for; matrix products, arithmetic and copies ran while one was open for 0% of the time, Pallas kernels for 17%

profile of v4, /device:TPU:0, one launch (start us, length us, event | category | flops | bytes accessed | tf_op | source)
XLA Modules:
  0.0 141.4 jit_solution(1666131671561796337)
XLA Ops:
  0.0 1.7 %outbox.1 = bf16[512,128]{1,0:T(8,128)(2,1)} custom-call(s32[16]{0:T(128)} %offsets.5, s32[16]{0:T(128)} %valid.5, f32[512,8192]{1,0:T(8,128)} %record.7), custom_call_target="tpu_custom_call" | custom-call | tf_op jit(solution)/shard_map/outbox/pallas_call | solution.py:78
  1.7 4.9 %collective-permute-start = (bf16[512,128]{1,0:T(8,128)(2,1)}, bf16[512,128]{1,0:T(8,128)(2,1)S(1)}, u32[]{:S(2)}, u32[]{:S(2)}) collective-permute-start(bf16[512,128]{1,0:T(8,128)(2,1)} %outbox.1), channel_id=1, source_target_pairs={{0,1},{1,2},{2,3},{3,4},{4,5},{5,6},{6,7},{8,9},{9,10},{10,11},{11... | collective-permute-start | bytes 393224 | tf_op jit(solution)/shard_map/ppermute | solution.py:30
  7.6 2.0 %collective-permute-done.inbox.rim = bf16[512,128]{1,0:T(8,128)(2,1)S(1)} collective-permute-done((bf16[512,128]{1,0:T(8,128)(2,1)}, bf16[512,128]{1,0:T(8,128)(2,1)S(1)}, u32[]{:S(2)}, u32[]{:S(2)}) %collective-permute-start) | collective-permute-done | bytes 131104 | tf_op jit(solution)/shard_map/ppermute | solution.py:30
  9.7 4.1 %border_parts.1 = (bf16[64,8,512]{2,1,0:T(8,128)(2,1)}, f32[8,128]{1,0:T(8,128)S(1)}) custom-call(bf16[512,128]{1,0:T(8,128)(2,1)S(1)} %collective-permute-done.inbox.rim, f32[512,8192]{1,0:T(8,128)} %record.7, bf16[2048,128]{1,0:T(8,128)(2,1)S(1)} %get-tuple-element.20.blocks, f32[384,128]{1,0:T(8,128)S(1)} %get-tuple-element.21.rise, ...), custom_call_target="tpu_custom_call" | custom-call | flops 402653184 | bytes 3670016 | tf_op jit(solution)/shard_map/border_parts/pallas_call | solution.py:169
  13.8 9.0 %own_spectra_0.1 = bf16[64,16,512]{2,1,0:T(8,128)(2,1)} custom-call(s32[16]{0:T(128)S(1)} %copy-done.3, s32[16]{0:T(128)S(1)} %copy-done.4, f32[512,8192]{1,0:T(8,128)} %record.7, bf16[512,128]{1,0:T(8,128)(2,1)S(1)} %collective-permute-done.inbox.rim, bf16[2048,128]{1,0:T(8,128)(2,1)S(1)} %get-tuple-element.20.blocks, ...), custom_call_target="tpu_custom_call" | custom-call | flops 939524096 | bytes 8388608 | tf_op jit(solution)/shard_map/own_spectra_0/pallas_call | solution.py:268
  22.8 6.7 %all-to-all-start = ((bf16[8,8,16,512]{3,2,1,0:T(8,128)(2,1)}), bf16[8,8,16,512]{3,2,1,0:T(8,128)(2,1)S(1)}, u32[]{:S(2)}, u32[]{:S(2)}) async-start(bf16[8,8,16,512]{3,2,1,0:T(8,128)(2,1)} %bitcast.1), calls=%async_computation | async-start | bytes 2097152 | tf_op jit(solution)/shard_map/all_to_all | solution.py:470
  29.5 1.3 collective-permute-start.1
  30.8 7.2 %own_spectra_1.1.own = bf16[64,16,512]{2,1,0:T(8,128)(2,1)S(1)} custom-call(s32[16]{0:T(128)S(1)} %copy-done.3, s32[16]{0:T(128)S(1)} %copy-done.4, f32[512,8192]{1,0:T(8,128)} %record.7, bf16[512,128]{1,0:T(8,128)(2,1)S(1)} %collective-permute-done.inbox.rim, bf16[2048,128]{1,0:T(8,128)(2,1)S(1)} %get-tuple-element.20.blocks, ...), custom_call_target="tpu_custom_call" | custom-call | flops 939524096 | bytes 8388608 | tf_op jit(solution)/shard_map/own_spectra_1/pallas_call | solution.py:268
  38.1 15.9 %collective-permute-done.1.parts = bf16[64,8,512]{2,1,0:T(8,128)(2,1)S(1)} collective-permute-done((bf16[64,8,512]{2,1,0:T(8,128)(2,1)}, bf16[64,8,512]{2,1,0:T(8,128)(2,1)S(1)}, u32[]{:S(2)}, u32[]{:S(2)}) %collective-permute-start.1) | collective-permute-done | bytes 524320 | tf_op jit(solution)/shard_map/ppermute | solution.py:30
  55.2 1.5 %all-to-all-done.shard = bf16[8,8,16,512]{3,2,1,0:T(8,128)(2,1)S(1)} async-done(((bf16[8,8,16,512]{3,2,1,0:T(8,128)(2,1)}), bf16[8,8,16,512]{3,2,1,0:T(8,128)(2,1)S(1)}, u32[]{:S(2)}, u32[]{:S(2)}) %all-to-all-start) | async-done | bytes 1048608 | tf_op jit(solution)/shard_map/all_to_all | solution.py:470
  56.8 13.1 %all-to-all-start.2 = ((bf16[8,5,16,512]{3,2,1,0:T(8,128)(2,1)}), bf16[8,5,16,512]{3,2,1,0:T(8,128)(2,1)S(1)}, u32[]{:S(2)}, u32[]{:S(2)}) async-start(bf16[8,5,16,512]{3,2,1,0:T(8,128)(2,1)} %get-tuple-element.27), calls=%async_computation.2 | async-start | bytes 1310720 | tf_op jit(solution)/shard_map/all_to_all | solution.py:470
  70.0 1.6 %collective-permute-start.4 = (bf16[8,8,16,512]{3,2,1,0:T(8,128)(2,1)S(1)}, bf16[8,8,16,512]{3,2,1,0:T(8,128)(2,1)S(1)}, u32[]{:S(2)}, u32[]{:S(2)}) collective-permute-start(bf16[8,8,16,512]{3,2,1,0:T(8,128)(2,1)S(1)} %after.4.early.rest_0_), channel_id=1, source_target_pairs={{0,16},{8,24},{16,0},{24,8},{1,17},{9,25},{17,1},{25,9},{2,18},{10... | collective-permute-start | bytes 3145736 | tf_op jit(solution)/shard_map/ppermute | solution.py:433
  71.5 13.8 %all-to-all-done.2.late.done.rest_1_ = bf16[8,5,16,512]{3,2,1,0:T(8,128)(2,1)S(1)} async-done(((bf16[8,5,16,512]{3,2,1,0:T(8,128)(2,1)}), bf16[8,5,16,512]{3,2,1,0:T(8,128)(2,1)S(1)}, u32[]{:S(2)}, u32[]{:S(2)}) %all-to-all-start.2) | async-done | bytes 655392 | tf_op jit(solution)/shard_map/all_to_all | solution.py:470
  85.4 1.5 %collective-permute-start.5 = (bf16[8,5,16,512]{3,2,1,0:T(8,128)(2,1)S(1)}, bf16[8,5,16,512]{3,2,1,0:T(8,128)(2,1)}, u32[]{:S(2)}, u32[]{:S(2)}) collective-permute-start(bf16[8,5,16,512]{3,2,1,0:T(8,128)(2,1)S(1)} %all-to-all-done.2.late.done.rest_1_), channel_id=1, source_target_pairs={{0,16},{8,24},{16,0},{24,8},{1,17},{9,25},{17,1},{25,9},{2,18},{10... | collective-permute-start | bytes 1966088 | tf_op jit(solution)/shard_map/ppermute | solution.py:433
  86.9 9.2 %collective-permute-done.4.shard = bf16[8,8,16,512]{3,2,1,0:T(8,128)(2,1)S(1)} collective-permute-done((bf16[8,8,16,512]{3,2,1,0:T(8,128)(2,1)S(1)}, bf16[8,8,16,512]{3,2,1,0:T(8,128)(2,1)S(1)}, u32[]{:S(2)}, u32[]{:S(2)}) %collective-permute-start.4) | collective-permute-done | bytes 1048608 | tf_op jit(solution)/shard_map/ppermute | solution.py:433
  98.5 6.0 %all-to-all-start.1 = ((bf16[8,3,16,512]{3,2,1,0:T(8,128)(2,1)}), bf16[8,3,16,512]{3,2,1,0:T(8,128)(2,1)S(1)}, u32[]{:S(2)}, u32[]{:S(2)}) async-start(bf16[8,3,16,512]{3,2,1,0:T(8,128)(2,1)} %get-tuple-element.26), calls=%async_computation.1 | async-start | bytes 786432 | tf_op jit(solution)/shard_map/all_to_all | solution.py:470
  105.9 1.5 %copy-done.6 = bf16[5,1024,256]{2,1,0:T(8,128)(2,1)} copy-done((bf16[5,1024,256]{2,1,0:T(8,128)(2,1)}, bf16[5,1024,256]{2,1,0:T(8,128)(2,1)S(1)}, u32[]{:S(2)}) %copy-start.6) | copy-done | bytes 2621464
  107.4 2.0 %after.6.rest_5_ = bf16[8,5,16,512]{3,2,1,0:T(8,128)(2,1)} custom-call(bf16[8,5,16,512]{3,2,1,0:T(8,128)(2,1)} %collective-permute-done.5.shard, f32[8,128]{1,0:T(8,128)S(1)} %get-tuple-element.29.done), custom_call_target="tpu_custom_call" | custom-call | tf_op jit(solution)/shard_map/after/pallas_call | solution.py:452
  109.7 7.1 %all-to-all-done.1.late.rest_1_ = bf16[8,3,16,512]{3,2,1,0:T(8,128)(2,1)S(1)} async-done(((bf16[8,3,16,512]{3,2,1,0:T(8,128)(2,1)}), bf16[8,3,16,512]{3,2,1,0:T(8,128)(2,1)S(1)}, u32[]{:S(2)}, u32[]{:S(2)}) %all-to-all-start.1) | async-done | bytes 393248 | tf_op jit(solution)/shard_map/all_to_all | solution.py:470
  116.8 1.5 %collective-permute-start.9 = (bf16[8,3,16,512]{3,2,1,0:T(8,128)(2,1)S(1)}, bf16[8,3,16,512]{3,2,1,0:T(8,128)(2,1)S(1)}, u32[]{:S(2)}, u32[]{:S(2)}) collective-permute-start(bf16[8,3,16,512]{3,2,1,0:T(8,128)(2,1)S(1)} %all-to-all-done.1.late.rest_1_), channel_id=1, source_target_pairs={{0,16},{8,24},{16,0},{24,8},{1,17},{9,25},{17,1},{25,9},{2,18},{10... | collective-permute-start | bytes 1179656 | tf_op jit(solution)/shard_map/ppermute | solution.py:433
  118.3 1.7 %copy-done.7 = bf16[5,1024,256]{2,1,0:T(8,128)(2,1)S(1)} copy-done((bf16[5,1024,256]{2,1,0:T(8,128)(2,1)S(1)}, bf16[5,1024,256]{2,1,0:T(8,128)(2,1)}, u32[]{:S(2)}) %copy-start.7) | copy-done | bytes 2621464
  120.1 11.1 %cross_products.2 = (bf16[8,2,512,2048]{3,2,1,0:T(8,128)(2,1)}, f32[8,128]{1,0:T(8,128)S(1)}) custom-call(s32[1]{0:T(128)} %bitcast.me.rest_8_, bf16[5,1024,256]{2,1,0:T(8,128)(2,1)S(1)} %copy-done.7, bf16[8,8,16,512]{3,2,1,0:T(8,128)(2,1)S(1)} %after.4.early.rest_0_, bf16[8,5,16,512]{3,2,1,0:T(8,128)(2,1)S(1)} %all-to-all-done.2.late.done.rest_1_, ...), custom_call_target="tpu_custom_call" | custom-call | flops 5368709120 | bytes 20971520 | tf_op jit(solution)/shard_map/cross_products/pallas_call | solution.py:411
  132.5 1.3 collective-permute-done.10.rest_7_
  133.9 7.6 %cross_products.3 = (bf16[8,2,512,2048]{3,2,1,0:T(8,128)(2,1)}, f32[8,128]{1,0:T(8,128)}) custom-call(s32[1]{0:T(128)} %bitcast.me.rest_8_, bf16[3,1024,256]{2,1,0:T(8,128)(2,1)S(1)} %get-tuple-element.31.left, bf16[8,8,16,512]{3,2,1,0:T(8,128)(2,1)S(1)} %after.4.early.rest_0_, ...), custom_call_target="tpu_custom_call", output_to_operand_aliasing={{0}: (10, {})} | custom-call | flops 3221225472 | bytes 12582912 | tf_op jit(solution)/shard_map/cross_products/pallas_call | solution.py:411
  (34 shorter events, 7.7 us)
Async XLA Ops:
  0.0 6.6 %copy-start.2 = (f32[2048,128]{1,0:T(8,128)S(1)}, f32[2048,128]{1,0:T(8,128)}, u32[]{:S(2)}) copy-start(f32[2048,128]{1,0:T(8,128)} %constant.7.clone.table) | copy-start | bytes 3145732
  0.0 13.8 %copy-start.4 = (s32[16]{0:T(128)S(1)}, s32[16]{0:T(128)}, u32[]{:S(2)}) copy-start(s32[16]{0:T(128)} %valid.5) | copy-start | bytes 196
  0.0 13.8 %copy-start.3 = (s32[16]{0:T(128)S(1)}, s32[16]{0:T(128)}, u32[]{:S(2)}) copy-start(s32[16]{0:T(128)} %offsets.5) | copy-start | bytes 196
  0.0 6.6 %copy-start.5 = (f32[65]{0:T(128)S(1)}, f32[65]{0:T(128)}, u32[]{:S(2)}) copy-start(f32[65]{0:T(128)} %taps.1) | copy-start | bytes 784
  1.7 7.9 %collective-permute-start = (bf16[512,128]{1,0:T(8,128)(2,1)}, bf16[512,128]{1,0:T(8,128)(2,1)S(1)}, u32[]{:S(2)}, u32[]{:S(2)}) collective-permute-start(bf16[512,128]{1,0:T(8,128)(2,1)} %outbox.1), channel_id=1, source_target_pairs={{0,1},{1,2},{2,3},{3,4},{4,5},{5,6},{6,7},{8,9},{9,10},{10,11},{11... | collective-permute-start | bytes 393224 | tf_op jit(solution)/shard_map/ppermute | solution.py:30
  22.8 33.9 %all-to-all-start = ((bf16[8,8,16,512]{3,2,1,0:T(8,128)(2,1)}), bf16[8,8,16,512]{3,2,1,0:T(8,128)(2,1)S(1)}, u32[]{:S(2)}, u32[]{:S(2)}) async-start(bf16[8,8,16,512]{3,2,1,0:T(8,128)(2,1)} %bitcast.1), calls=%async_computation | async-start | bytes 2097152 | tf_op jit(solution)/shard_map/all_to_all | solution.py:470
  29.5 24.4 %collective-permute-start.1 = (bf16[64,8,512]{2,1,0:T(8,128)(2,1)}, bf16[64,8,512]{2,1,0:T(8,128)(2,1)S(1)}, u32[]{:S(2)}, u32[]{:S(2)}) collective-permute-start(bf16[64,8,512]{2,1,0:T(8,128)(2,1)} %get-tuple-element.24), channel_id=1, source_target_pairs={{1,0},{2,1},{3,2},{4,3},{5,4},{6,5},{7,6},{9,8},{10,9},{11,10},{12... | collective-permute-start | bytes 1572872 | tf_op jit(solution)/shard_map/ppermute | solution.py:30
  56.8 28.6 %all-to-all-start.2 = ((bf16[8,5,16,512]{3,2,1,0:T(8,128)(2,1)}), bf16[8,5,16,512]{3,2,1,0:T(8,128)(2,1)S(1)}, u32[]{:S(2)}, u32[]{:S(2)}) async-start(bf16[8,5,16,512]{3,2,1,0:T(8,128)(2,1)} %get-tuple-element.27), calls=%async_computation.2 | async-start | bytes 1310720 | tf_op jit(solution)/shard_map/all_to_all | solution.py:470
  70.0 26.2 %collective-permute-start.4 = (bf16[8,8,16,512]{3,2,1,0:T(8,128)(2,1)S(1)}, bf16[8,8,16,512]{3,2,1,0:T(8,128)(2,1)S(1)}, u32[]{:S(2)}, u32[]{:S(2)}) collective-permute-start(bf16[8,8,16,512]{3,2,1,0:T(8,128)(2,1)S(1)} %after.4.early.rest_0_), channel_id=1, source_target_pairs={{0,16},{8,24},{16,0},{24,8},{1,17},{9,25},{17,1},{25,9},{2,18},{10... | collective-permute-start | bytes 3145736 | tf_op jit(solution)/shard_map/ppermute | solution.py:433
  85.4 22.0 %collective-permute-start.5 = (bf16[8,5,16,512]{3,2,1,0:T(8,128)(2,1)S(1)}, bf16[8,5,16,512]{3,2,1,0:T(8,128)(2,1)}, u32[]{:S(2)}, u32[]{:S(2)}) collective-permute-start(bf16[8,5,16,512]{3,2,1,0:T(8,128)(2,1)S(1)} %all-to-all-done.2.late.done.rest_1_), channel_id=1, source_target_pairs={{0,16},{8,24},{16,0},{24,8},{1,17},{9,25},{17,1},{25,9},{2,18},{10... | collective-permute-start | bytes 1966088 | tf_op jit(solution)/shard_map/ppermute | solution.py:433
  86.9 31.4 %collective-permute-start.2 = (bf16[8,8,16,512]{3,2,1,0:T(8,128)(2,1)S(1)}, bf16[8,8,16,512]{3,2,1,0:T(8,128)(2,1)}, u32[]{:S(2)}, u32[]{:S(2)}) collective-permute-start(bf16[8,8,16,512]{3,2,1,0:T(8,128)(2,1)S(1)} %after.4.early.rest_0_), channel_id=1, source_target_pairs={{0,8},{8,0},{16,24},{24,16},{1,9},{9,1},{17,25},{25,17},{2,10},{10... | collective-permute-start | bytes 3145736 | tf_op jit(solution)/shard_map/ppermute | solution.py:433
  96.1 1.0 copy-start
  97.1 1.2 copy-start.1
  98.4 19.9 %collective-permute-start.6 = (bf16[8,8,16,512]{3,2,1,0:T(8,128)(2,1)S(1)}, bf16[8,8,16,512]{3,2,1,0:T(8,128)(2,1)}, u32[]{:S(2)}, u32[]{:S(2)}) collective-permute-start(bf16[8,8,16,512]{3,2,1,0:T(8,128)(2,1)S(1)} %after.5.rest_4_), channel_id=1, source_target_pairs={{0,8},{8,0},{16,24},{24,16},{1,9},{9,1},{17,25},{25,17},{2,10},{10... | collective-permute-start | bytes 3145736 | tf_op jit(solution)/shard_map/ppermute | solution.py:433
  98.5 18.3 %all-to-all-start.1 = ((bf16[8,3,16,512]{3,2,1,0:T(8,128)(2,1)}), bf16[8,3,16,512]{3,2,1,0:T(8,128)(2,1)S(1)}, u32[]{:S(2)}, u32[]{:S(2)}) async-start(bf16[8,3,16,512]{3,2,1,0:T(8,128)(2,1)} %get-tuple-element.26), calls=%async_computation.1 | async-start | bytes 786432 | tf_op jit(solution)/shard_map/all_to_all | solution.py:470
  104.5 13.8 %collective-permute-start.3 = (bf16[8,5,16,512]{3,2,1,0:T(8,128)(2,1)S(1)}, bf16[8,5,16,512]{3,2,1,0:T(8,128)(2,1)}, u32[]{:S(2)}, u32[]{:S(2)}) collective-permute-start(bf16[8,5,16,512]{3,2,1,0:T(8,128)(2,1)S(1)} %all-to-all-done.2.late.done.rest_1_), channel_id=1, source_target_pairs={{0,8},{8,0},{16,24},{24,16},{1,9},{9,1},{17,25},{25,17},{2,10},{10... | collective-permute-start | bytes 1966088 | tf_op jit(solution)/shard_map/ppermute | solution.py:433
  105.9 1.5 %copy-start.6 = (bf16[5,1024,256]{2,1,0:T(8,128)(2,1)}, bf16[5,1024,256]{2,1,0:T(8,128)(2,1)S(1)}, u32[]{:S(2)}) copy-start(bf16[5,1024,256]{2,1,0:T(8,128)(2,1)S(1)} %get-tuple-element.28.left) | copy-start | bytes 7864324
  109.4 9.0 %collective-permute-start.7 = (bf16[8,5,16,512]{3,2,1,0:T(8,128)(2,1)}, bf16[8,5,16,512]{3,2,1,0:T(8,128)(2,1)}, u32[]{:S(2)}, u32[]{:S(2)}) collective-permute-start(bf16[8,5,16,512]{3,2,1,0:T(8,128)(2,1)} %after.6.rest_5_), channel_id=1, source_target_pairs={{0,8},{8,0},{16,24},{24,16},{1,9},{9,1},{17,25},{25,17},{2,10},{10... | collective-permute-start | bytes 1966088 | tf_op jit(solution)/shard_map/ppermute | solution.py:433
  116.8 15.1 %collective-permute-start.9 = (bf16[8,3,16,512]{3,2,1,0:T(8,128)(2,1)S(1)}, bf16[8,3,16,512]{3,2,1,0:T(8,128)(2,1)S(1)}, u32[]{:S(2)}, u32[]{:S(2)}) collective-permute-start(bf16[8,3,16,512]{3,2,1,0:T(8,128)(2,1)S(1)} %all-to-all-done.1.late.rest_1_), channel_id=1, source_target_pairs={{0,16},{8,24},{16,0},{24,8},{1,17},{9,25},{17,1},{25,9},{2,18},{10... | collective-permute-start | bytes 1179656 | tf_op jit(solution)/shard_map/ppermute | solution.py:433
  118.3 14.2 %collective-permute-start.8 = (bf16[8,3,16,512]{3,2,1,0:T(8,128)(2,1)S(1)}, bf16[8,3,16,512]{3,2,1,0:T(8,128)(2,1)S(1)}, u32[]{:S(2)}, u32[]{:S(2)}) collective-permute-start(bf16[8,3,16,512]{3,2,1,0:T(8,128)(2,1)S(1)} %all-to-all-done.1.late.rest_1_), channel_id=1, source_target_pairs={{0,8},{8,0},{16,24},{24,16},{1,9},{9,1},{17,25},{25,17},{2,10},{10... | collective-permute-start | bytes 1179656 | tf_op jit(solution)/shard_map/ppermute | solution.py:433
  118.3 1.7 %copy-start.7 = (bf16[5,1024,256]{2,1,0:T(8,128)(2,1)S(1)}, bf16[5,1024,256]{2,1,0:T(8,128)(2,1)}, u32[]{:S(2)}) copy-start(bf16[5,1024,256]{2,1,0:T(8,128)(2,1)} %copy-done.6) | copy-start | bytes 7864324
  132.0 1.9 %collective-permute-start.10 = (bf16[8,3,16,512]{3,2,1,0:T(8,128)(2,1)S(1)}, bf16[8,3,16,512]{3,2,1,0:T(8,128)(2,1)S(1)}, u32[]{:S(2)}, u32[]{:S(2)}) collective-permute-start(bf16[8,3,16,512]{3,2,1,0:T(8,128)(2,1)S(1)} %after.7.rest_5_), channel_id=1, source_target_pairs={{0,8},{8,0},{16,24},{24,16},{1,9},{9,1},{17,25},{25,17},{2,10},{10... | collective-permute-start | bytes 1179656 | tf_op jit(solution)/shard_map/ppermute | solution.py:433
